TPU v7x, 128 devices: a whole 4x4x4 slice. The times are simulated.
128 devices in a mesh: resp: 16 (over z, x_lo, core), exp: 8 (over y, x_hi).
Axes of the slice: x: 4 (x_hi: 2, x_lo: 2; x = x_hi * 2 + x_lo), y: 4, z: 4, core: 2. Of those that a mesh axis runs over, the one named last changes fastest.
Arguments:
- queries: bfloat16 [256, 32, 36864], P('resp', None, 'exp'), may hold values from -4 to 4
- resp_latent: bfloat16 [256, 32, 576], P('resp'), may hold values from -4 to 4
- prompt_cache: bfloat16 [16, 128, 576], P('resp'), may hold values from -4 to 4
- prompt_len: int32 [16], replicated, may hold values from 32 to 128, as said below
- w_uv: bfloat16 [64, 512, 128], P('exp'), may hold values from -0.25 to 0.25
- w_o: bfloat16 [8192, 7168], P('exp', 'resp'), may hold values from -0.0625 to 0.0625
- residual: bfloat16 [8192, 7168], P(('resp', 'exp')), may hold values from -3 to 3
- norm_gain: float32 [7168], replicated, may hold values from 0.1 to 1.9
- expert_in: bfloat16 [16, 2, 7168, 1024], P('resp', None, None, 'exp'), may hold values from -0.0625 to 0.0625
- expert_out: bfloat16 [16, 1024, 7168], P('resp', None, 'exp'), may hold values from -0.1875 to 0.1875
- routes: int32 [8192, 1], P(('resp', 'exp')), may hold values from 0 to 15; in each aligned block of 64 rows (0 to 63, 64 to 127, ...) at most 4 rows name the same one
- gate_probs: float32 [8192, 1], P(('resp', 'exp')), may hold values from 0.1 to 1
Outputs:
- layer_out: bfloat16 [8192, 7168], P(('resp', 'exp'))
Inputs may be any that keep to these rules, and one draw needn't show every extreme that they name: `prompt_len`: some prompt has exactly 128 live entries. `routes`: among the rows of one device (aligned blocks of 64 rows) no expert is chosen more than 4 times, a bound that some block reaches.
All inputs are finite; a program needn't handle non-finite values.
Results may differ from a plain program's by a relative error of at most 0.029.
Values may be sent and summed in bfloat16 or wider, within the bound.
No kernel may reach another device: no remote copies, remote signals or barrier semaphores. Data moves between devices by JAX's collectives and lax.ppermute only.
A program may use at most 128 MiB of HBM per device.

v0:
```python
import jax
import jax.numpy as jnp
from jax import lax
from jax.sharding import PartitionSpec as P

SCALE = 192.0 ** (-0.5)
ROUTED = 2.5
EPSILON = 1e-06
NEGATIVE = -1e30


def combine(earlier, update):
    peak_a, weight_a, summed_a = earlier
    peak_b, weight_b, summed_b = update
    peak_new = jnp.maximum(peak_a, peak_b)
    factor_a = jnp.exp(peak_a - peak_new)
    factor_b = jnp.exp(peak_b - peak_new)
    return (
        peak_new,
        weight_a * factor_a + weight_b * factor_b,
        summed_a * factor_a[..., None] + summed_b * factor_b[..., None],
    )


def body(
    queries,
    resp_latent,
    prompt_cache,
    prompt_len,
    w_uv,
    w_o,
    residual,
    norm_gain,
    expert_in,
    expert_out,
    routes,
    gate_probs,
):
    group_count = lax.axis_size("resp")
    shard_count = lax.axis_size("exp")
    group_rows, resp_len, packed = queries.shape
    entry_width = resp_latent.shape[2]
    heads_local, lat_width, value_width = w_uv.shape
    prompt_count = prompt_len.shape[0]
    repeats = group_rows // prompt_count
    cache_len = prompt_cache.shape[1]
    query_grid = queries.reshape(repeats, prompt_count, resp_len, heads_local, entry_width)
    own_grid = resp_latent.reshape(repeats, prompt_count, resp_len, entry_width)
    stat_shape = (repeats, prompt_count, heads_local, resp_len)
    blank = (
        jnp.full(stat_shape, NEGATIVE, jnp.float32),
        jnp.zeros(stat_shape, jnp.float32),
        jnp.zeros(stat_shape + (lat_width,), jnp.float32),
    )
    shard_piece = lax.all_gather(prompt_cache, "resp", axis=0, tiled=True)
    scores = (
        jnp.einsum("mjthc,jpc->mjhtp", query_grid, shard_piece, preferred_element_type=jnp.float32)
        * SCALE
    )
    allowed = jnp.arange(cache_len)[None, :] < prompt_len[:, None]
    scores = jnp.where(allowed[None, :, None, None, :], scores, NEGATIVE)
    peak_score = jnp.max(scores, axis=-1)
    weights = jnp.exp(scores - peak_score[..., None])
    weight_sum = jnp.sum(weights, axis=-1)
    weighted = jnp.einsum(
        "mjhtp,jpc->mjhtc",
        weights.astype(jnp.bfloat16),
        shard_piece[..., :lat_width],
        preferred_element_type=jnp.float32,
    )
    merged = combine(blank, (peak_score, weight_sum, weighted))
    carried = merged
    scores = (
        jnp.einsum("mjthc,mjsc->mjhts", query_grid, own_grid, preferred_element_type=jnp.float32)
        * SCALE
    )
    causal = jnp.arange(resp_len)[None, :] <= jnp.arange(resp_len)[:, None]
    scores = jnp.where(causal, scores, NEGATIVE)
    peak_score = jnp.max(scores, axis=-1)
    weights = jnp.exp(scores - peak_score[..., None])
    weight_sum = jnp.sum(weights, axis=-1)
    weighted = jnp.einsum(
        "mjhts,mjsc->mjhtc",
        weights.astype(jnp.bfloat16),
        own_grid[..., :lat_width],
        preferred_element_type=jnp.float32,
    )
    carried = combine(carried, (peak_score, weight_sum, weighted))
    peak_score, weight_sum, weighted = carried
    latent = (weighted / weight_sum[..., None]).astype(jnp.bfloat16)
    values = jnp.einsum(
        "mjhtc,hcv->mjthv", latent, w_uv, preferred_element_type=jnp.float32
    ).astype(jnp.bfloat16)
    values = values.reshape(group_rows * resp_len, heads_local * value_width)
    rows_moe = group_rows * resp_len // shard_count
    everyone = lax.all_gather(values, "resp", axis=0, tiled=True)
    value_grid = everyone.reshape(group_count, shard_count, rows_moe, heads_local * value_width)
    block_rows = group_count * rows_moe
    term = jnp.einsum("rets,sc->ertc", value_grid, w_o, preferred_element_type=jnp.float32)
    shares = lax.psum_scatter(
        term.reshape(block_rows * lax.axis_size("exp"), w_o.shape[1]).astype(jnp.bfloat16),
        "exp",
        scatter_dimension=0,
        tiled=True,
    ).astype(jnp.float32)
    swapped = lax.all_to_all(
        shares.reshape(group_count, rows_moe, w_o.shape[1]).astype(jnp.bfloat16),
        "resp",
        split_axis=0,
        concat_axis=2,
        tiled=True,
    ).astype(jnp.float32)
    attention = swapped.reshape(rows_moe, -1)
    hidden = residual.astype(jnp.float32) + attention
    scale_rows = lax.rsqrt(jnp.mean(hidden * hidden, axis=-1, keepdims=True) + EPSILON)
    normed = (hidden * scale_rows * norm_gain).astype(jnp.bfloat16)
    gate_share = ROUTED * gate_probs
    token_count, choices_each = routes.shape
    capacity = max(2, 9 * token_count * choices_each // (8 * group_count))
    matches = routes[:, :, None] == jnp.arange(group_count, dtype=jnp.int32)[None, None, :]
    running = (
        jnp.cumsum(matches.reshape(-1, group_count).astype(jnp.int32), axis=0).reshape(
            matches.shape
        )
        - 1
    )
    slot_index = jnp.sum(jnp.where(matches, running, 0), axis=-1)
    slot_match = slot_index[:, :, None] == jnp.arange(capacity, dtype=jnp.int32)[None, None, :]
    placed = matches[:, :, :, None] & slot_match[:, :, None, :]
    select = jnp.sum(placed.astype(jnp.int32), axis=1).astype(jnp.bfloat16)
    weight_map = jnp.sum(jnp.where(placed, gate_share[:, :, None, None], 0.0), axis=1)
    outgoing = jnp.einsum("txc,td->xcd", select, normed, preferred_element_type=jnp.float32).astype(
        jnp.bfloat16
    )
    arrived = lax.all_to_all(outgoing, "resp", split_axis=0, concat_axis=0, tiled=True)
    shard_piece = lax.all_gather(arrived, "exp", axis=0, tiled=True)
    gate_act = jnp.einsum(
        "scd,df->scf", shard_piece, expert_in[0, 0], preferred_element_type=jnp.float32
    )
    up_act = jnp.einsum(
        "scd,df->scf", shard_piece, expert_in[0, 1], preferred_element_type=jnp.float32
    )
    act_part = (jax.nn.silu(gate_act) * up_act).astype(jnp.bfloat16)
    act_full = lax.all_gather(act_part, "exp", axis=2, tiled=True)
    result = jnp.einsum(
        "scf,fd->scd", act_full, expert_out[0], preferred_element_type=jnp.float32
    ).astype(jnp.bfloat16)
    result = result.reshape(shard_count, group_count, capacity, result.shape[2])
    returned = lax.all_to_all(
        lax.all_to_all(result, "resp", split_axis=1, concat_axis=1, tiled=True),
        "exp",
        split_axis=0,
        concat_axis=3,
        tiled=True,
    )
    returned = returned.reshape(group_count, capacity, -1)
    mixture = jnp.einsum(
        "txc,xcd->td", weight_map, returned.astype(jnp.float32), precision=lax.Precision.HIGHEST
    )
    return (hidden + mixture).astype(jnp.bfloat16)


def solution(mesh):
    return jax.shard_map(
        body,
        mesh=mesh,
        in_specs=(
            P("resp", None, "exp"),
            P("resp", None, None),
            P("resp", None, None),
            P(),
            P("exp", None, None),
            P("exp", "resp"),
            P(("resp", "exp"), None),
            P(),
            P("resp", None, None, "exp"),
            P("resp", None, "exp"),
            P(("resp", "exp"), None),
            P(("resp", "exp"), None),
        ),
        out_specs=P(("resp", "exp"), None),
        check_vma=False,
    )
```

profile of v0, /device:TPU:1, one launch (start us, length us, event | category | flops | bytes accessed | tf_op | source)
XLA Modules:
  0.0 548.3 jit_solution(9124238566953121464)
XLA Ops:
  6.5 0.0 copy-start
  6.5 0.0 all-gather.5.cloned.1.call-start
  6.5 0.7 all-gather.5.cloned.1.call-update
  7.3 0.0 copy-start.7
  7.3 0.0 copy-start.12
  7.3 0.0 all-gather.7.cloned.1.call-start
  7.3 9.5 %reshape.318 = bf16[16,32,8,576]{3,2,1,0:T(8,128)(2,1)} reshape(bf16[16,32,4608]{2,1,0:T(8,128)(2,1)} %param.12) | data formatting | bytes 9437184 | tf_op jit(solution)/shard_map/reshape.1
  16.9 0.1 iota_compare_fusion.2
  16.9 0.0 copy-done.12
  16.9 7.3 %fusion.30 = (f32[16,8,32]{2,1,0:T(8,128)S(1)}, f32[16,32,32,8]{2,1,3,0:T(8,128)S(1)}) fusion(pred[32,32]{0,1:T(8,128)(4,1)S(1)} %iota_compare_fusion, bf16[16,32,8,576]{3,2,1,0:T(8,128)(2,1)} %reshape.318, bf16[16,32,576]{2,1,0:T(8,128)(2,1)S(1)} %copy-done.12), kind=kOutput, calls=%fused_computation.44 | convolution fusion | flops 151384064 | bytes 5850112 | tf_op jit(solution)/shard_map/mjthc,mjsc->mjhts/dot_general | solution.py:74
  24.3 0.0 copy-start.3
  24.3 1.4 copy-done.3
  25.7 0.8 fusion.18
  26.4 20.8 %all-gather.5.cloned.1.call-done = bf16[16,128,576]{1,2,0:T(8,128)(2,1)} async-done(((bf16[1,128,576]{1,2,0:T(8,128)(2,1)}), bf16[16,128,576]{1,2,0:T(8,128)(2,1)}) %all-gather.5.cloned.1.call-update) | async-done | bytes 2359312 | tf_op jit(solution)/shard_map/all_gather | solution.py:55
  47.2 4.8 bitcast_reduce_fusion
  52.0 1.3 fusion.28
  53.4 0.1 multiply_add_fusion
  53.4 0.3 copy-done.5
  53.7 2.0 fusion.16
  55.7 0.0 copy-start.10
  55.7 4.3 fusion.14
  60.0 1.3 fusion.37
  61.3 0.7 copy.33
  62.0 0.0 copy-start.11
  62.0 1.3 copy.65
  63.2 0.0 all-gather.7.cloned.1.call-update
  63.3 0.2 reduce-scatter.2.cloned.1.call-start
  63.5 91.6 %all-gather.7.cloned.1.call-done = bf16[8192,1024]{1,0:T(8,128)(2,1)} async-done(((bf16[512,1024]{1,0:T(8,128)(2,1)}), bf16[8192,1024]{1,0:T(8,128)(2,1)}) %all-gather.7.cloned.1.call-update) | async-done | bytes 16777232 | tf_op jit(solution)/shard_map/all_gather | solution.py:96
  155.1 0.0 copy-done.11
  155.1 16.9 %convert_bitcast_fusion = bf16[8,16,64,448]{3,2,0,1:T(8,128)(2,1)} fusion(bf16[16,8,64,1024]{3,2,1,0:T(8,128)(2,1)} %bitcast.192, bf16[1024,448]{0,1:T(8,128)(2,1)S(1)} %copy-done.11), kind=kOutput, calls=%fused_computation.6 | convolution fusion | flops 7519862784 | bytes 25034752 | tf_op jit(solution)/shard_map/rets,sc->ertc/dot_general | solution.py:99
  172.0 7.7 %copy.34 = bf16[8,16,64,448]{3,2,1,0:T(8,128)(2,1)} copy(bf16[8,16,64,448]{3,2,0,1:T(8,128)(2,1)} %convert_bitcast_fusion) | data formatting | bytes 14680064 | tf_op jit(solution)/shard_map/convert_element_type | solution.py:101
  179.7 0.0 reduce-scatter.2.cloned.1.call-update
  179.8 0.0 copy-start.8
  179.8 114.8 %reduce-scatter.2.cloned.1.call-done = bf16[1024,448]{1,0:T(8,128)(2,1)} async-done(((bf16[8192,448]{1,0:T(8,128)(2,1)}), bf16[1024,448]{1,0:T(8,128)(2,1)}) %reduce-scatter.2.cloned.1.call-update) | async-done | bytes 917520 | tf_op jit(solution)/shard_map/reduce_scatter | solution.py:100
  294.6 5.7 %all-to-all-start = ((bf16[16,64,448]{2,1,0:T(8,128)(2,1)}), bf16[16,64,448]{2,1,0:T(8,128)(2,1)S(1)}, u32[]{:S(2)}, u32[]{:S(2)}) async-start(bf16[16,64,448]{2,1,0:T(8,128)(2,1)} %bitcast.188), calls=%async_computation.1 | async-start | bytes 2097152 | tf_op jit(solution)/shard_map/all_to_all | solution.py:106
  300.3 0.0 all-gather.9.cloned.1.call-start
  300.3 1.4 fusion.88
  301.7 14.4 %all-to-all-done = bf16[16,64,448]{2,1,0:T(8,128)(2,1)S(1)} async-done(((bf16[16,64,448]{2,1,0:T(8,128)(2,1)}), bf16[16,64,448]{2,1,0:T(8,128)(2,1)S(1)}, u32[]{:S(2)}, u32[]{:S(2)}) %all-to-all-start) | async-done | bytes 917536 | tf_op jit(solution)/shard_map/all_to_all | solution.py:106
  316.1 0.3 convert_bitcast_fusion.1
  316.4 2.6 copy.35
  318.9 3.2 reshape.328
  322.2 2.0 multiply_reduce_fusion
  324.1 0.1 copy-done.1
  324.2 0.0 copy-done.6
  324.2 0.5 convolution_convert_fusion
  324.7 0.7 copy.36
  325.5 17.4 %all_to_all.34 = bf16[16,4,7168]{2,1,0:T(4,128)(2,1)S(1)} all-to-all(bf16[16,4,7168]{2,1,0:T(4,128)(2,1)S(1)} %copy.36), channel_id=1, replica_groups=mesh['resp'=16,'exp'=8] {'resp'}, dimensions={0} | all-to-all | bytes 1835008 | tf_op jit(solution)/shard_map/all_to_all | solution.py:135
  342.9 1.2 copy.37
  344.0 0.0 all-gather.9.cloned.1.call-update
  344.1 0.3 all-gather.11.cloned.1.call-start
  344.3 94.0 %all-gather.9.cloned.1.call-done = bf16[128,4,7168]{2,0,1:T(8,128)(2,1)} async-done(((bf16[16,4,7168]{2,0,1:T(8,128)(2,1)}), bf16[128,4,7168]{2,0,1:T(8,128)(2,1)}) %all-gather.9.cloned.1.call-update) | async-done | bytes 7340048 | tf_op jit(solution)/shard_map/all_gather | solution.py:136
  438.3 5.8 %fusion.22 = f32[128,4,128]{2,0,1:T(8,128)S(1)} fusion(bf16[128,4,7168]{2,0,1:T(8,128)(2,1)} %all-gather.9.cloned.1.call-done, bf16[1,2,7168,128]{3,2,1,0:T(8,128)(2,1)} %param.20), kind=kOutput, calls=%fused_computation.33 | convolution fusion | flops 939524096 | bytes 9437184 | tf_op jit(solution)/shard_map/scd,df->scf/dot_general | solution.py:137
  444.1 4.2 fusion.43
  448.4 0.0 all-gather.11.cloned.1.call-update
  448.4 42.8 %all-gather.11.cloned.1.call-done = bf16[128,4,1024]{2,0,1:T(8,128)(2,1)} async-done(((bf16[128,4,128]{2,0,1:T(8,128)(2,1)}), bf16[128,4,1024]{2,0,1:T(8,128)(2,1)}) %all-gather.11.cloned.1.call-update) | async-done | bytes 1048592 | tf_op jit(solution)/shard_map/all_gather | solution.py:144
  491.2 2.5 fusion.34
  493.7 0.2 copy.38
  493.8 19.8 %all_to_all.35 = bf16[8,16,4,896]{3,0,2,1:T(8,128)(2,1)S(1)} all-to-all(bf16[8,16,4,896]{3,0,2,1:T(8,128)(2,1)S(1)} %copy.38), channel_id=1, replica_groups=mesh['resp'=16,'exp'=8] {'resp'}, dimensions={1} | all-to-all | bytes 1835008 | tf_op jit(solution)/shard_map/all_to_all | solution.py:150
  513.6 1.2 copy.39
  514.8 4.2 all-to-all-start.3
  519.0 14.2 %all-to-all-done.3 = bf16[8,16,4,896]{3,1,2,0:T(8,128)(2,1)} async-done(((bf16[8,16,4,896]{3,1,2,0:T(8,128)(2,1)}), bf16[8,16,4,896]{3,1,2,0:T(8,128)(2,1)}, u32[]{:S(2)}, u32[]{:S(2)}) %all-to-all-start.3) | async-done | bytes 917536 | tf_op jit(solution)/shard_map/all_to_all | solution.py:149
  533.2 2.6 copy.40
  535.8 2.3 reshape.327
  538.1 3.7 fusion.7
  (20 shorter events, 0.1 us)
Async XLA Ops:
  6.5 484.7 %copy-start = (bf16[1,1024,896]{2,1,0:T(8,128)(2,1)S(1)}, bf16[1,1024,896]{2,1,0:T(8,128)(2,1)}, u32[]{:S(2)}) copy-start(bf16[1,1024,896]{2,1,0:T(8,128)(2,1)} %param.21) | copy-start | bytes 5505028
  6.5 40.7 %all-gather.5.cloned.1.call-start = ((), (), s32[]{:S(2)}) async-start(), calls=%async_computation.5 | async-start | bytes 2506752 | tf_op jit(solution)/shard_map/all_gather | solution.py:55
  7.3 9.6 %copy-start.7 = (s32[16]{0:T(128)S(1)}, s32[16]{0:T(128)}, u32[]{:S(2)}) copy-start(s32[16]{0:T(128)} %param.15) | copy-start | bytes 196
  7.3 9.7 %copy-start.12 = (bf16[16,32,576]{2,1,0:T(8,128)(2,1)S(1)}, bf16[16,32,576]{2,1,0:T(8,128)(2,1)}, u32[]{:S(2)}) copy-start(bf16[16,32,576]{2,1,0:T(8,128)(2,1)} %param.13) | copy-start | bytes 1769476
  7.3 147.8 %all-gather.7.cloned.1.call-start = ((), (), s32[]{:S(2)}) async-start(), calls=%async_computation.6 | async-start | bytes 17825792 | tf_op jit(solution)/shard_map/all_gather | solution.py:96
  24.3 1.4 copy-start.3
  52.0 1.7 copy-start.5
  53.7 2.0 copy-start.4
  55.7 4.3 copy-start.10
  62.0 93.1 %copy-start.11 = (bf16[1024,448]{0,1:T(8,128)(2,1)S(1)}, bf16[1024,448]{0,1:T(8,128)(2,1)}, u32[]{:S(2)}) copy-start(bf16[1024,448]{0,1:T(8,128)(2,1)} %param.17) | copy-start | bytes 2752516
  63.3 231.3 %reduce-scatter.2.cloned.1.call-start = ((), (), s32[]{:S(2)}) async-start(), calls=%async_computation.7 | async-start | bytes 9437184 | tf_op jit(solution)/shard_map/reduce_scatter | solution.py:100
  179.8 120.6 %copy-start.8 = (s32[64,1]{0,1:T(1,128)S(1)}, s32[64,1]{0,1:T(1,128)}, u32[]{:S(2)}) copy-start(s32[64,1]{0,1:T(1,128)} %param.22) | copy-start | bytes 772
  294.6 21.5 %all-to-all-start = ((bf16[16,64,448]{2,1,0:T(8,128)(2,1)}), bf16[16,64,448]{2,1,0:T(8,128)(2,1)S(1)}, u32[]{:S(2)}, u32[]{:S(2)}) async-start(bf16[16,64,448]{2,1,0:T(8,128)(2,1)} %bitcast.188), calls=%async_computation.1 | async-start | bytes 2097152 | tf_op jit(solution)/shard_map/all_to_all | solution.py:106
  300.3 138.1 %all-gather.9.cloned.1.call-start = ((), (), s32[]{:S(2)}) async-start(), calls=%async_computation.8 | async-start | bytes 8257536 | tf_op jit(solution)/shard_map/all_gather | solution.py:136
  318.9 3.2 copy-start.2
  322.2 2.1 copy-start.1
  322.2 2.1 copy-start.6
  344.1 147.1 %all-gather.11.cloned.1.call-start = ((), (), s32[]{:S(2)}) async-start(), calls=%async_computation.9 | async-start | bytes 1179648 | tf_op jit(solution)/shard_map/all_gather | solution.py:144
  438.3 5.8 %copy-start.9 = (bf16[128,4,7168]{2,0,1:T(8,128)(2,1)S(1)}, bf16[128,4,7168]{2,0,1:T(8,128)(2,1)}, u32[]{:S(2)}) copy-start(bf16[128,4,7168]{2,0,1:T(8,128)(2,1)} %all-gather.9.cloned.1.call-done) | copy-start | bytes 22020100
  513.6 5.4 copy-start.13
  514.8 18.4 %all-to-all-start.3 = ((bf16[8,16,4,896]{3,1,2,0:T(8,128)(2,1)}), bf16[8,16,4,896]{3,1,2,0:T(8,128)(2,1)}, u32[]{:S(2)}, u32[]{:S(2)}) async-start(bf16[8,16,4,896]{3,1,2,0:T(8,128)(2,1)} %copy.39), calls=%async_computation.4 | async-start | bytes 1835008 | tf_op jit(solution)/shard_map/all_to_all | solution.py:149
Sparse Core Ops, SparseCore 0:
  9.1 38.1 all-gather.4
  63.4 91.6 all-gather.6
  179.9 114.6 reduce-scatter.1
  344.2 94.0 all-gather.8
  448.5 42.6 all-gather.10
where the time goes:
time: 550 us; the launch traced here: 548 us
  waiting for transfers between devices  393 us (71%)
  matrix products  53.2 us (10%)
  blocking collectives  37.2 us (7%)
  local copies, waits for them, and re-layouts  34.9 us (6%)
  between operations  13.4 us (2%)
  starting transfers between devices  10.5 us (2%)
  other arithmetic  5.88 us (1%)
    reduce_scatter x1, waiting for transfers between devices, body(): lax.psum_scatter(term.reshape(block_rows * lax.axis_size('exp'), w_o.shap...  115 us
    all_gather x1, waiting for transfers between devices, body(): shard_piece = lax.all_gather(arrived, 'exp', axis=0, tiled=True)  94 us
    all_gather x1, waiting for transfers between devices, body(): everyone = lax.all_gather(values, 'resp', axis=0, tiled=True)  91.6 us
    all_gather x1, waiting for transfers between devices, body(): act_full = lax.all_gather(act_part, 'exp', axis=2, tiled=True)  42.8 us
    all_gather x1, waiting for transfers between devices, body(): shard_piece = lax.all_gather(prompt_cache, 'resp', axis=0, tiled=True)  20.8 us
    all_to_all x1, blocking collectives, body(): lax.all_to_all(result, 'resp', split_axis=1, concat_axis=1, tiled=True)  19.8 us
    all_to_all x1, blocking collectives, body(): lax.all_to_all(outgoing, 'resp', split_axis=0, concat_axis=0, tiled=True)  17.4 us
    dot_general x1, matrix products, body(): jnp.einsum('rets,sc->ertc', value_grid, w_o, preferred_element_type=jnp.f...  16.9 us
  transfers between devices with their start and end apart: 7, of which 7 were waited for; matrix products, arithmetic and copies ran while one was open for 3% of the time, Pallas kernels for 0%

commit v1 on v0

v1 whole, which is shorter than its diff:
```python
import functools

import jax
import jax.numpy as jnp
from jax import lax
from jax.experimental import pallas as pl
from jax.experimental.pallas import tpu as pltpu
from jax.sharding import PartitionSpec as P

SCALE = 192.0 ** (-0.5)
ROUTED = 2.5
EPSILON = 1e-06
NEGATIVE = -1e30
NZ, NX, NC, NY, NH = 4, 2, 2, 4, 2
RLEN, ENTRY, LAT, PLEN, HEADS, VHEAD = 32, 576, 512, 128, 8, 128
DIM, SLICE, HALF, FF, HID = 7168, 896, 448, 1024, 128
GROUP, BLOCK, EXPERTS, CAP = 512, 64, 16, 4
MESSAGE = 2 * FF + 128
BF = jnp.bfloat16
F32 = jnp.float32
VMEM_BYTES = 56 * 1024 * 1024


def params():
    return pltpu.CompilerParams(vmem_limit_bytes=VMEM_BYTES)


def resp_perm(dz, dx, dc):
    pairs = []
    for z in range(NZ):
        for x in range(NX):
            for c in range(NC):
                source = (z * NX + x) * NC + c
                target = (((z + dz) % NZ) * NX + (x ^ dx)) * NC + (c ^ dc)
                pairs.append((source, target))
    return pairs


def exp_perm(dy, dh):
    pairs = []
    for y in range(NY):
        for h in range(NH):
            pairs.append((y * NH + h, ((y + dy) % NY) * NH + (h ^ dh)))
    return pairs


def over_resp(x, dz, dx, dc):
    return lax.ppermute(x, "resp", resp_perm(dz, dx, dc))


def over_exp(x, dy, dh):
    return lax.ppermute(x, "exp", exp_perm(dy, dh))


def everywhere(z, x, c, y, h):
    return ((z * NX + x) * NC + c) * (NY * NH) + y * NH + h


def crossing():
    return [
        (everywhere(z, x, c, y, h), everywhere(-y % NZ, x, c, z, h))
        for z in range(NZ)
        for x in range(NX)
        for c in range(NC)
        for y in range(NY)
        for h in range(NH)
    ]


def diagonal():
    return [
        (everywhere(z, x, c, y, h), everywhere(z, x, 1 - c, y, 1 - h))
        for z in range(NZ)
        for x in range(NX)
        for c in range(NC)
        for y in range(NY)
        for h in range(NH)
    ]


def over_z(x, step):
    return over_resp(x, step, 0, 0)


def over_y(x, step):
    return over_exp(x, step, 0)


def ring(x, shift):
    half = x.shape[0] // 2
    left = shift(x, 1)
    right = shift(x, 3)
    return [x, left, shift(left[:half], 1), shift(right[half:], 3), right]


def dot(a, b):
    return lax.dot_general(a, b, (((1,), (0,)), ((), ())), preferred_element_type=F32)


def dot_nt(a, b):
    return lax.dot_general(a, b, (((1,), (1,)), ((), ())), preferred_element_type=F32)


def attention_kernel(lens, q_ref, keys, own, w_uv, out, lat, even, odd, bias):
    step = pl.program_id(0)
    rows = HEADS * RLEN
    total = PLEN + RLEN

    @pl.when(step == 0)
    def _():
        even[:, :, ENTRY:] = jnp.zeros((2, total, 640 - ENTRY), BF)
        odd[:, :, :64] = jnp.zeros((2, total, 64), BF)
        column = lax.broadcasted_iota(jnp.int32, (rows, total), 1)
        token = lax.broadcasted_iota(jnp.int32, (rows, total), 0) % RLEN
        seen = (column < PLEN) | (column <= token + PLEN)
        bias[...] = jnp.where(seen, 0.0, NEGATIVE)

    for part in range(2):
        resp = 2 * step + part
        even[part, :PLEN, :ENTRY] = keys[part]
        even[part, PLEN:, :ENTRY] = own[part]
        odd[part, :PLEN, 64:] = keys[part]
        odd[part, PLEN:, 64:] = own[part]
        first = [q_ref[part, :, p * 1152 : p * 1152 + 640] for p in range(HEADS // 2)]
        second = [q_ref[part, :, p * 1152 + 512 : p * 1152 + 1152] for p in range(HEADS // 2)]
        scores = jnp.concatenate(
            [
                dot_nt(jnp.concatenate(first, axis=0), even[part]),
                dot_nt(jnp.concatenate(second, axis=0), odd[part]),
            ],
            axis=0,
        )
        column = lax.broadcasted_iota(jnp.int32, (1, total), 1)
        dead = (column >= lens[resp]) & (column < PLEN)
        scores = scores + (bias[...] + jnp.where(dead, NEGATIVE, 0.0))
        peak = jnp.max(scores, axis=1, keepdims=True)
        weights = jnp.exp((scores - peak) * SCALE)
        probs = (weights * (1.0 / jnp.sum(weights, axis=1, keepdims=True))).astype(BF)
        latent = dot(probs, even[part, :, :LAT]).astype(BF)
        start = pl.multiple_of(resp * RLEN, RLEN)
        for p in range(HEADS // 2):
            lat[2 * p, pl.ds(start, RLEN), :] = latent[p * RLEN : (p + 1) * RLEN]
            lat[2 * p + 1, pl.ds(start, RLEN), :] = latent[
                rows // 2 + p * RLEN : rows // 2 + (p + 1) * RLEN
            ]

    @pl.when(step == pl.num_programs(0) - 1)
    def _():
        for head in range(HEADS):
            out[:, head * VHEAD : (head + 1) * VHEAD] = dot(lat[head], w_uv[head]).astype(BF)


def attention(lens, queries, keys, own, w_uv):
    count = queries.shape[0]
    spec = pltpu.PrefetchScalarGridSpec(
        num_scalar_prefetch=1,
        grid=(count // 2,),
        in_specs=[
            pl.BlockSpec((2, RLEN, HEADS * ENTRY), lambda i, n: (i, 0, 0)),
            pl.BlockSpec((2, PLEN, ENTRY), lambda i, n: (i, 0, 0)),
            pl.BlockSpec((2, RLEN, ENTRY), lambda i, n: (i, 0, 0)),
            pl.BlockSpec((HEADS, LAT, VHEAD), lambda i, n: (0, 0, 0)),
        ],
        out_specs=pl.BlockSpec((GROUP, HEADS * VHEAD), lambda i, n: (0, 0)),
        scratch_shapes=[
            pltpu.VMEM((HEADS, GROUP, LAT), BF),
            pltpu.VMEM((2, PLEN + RLEN, 640), BF),
            pltpu.VMEM((2, PLEN + RLEN, 640), BF),
            pltpu.VMEM((HEADS * RLEN, PLEN + RLEN), F32),
        ],
    )
    return pl.pallas_call(
        attention_kernel,
        grid_spec=spec,
        out_shape=jax.ShapeDtypeStruct((GROUP, HEADS * VHEAD), BF),
        compiler_params=params(),
        name="attention",
    )(lens, queries, keys, own, w_uv)


def project_kernel(side, first_match, *refs):
    heads, weights = refs[:10], refs[10:20]
    out, v_all, w_all, v_sem, w_sem = refs[20:]
    half = GROUP // 2
    cut = HALF // 2

    def head_copies(k):
        copies = []
        for core in range(2):
            own = heads[5 * core : 5 * core + 5]
            base = core * GROUP
            if k == 2:
                copies.append((own[2], v_all.at[k, pl.ds(base, half)], 4 * core + 2))
                copies.append((own[3], v_all.at[k, pl.ds(base + half, half)], 8 + core))
            else:
                source = own[k] if k < 2 else own[4]
                copies.append((source, v_all.at[k, pl.ds(base, GROUP)], 4 * core + k))
        return [pltpu.make_async_copy(a, b, v_sem.at[n]) for a, b, n in copies]

    def weight_copies(k, which):
        own = weights[5 * which : 5 * which + 5]
        copies = []
        if k == 2:
            copies.append((own[2], w_all.at[k, pl.ds(0, cut)], 2))
            copies.append((own[3], w_all.at[k, pl.ds(cut, cut)], 4))
        else:
            source = own[k] if k < 2 else own[4]
            copies.append((source, w_all.at[k], k))
        return [pltpu.make_async_copy(a, b, w_sem.at[n]) for a, b, n in copies]

    for k in range(NZ):
        for which in range(2):

            @pl.when(side[0] == which)
            def _(k=k, which=which):
                for copy in weight_copies(k, which):
                    copy.start()

        for copy in head_copies(k):
            copy.start()
    for k in range(NZ):
        for copy in weight_copies(k, 0):
            copy.wait()
        for copy in head_copies(k):
            copy.wait()
    tile = 256
    for t in range(2 * GROUP // tile):
        total = None
        for k in range(NZ):
            match = (first_match[0] + 2 * NZ - k) % NY
            term = dot_nt(w_all[k], v_all[match, t * tile : (t + 1) * tile, :])
            total = term if total is None else total + term
        out[:, t * tile : (t + 1) * tile] = total.astype(BF)


def project(side, first_match, heads, weights):
    vmem = pl.BlockSpec(memory_space=pltpu.VMEM)
    smem = pl.BlockSpec(memory_space=pltpu.SMEM)
    anywhere = pl.BlockSpec(memory_space=pl.ANY)
    return pl.pallas_call(
        project_kernel,
        in_specs=[smem, smem] + [anywhere] * 20,
        out_specs=vmem,
        out_shape=jax.ShapeDtypeStruct((HALF, 2 * GROUP), BF),
        scratch_shapes=[
            pltpu.VMEM((NY, 2 * GROUP, HEADS * VHEAD), BF),
            pltpu.VMEM((NZ, HALF, HEADS * VHEAD), BF),
            pltpu.SemaphoreType.DMA((10,)),
            pltpu.SemaphoreType.DMA((5,)),
        ],
        compiler_params=params(),
        name="project",
    )(side, first_match, *heads, *weights)


def dispatch_kernel(core, kept, sent, kept_far, sent_far, rest, place, out, attended):
    near = kept[:, :GROUP].astype(F32) + sent[...].astype(F32)
    far = kept_far[...].astype(F32) + sent_far[...].astype(F32)
    lower = core[0] == 0
    attended[:HALF, :] = jnp.where(lower, near, far).astype(BF)
    attended[HALF:, :] = jnp.where(lower, far, near).astype(BF)
    rows = lax.broadcasted_iota(jnp.int32, (GROUP, GROUP), 0)
    select = jnp.where(rows == place[...], 1.0, 0.0).astype(BF)
    moved = dot(select, rest[...])
    out[:, :SLICE] = (moved[:, :SLICE] + dot_nt(select, attended[...])).astype(BF)
    out[:, SLICE:] = moved[:, SLICE:].astype(BF)


def dispatch(core, kept, sent, kept_far, sent_far, rest, place):
    vmem = pl.BlockSpec(memory_space=pltpu.VMEM)
    return pl.pallas_call(
        dispatch_kernel,
        in_specs=[pl.BlockSpec(memory_space=pltpu.SMEM)] + [vmem] * 6,
        out_specs=vmem,
        out_shape=jax.ShapeDtypeStruct((GROUP, SLICE + 128), BF),
        scratch_shapes=[pltpu.VMEM((SLICE, GROUP), BF)],
        compiler_params=params(),
        name="dispatch",
    )(core, kept, sent, kept_far, sent_far, rest, place)


def enter_kernel(tokens, gain, weights, out):
    hidden = tokens[:, :SLICE].astype(F32)
    square = jnp.sum(hidden * hidden, axis=1, keepdims=True)
    scaled = (hidden * gain[...]).astype(BF)
    for k in range(FF // HID):
        out[:, k * 2 * HID : (k + 1) * 2 * HID] = dot(
            scaled, weights[k * SLICE : (k + 1) * SLICE, :]
        ).astype(BF)
    high = square.astype(BF)
    low = (square - high.astype(F32)).astype(BF)
    lane = lax.broadcasted_iota(jnp.int32, (GROUP, 128), 1)
    out[:, 2 * FF :] = jnp.where(lane < 64, high.astype(F32), low.astype(F32)).astype(BF)


def enter(tokens, gain, weights):
    vmem = pl.BlockSpec(memory_space=pltpu.VMEM)
    return pl.pallas_call(
        enter_kernel,
        in_specs=[vmem] * 3,
        out_specs=vmem,
        out_shape=jax.ShapeDtypeStruct((GROUP, MESSAGE), BF),
        compiler_params=params(),
        name="enter",
    )(tokens, gain, weights)


def act_kernel(parts, out):
    total = parts[:BLOCK, :].astype(F32)
    for k in range(1, GROUP // BLOCK):
        total = total + parts[k * BLOCK : (k + 1) * BLOCK, :].astype(F32)
    square = total[:, 2 * FF : 2 * FF + 1] + total[:, 2 * FF + 64 : 2 * FF + 65]
    scale = lax.rsqrt(square * (1.0 / DIM) + EPSILON)
    for k in range(FF // HID):
        gate = total[:, 2 * k * HID : (2 * k + 1) * HID] * scale
        up = total[:, (2 * k + 1) * HID : (2 * k + 2) * HID] * scale
        act = (gate / (1.0 + jnp.exp(-gate)) * up).astype(BF)
        for b in range(GROUP // BLOCK):
            out[b * BLOCK : (b + 1) * BLOCK, k * HID : (k + 1) * HID] = act


def activate(parts):
    vmem = pl.BlockSpec(memory_space=pltpu.VMEM)
    return pl.pallas_call(
        act_kernel,
        in_specs=[vmem],
        out_specs=vmem,
        out_shape=jax.ShapeDtypeStruct((GROUP, FF), BF),
        compiler_params=params(),
        name="activate",
    )(parts)


def leave_kernel(act, w_out, tokens, out):
    result = dot(act[...], w_out[0]).astype(BF).astype(F32)
    parts = tokens[:, SLICE:].astype(F32)
    share = ROUTED * (parts[:, 1:2] + parts[:, 2:3] + parts[:, 3:4])
    out[...] = (tokens[:, :SLICE].astype(F32) + share * result).astype(BF)


def leave(act, w_out, tokens):
    vmem = pl.BlockSpec(memory_space=pltpu.VMEM)
    return pl.pallas_call(
        leave_kernel,
        in_specs=[vmem] * 3,
        out_specs=vmem,
        out_shape=jax.ShapeDtypeStruct((GROUP, SLICE), BF),
        compiler_params=params(),
        name="leave",
    )(act, w_out, tokens)


def restore_kernel(rows, place, out):
    lane = lax.broadcasted_iota(jnp.int32, (BLOCK, GROUP), 1)
    data = rows[...]
    for k in range(DIM // SLICE):
        select = jnp.where(lane == place[...] + k * CAP, 1.0, 0.0).astype(BF)
        out[:, k * SLICE : (k + 1) * SLICE] = dot(select, data).astype(BF)


def restore(rows, place):
    vmem = pl.BlockSpec(memory_space=pltpu.VMEM)
    return pl.pallas_call(
        restore_kernel,
        in_specs=[vmem] * 2,
        out_specs=vmem,
        out_shape=jax.ShapeDtypeStruct((BLOCK, DIM), BF),
        compiler_params=params(),
        name="restore",
    )(rows, place)


def body(
    queries,
    resp_latent,
    prompt_cache,
    prompt_len,
    w_uv,
    w_o,
    residual,
    norm_gain,
    expert_in,
    expert_out,
    routes,
    gate_probs,
):
    r = lax.axis_index("resp")
    e = lax.axis_index("exp")
    z, x, c = r // 4, (r // 2) % 2, r % 2
    y, h = e // 2, e % 2

    keys = lax.all_gather(prompt_cache, "resp", axis=0, tiled=True)

    near_w = ring(lax.ppermute(w_o.T, ("resp", "exp"), crossing()), over_z)
    side_w = ring(over_resp(near_w[0], 0, 1, 0), over_z)

    both = jnp.concatenate([expert_in[0, 0], expert_in[0, 1]], axis=1)
    enter_w = lax.all_to_all(both, "exp", split_axis=0, concat_axis=0, tiled=True)

    first = gate_probs.astype(BF)
    second = (gate_probs - first.astype(F32)).astype(BF)
    third = (gate_probs - first.astype(F32) - second.astype(F32)).astype(BF)
    extra = jnp.concatenate([routes.astype(BF), first, second, third], axis=1)
    extra = jnp.pad(extra, ((0, 0), (0, 124)))
    extra = jnp.broadcast_to(extra[None], (8, BLOCK, 128))
    rest = residual.reshape(BLOCK, 8, SLICE).transpose(1, 0, 2)
    rest = jnp.concatenate([rest, extra], axis=2).reshape(GROUP, SLICE + 128)
    rest = lax.all_to_all(rest, "exp", split_axis=0, concat_axis=0, tiled=True)

    table = rest[:, SLICE].astype(jnp.int32).reshape(8, BLOCK)
    earlier = jnp.arange(BLOCK)[None, :] < jnp.arange(BLOCK)[:, None]
    same = (table[:, :, None] == table[:, None, :]) & earlier[None]
    rank = jnp.sum(same.astype(jnp.int32), axis=2)
    place = table * (8 * CAP) + jnp.arange(8, dtype=jnp.int32)[:, None] * CAP + rank
    place = place.reshape(1, GROUP)
    own_same = (routes == routes[:, 0][None, :]) & earlier
    own_place = routes * (8 * CAP) + jnp.sum(own_same.astype(jnp.int32), axis=1, keepdims=True)
    gain = lax.dynamic_slice_in_dim(norm_gain, e * SLICE, SLICE, 0).reshape(1, SLICE)

    values = attention(prompt_len, queries, keys, resp_latent, w_uv)
    heads = ring(values, over_y)
    heads = heads + [over_resp(piece, 0, 0, 1) for piece in heads]

    first_match = ((y + z) % NY).reshape(1).astype(jnp.int32)
    away = jnp.where(h == x, 1, 0).reshape(1).astype(jnp.int32)
    sent = project(away, first_match, heads, near_w + side_w)
    kept = project(1 - away, first_match, heads, near_w + side_w)
    sent_near = over_exp(sent[:, :GROUP], 0, 1)
    sent_far = lax.ppermute(sent[:, GROUP:], ("resp", "exp"), diagonal())
    kept_far = over_resp(kept[:, GROUP:], 0, 0, 1)
    core = c.reshape(1).astype(jnp.int32)
    sorted_rows = dispatch(core, kept, sent_near, kept_far, sent_far, rest, place)
    tokens = lax.all_to_all(sorted_rows, "resp", split_axis=0, concat_axis=0, tiled=True)
    message = enter(tokens, gain, enter_w)
    message = lax.all_to_all(message, "exp", split_axis=0, concat_axis=0, tiled=True)
    act = activate(message)
    act = lax.all_to_all(act, "exp", split_axis=0, concat_axis=0, tiled=True)
    finished = leave(act, expert_out, tokens)
    finished = lax.all_to_all(
        finished.reshape(128, CAP, SLICE),
        ("resp", "exp"),
        split_axis=0,
        concat_axis=0,
        tiled=True,
    ).reshape(GROUP, SLICE)
    return restore(finished, own_place)


def solution(mesh):
    return jax.shard_map(
        body,
        mesh=mesh,
        in_specs=(
            P("resp", None, "exp"),
            P("resp", None, None),
            P("resp", None, None),
            P(),
            P("exp", None, None),
            P("exp", "resp"),
            P(("resp", "exp"), None),
            P(),
            P("resp", None, None, "exp"),
            P("resp", None, "exp"),
            P(("resp", "exp"), None),
            P(("resp", "exp"), None),
        ),
        out_specs=P(("resp", "exp"), None),
        check_vma=False,
    )
```

time: 550 us -> 358 us (0.65)
  waiting for transfers between devices: 393 us -> 114 us
  starting transfers between devices: 10.5 us -> 90.2 us
  Pallas kernels: 0 us -> 55.1 us
  matrix products: 53.2 us -> 0 us
  blocking collectives: 37.2 us -> 53 us
  local copies, waits for them, and re-layouts: 34.9 us -> 22.9 us
    all_gather x4 -> x1, waiting for transfers between devices: 249 us -> 5.67 us  [body(): keys = lax.all_gather(prompt_cache, 'resp', axis=0, tiled=True)]
    reduce_scatter x1 -> x0, waiting for transfers between devices: 115 us -> none  [body(): lax.psum_scatter(term.reshape(block_rows * lax.axis_size('exp'), w_o.shap...]
    ppermute x0 -> x22, waiting for transfers between devices: none -> 75.4 us  [the longest x15 34.4 us: over_resp(): return lax.ppermute(x, 'resp', resp_perm(dz, dx, dc))]
    ppermute x0 -> x22, starting transfers between devices: none -> 68.2 us  [the longest x15 51.4 us: over_resp(): return lax.ppermute(x, 'resp', resp_perm(dz, dx, dc))]
    pallas_call x0 -> x8, Pallas kernels: none -> 55.1 us  [the longest x2 19.1 us: project(): pl.pallas_call(project_kernel, in_specs=[smem, smem] + [anywhere] * 20, o...]
    dot_general x11 -> x0, matrix products: 53.2 us -> none  [the longest x1 16.9 us: body(): jnp.einsum('rets,sc->ertc', value_grid, w_o, preferred_element_type=jnp.f...]
    all_to_all x2, blocking collectives: 37.2 us -> 53 us  [the longest x1 34 us: body(): lax.all_to_all(message, 'exp', split_axis=0, concat_axis=0, tiled=True)]
    convert_element_type x5 -> x1, local copies, waits for them, and re-layouts: 14.9 us -> 0.08 us  [body(): table = rest[:, SLICE].astype(jnp.int32).reshape(8, BLOCK)]
  transfers between devices with their start and end apart: 7 -> 27, of which waited for: 7 -> 11; matrix products, arithmetic and copies ran while one was open for 3% -> 7% of each run, Pallas kernels for 0% -> 11%
where the time goes in v1:
time: 358 us; the launch traced here: 356 us
  waiting for transfers between devices  114 us (32%)
  starting transfers between devices  90.2 us (25%)
  Pallas kernels  55.1 us (15%)
  blocking collectives  53 us (15%)
  local copies, waits for them, and re-layouts  22.9 us (6%)
  between operations  13.6 us (4%)
  other arithmetic  7.79 us (2%)
    ppermute x15, starting transfers between devices, over_resp(): return lax.ppermute(x, 'resp', resp_perm(dz, dx, dc))  51.4 us
    ppermute x15, waiting for transfers between devices, over_resp(): return lax.ppermute(x, 'resp', resp_perm(dz, dx, dc))  34.4 us
    all_to_all x1, blocking collectives, body(): lax.all_to_all(message, 'exp', split_axis=0, concat_axis=0, tiled=True)  34 us
    ppermute x5, waiting for transfers between devices, over_exp(): return lax.ppermute(x, 'exp', exp_perm(dy, dh))  29.7 us
    pallas_call x2, Pallas kernels, project(): pl.pallas_call(project_kernel, in_specs=[smem, smem] + [anywhere] * 20, o...  19.1 us
    all_to_all x1, blocking collectives, body(): act = lax.all_to_all(act, 'exp', split_axis=0, concat_axis=0, tiled=True)  19 us
    all_to_all x1, waiting for transfers between devices, body(): lax.all_to_all(finished.reshape(128, CAP, SLICE), ('resp', 'exp'), split_...  17.6 us
    pallas_call x1, Pallas kernels, attention(): pl.pallas_call(attention_kernel, grid_spec=spec, out_shape=jax.ShapeDtype...  14.6 us
  transfers between devices with their start and end apart: 27, of which 11 were waited for; matrix products, arithmetic and copies ran while one was open for 7% of the time, Pallas kernels for 11%

profile of v1, /device:TPU:1, one launch (start us, length us, event | category | flops | bytes accessed | tf_op | source)
XLA Modules:
  0.0 356.3 jit_solution(14346983983462213782)
XLA Ops:
  6.5 0.7 all-gather.2.cloned.1.call-update
  7.3 8.3 %collective-permute-start.9 = (bf16[448,1024]{1,0:T(8,128)(2,1)}, bf16[448,1024]{1,0:T(8,128)(2,1)}, u32[]{:S(2)}, u32[]{:S(2)}) collective-permute-start(bf16[448,1024]{1,0:T(8,128)(2,1)} %bitcast.38), channel_id=1, source_target_pairs={{0,0},{1,1},{2,96},{3,97},{4,64},{5,65},{6,32},{7,33},{8,8},{9,9},... | collective-permute-start | bytes 2752520 | tf_op jit(solution)/shard_map/ppermute | solution.py:394
  15.6 0.9 convert_reduce_fusion.2
  16.5 0.7 fusion.4
  17.2 0.7 bitcast_add_fusion
  18.1 1.3 copy.44
  19.4 1.1 pad_maximum_fusion.1
  20.6 4.8 %all-to-all-start = ((bf16[8,64,1024]{2,1,0:T(8,128)(2,1)}), bf16[8,64,1024]{2,1,0:T(8,128)(2,1)}, u32[]{:S(2)}, u32[]{:S(2)}) async-start(bf16[8,64,1024]{2,1,0:T(8,128)(2,1)} %pad_maximum_fusion.1), calls=%async_computation | async-start | bytes 2097152 | tf_op jit(solution)/shard_map/all_to_all | solution.py:408
  25.4 38.0 %collective-permute-start.10 = (bf16[448,1024]{1,0:T(8,128)(2,1)}, bf16[448,1024]{1,0:T(8,128)(2,1)}, u32[]{:S(2)}, u32[]{:S(2)}) collective-permute-start(bf16[448,1024]{1,0:T(8,128)(2,1)} %collective-permute-done.9.refs_10_), channel_id=1, source_target_pairs={{0,32},{8,40},{16,48},{24,56},{32,64},{40,72},{48,80},{56,88},{64,... | collective-permute-start | bytes 2752520 | tf_op jit(solution)/shard_map/ppermute | solution.py:48
  63.4 1.3 collective-permute-start.14
  64.7 3.5 fusion.2
  68.2 5.7 %all-gather.2.cloned.1.call-done = bf16[16,128,576]{1,2,0:T(8,128)(2,1)} async-done(((bf16[1,128,576]{1,2,0:T(8,128)(2,1)}), bf16[16,128,576]{1,2,0:T(8,128)(2,1)}) %all-gather.2.cloned.1.call-update) | async-done | bytes 2359312 | tf_op jit(solution)/shard_map/all_gather | solution.py:392
  73.9 4.3 %copy.37.keys = bf16[16,128,576]{2,1,0:T(8,128)(2,1)} copy(bf16[16,128,576]{1,2,0:T(8,128)(2,1)} %all-gather.2.cloned.1.call-done) | data formatting | bytes 4718592 | tf_op jit(solution)/shard_map/all_gather | solution.py:392
  78.2 14.6 %attention.1.refs_0_ = bf16[512,1024]{1,0:T(8,128)(2,1)} custom-call(s32[16]{0:T(128)} %lens.1, bf16[16,32,4608]{2,1,0:T(8,128)(2,1)} %q_ref.1, bf16[16,128,576]{2,1,0:T(8,128)(2,1)} %copy.37.keys, bf16[16,32,576]{2,1,0:T(8,128)(2,1)} %own.1, bf16[8,512,128]{2,1,0:T(8,128)(2,1)} %w_uv.1), custom_call_target="tpu_custom_call" | custom-call | tf_op jit(solution)/shard_map/attention/pallas_call | solution.py:172
  92.8 2.2 pad_maximum_fusion
  95.0 6.7 %all-to-all-start.2 = ((bf16[8,896,256]{2,1,0:T(8,128)(2,1)}), bf16[8,896,256]{2,1,0:T(8,128)(2,1)}, u32[]{:S(2)}, u32[]{:S(2)}) async-start(bf16[8,896,256]{2,1,0:T(8,128)(2,1)} %pad_maximum_fusion), calls=%async_computation.2 | async-start | bytes 7340032 | tf_op jit(solution)/shard_map/all_to_all | solution.py:398
  101.7 1.1 collective-permute-start.12
  103.2 2.3 collective-permute-start.17
  105.5 2.7 collective-permute-start.2
  108.2 1.0 slice.50
  109.3 13.8 %collective-permute-done.12.refs_14_ = bf16[448,1024]{1,0:T(8,128)(2,1)S(1)} collective-permute-done((bf16[448,1024]{1,0:T(8,128)(2,1)}, bf16[448,1024]{1,0:T(8,128)(2,1)S(1)}, u32[]{:S(2)}, u32[]{:S(2)}) %collective-permute-start.12) | collective-permute-done | bytes 917536 | tf_op jit(solution)/shard_map/ppermute | solution.py:48
  123.1 2.1 collective-permute-done.15.refs_16_
  125.2 0.7 collective-permute-start.13
  125.9 16.8 %collective-permute-done.17.refs_19_ = bf16[448,1024]{1,0:T(8,128)(2,1)S(1)} collective-permute-done((bf16[448,1024]{1,0:T(8,128)(2,1)}, bf16[448,1024]{1,0:T(8,128)(2,1)S(1)}, u32[]{:S(2)}, u32[]{:S(2)}) %collective-permute-start.17) | collective-permute-done | bytes 917536 | tf_op jit(solution)/shard_map/ppermute | solution.py:48
  142.8 2.7 collective-permute-start.18
  145.6 19.6 %collective-permute-done.2.refs_4_ = bf16[512,1024]{1,0:T(8,128)(2,1)} collective-permute-done((bf16[512,1024]{1,0:T(8,128)(2,1)S(1)}, bf16[512,1024]{1,0:T(8,128)(2,1)}, u32[]{:S(2)}, u32[]{:S(2)}) %collective-permute-start.2) | collective-permute-done | bytes 1048608 | tf_op jit(solution)/shard_map/ppermute | solution.py:52
  165.2 1.7 collective-permute-start.4
  167.0 1.1 slice.49
  168.1 1.2 collective-permute-start.1
  170.1 1.5 collective-permute-start.3
  171.6 0.8 copy-done.11
  172.4 0.6 collective-permute-start.8
  173.0 10.1 %collective-permute-done.1.refs_2_ = bf16[256,1024]{1,0:T(8,128)(2,1)} collective-permute-done((bf16[256,1024]{1,0:T(8,128)(2,1)S(1)}, bf16[256,1024]{1,0:T(8,128)(2,1)}, u32[]{:S(2)}, u32[]{:S(2)}) %collective-permute-start.1) | collective-permute-done | bytes 524320 | tf_op jit(solution)/shard_map/ppermute | solution.py:52
  183.0 0.8 collective-permute-start.6
  183.8 0.7 collective-permute-start.7
  184.8 0.9 collective-permute-done.6.refs_7_
  185.7 0.7 collective-permute-done.7.refs_8_
  186.4 9.5 %project.3 = bf16[448,1024]{1,0:T(8,128)(2,1)} custom-call(s32[1]{0:T(128)} %bitcast.1.side, s32[1]{0:T(128)} %bitcast.2.first_match, bf16[512,1024]{1,0:T(8,128)(2,1)} %attention.1.refs_0_, bf16[512,1024]{1,0:T(8,128)(2,1)} %copy-done.3, bf16[256,1024]{1,0:T(8,128)(2,1)} %collective-permute-done.1.refs_2_, ...), custom_call_target="tpu_custom_call" | custom-call | tf_op jit(solution)/shard_map/project/pallas_call | solution.py:240
  196.0 1.2 fusion.3
  197.2 2.8 collective-permute-start.19
  200.0 9.5 %project.2.kept = bf16[448,1024]{1,0:T(8,128)(2,1)} custom-call(s32[1]{0:T(128)S(6)} %sub.21.side, s32[1]{0:T(128)} %bitcast.2.first_match, bf16[512,1024]{1,0:T(8,128)(2,1)} %attention.1.refs_0_, bf16[512,1024]{1,0:T(8,128)(2,1)} %copy-done.3, bf16[256,1024]{1,0:T(8,128)(2,1)} %collective-permute-done.1.refs_2_, ...), custom_call_target="tpu_custom_call" | custom-call | tf_op jit(solution)/shard_map/project/pallas_call | solution.py:240
  209.5 1.1 slice.55
  210.6 0.7 collective-permute-start.20
  211.6 1.1 fusion
  213.2 0.6 add_add_fusion.place
  213.8 11.2 %collective-permute-done.21.sent_far = bf16[448,512]{1,0:T(8,128)(2,1)S(1)} collective-permute-done((bf16[448,512]{1,0:T(8,128)(2,1)S(1)}, bf16[448,512]{1,0:T(8,128)(2,1)S(1)}, u32[]{:S(2)}, u32[]{:S(2)}) %collective-permute-start.21) | collective-permute-done | bytes 458784 | tf_op jit(solution)/shard_map/ppermute | solution.py:429
  225.0 0.8 copy-done.14
  225.8 4.2 %dispatch.1 = bf16[512,1024]{1,0:T(8,128)(2,1)} custom-call(s32[1]{0:T(128)} %bitcast.core, bf16[448,1024]{1,0:T(8,128)(2,1)} %project.2.kept, bf16[448,512]{1,0:T(8,128)(2,1)} %copy-done.12, bf16[448,512]{1,0:T(8,128)(2,1)} %copy-done.13, bf16[448,512]{1,0:T(8,128)(2,1)} %copy-done.14, bf16[512,1024]{1,0:T(8,128)(2,1)} %bitcast.5.rest, ...), custom_call_target="tpu_custom_call" | custom-call | tf_op jit(solution)/shard_map/dispatch/pallas_call | solution.py:271
  230.0 3.6 %all-to-all-start.1 = ((bf16[16,32,1024]{2,1,0:T(8,128)(2,1)}), bf16[16,32,1024]{2,1,0:T(8,128)(2,1)S(1)}, u32[]{:S(2)}, u32[]{:S(2)}) async-start(bf16[16,32,1024]{2,1,0:T(8,128)(2,1)} %bitcast.33), calls=%async_computation.1 | async-start | bytes 2097152 | tf_op jit(solution)/shard_map/all_to_all | solution.py:433
  233.6 0.8 dynamic_slice.3
  234.4 0.6 reshape.113.gain
  235.0 14.5 %all-to-all-done.1 = bf16[16,32,1024]{2,1,0:T(8,128)(2,1)S(1)} async-done(((bf16[16,32,1024]{2,1,0:T(8,128)(2,1)}), bf16[16,32,1024]{2,1,0:T(8,128)(2,1)S(1)}, u32[]{:S(2)}, u32[]{:S(2)}) %all-to-all-start.1) | async-done | bytes 1048608 | tf_op jit(solution)/shard_map/all_to_all | solution.py:433
  249.5 1.0 copy-done.1
  250.5 6.1 %enter.1 = bf16[512,2176]{1,0:T(8,128)(2,1)} custom-call(bf16[512,1024]{1,0:T(8,128)(2,1)} %bitcast.25, f32[1,896]{1,0:T(1,128)} %reshape.113.gain, bf16[7168,256]{1,0:T(8,128)(2,1)} %bitcast.10.weights), custom_call_target="tpu_custom_call" | custom-call | tf_op jit(solution)/shard_map/enter/pallas_call | solution.py:298
  256.6 34.0 %all_to_all.54 = bf16[8,64,2176]{2,1,0:T(8,128)(2,1)} all-to-all(bf16[8,64,2176]{2,1,0:T(8,128)(2,1)} %bitcast.27), channel_id=1, replica_groups=mesh['resp'=16,'exp'=8] {'exp'}, dimensions={0} | all-to-all | bytes 4456448 | tf_op jit(solution)/shard_map/all_to_all | solution.py:435
  290.6 3.4 activate.1
  293.9 19.0 %all_to_all.55 = bf16[8,64,1024]{2,1,0:T(8,128)(2,1)} all-to-all(bf16[8,64,1024]{2,1,0:T(8,128)(2,1)} %bitcast.32), channel_id=1, replica_groups=mesh['resp'=16,'exp'=8] {'exp'}, dimensions={0} | all-to-all | bytes 2097152 | tf_op jit(solution)/shard_map/all_to_all | solution.py:437
  312.9 4.3 %leave.1 = bf16[512,896]{1,0:T(8,128)(2,1)} custom-call(bf16[512,1024]{1,0:T(8,128)(2,1)} %bitcast.31, bf16[1,1024,896]{2,1,0:T(8,128)(2,1)} %w_out.1, bf16[512,1024]{1,0:T(8,128)(2,1)} %bitcast.26), custom_call_target="tpu_custom_call" | custom-call | tf_op jit(solution)/shard_map/leave/pallas_call | solution.py:343
  317.2 2.5 reshape.114
  319.7 6.8 %all-to-all-start.5 = ((bf16[128,4,896]{2,1,0:T(4,128)(2,1)}), bf16[128,4,896]{2,1,0:T(4,128)(2,1)S(1)}, u32[]{:S(2)}, u32[]{:S(2)}) async-start(bf16[128,4,896]{2,1,0:T(4,128)(2,1)} %reshape.114), calls=%async_computation.5 | async-start | bytes 1835008 | tf_op jit(solution)/shard_map/all_to_all | solution.py:439
  326.6 0.7 copy.40.place
  327.3 17.6 %all-to-all-done.5 = bf16[128,4,896]{2,1,0:T(4,128)(2,1)S(1)} async-done(((bf16[128,4,896]{2,1,0:T(4,128)(2,1)}), bf16[128,4,896]{2,1,0:T(4,128)(2,1)S(1)}, u32[]{:S(2)}, u32[]{:S(2)}) %all-to-all-start.5) | async-done | bytes 917536 | tf_op jit(solution)/shard_map/all_to_all | solution.py:439
  344.8 1.1 reshape.115.rows
  346.0 3.5 restore.1
  (65 shorter events, 2.4 us)
Async XLA Ops:
  6.5 67.4 %all-gather.2.cloned.1.call-start = ((), (), s32[]{:S(2)}) async-start(), calls=%async_computation.6 | async-start | bytes 2506752 | tf_op jit(solution)/shard_map/all_gather | solution.py:392
  7.3 18.2 %collective-permute-start.9 = (bf16[448,1024]{1,0:T(8,128)(2,1)}, bf16[448,1024]{1,0:T(8,128)(2,1)}, u32[]{:S(2)}, u32[]{:S(2)}) collective-permute-start(bf16[448,1024]{1,0:T(8,128)(2,1)} %bitcast.38), channel_id=1, source_target_pairs={{0,0},{1,1},{2,96},{3,97},{4,64},{5,65},{6,32},{7,33},{8,8},{9,9},... | collective-permute-start | bytes 2752520 | tf_op jit(solution)/shard_map/ppermute | solution.py:394
  20.6 74.5 %all-to-all-start = ((bf16[8,64,1024]{2,1,0:T(8,128)(2,1)}), bf16[8,64,1024]{2,1,0:T(8,128)(2,1)}, u32[]{:S(2)}, u32[]{:S(2)}) async-start(bf16[8,64,1024]{2,1,0:T(8,128)(2,1)} %pad_maximum_fusion.1), calls=%async_computation | async-start | bytes 2097152 | tf_op jit(solution)/shard_map/all_to_all | solution.py:408
  25.4 80.1 %collective-permute-start.10 = (bf16[448,1024]{1,0:T(8,128)(2,1)}, bf16[448,1024]{1,0:T(8,128)(2,1)}, u32[]{:S(2)}, u32[]{:S(2)}) collective-permute-start(bf16[448,1024]{1,0:T(8,128)(2,1)} %collective-permute-done.9.refs_10_), channel_id=1, source_target_pairs={{0,32},{8,40},{16,48},{24,56},{32,64},{40,72},{48,80},{56,88},{64,... | collective-permute-start | bytes 2752520 | tf_op jit(solution)/shard_map/ppermute | solution.py:48
  63.4 39.4 %collective-permute-start.14 = (bf16[448,1024]{1,0:T(8,128)(2,1)}, bf16[448,1024]{1,0:T(8,128)(2,1)}, u32[]{:S(2)}, u32[]{:S(2)}) collective-permute-start(bf16[448,1024]{1,0:T(8,128)(2,1)} %collective-permute-done.9.refs_10_), channel_id=1, source_target_pairs={{0,16},{8,24},{16,0},{24,8},{32,48},{40,56},{48,32},{56,40},{64,80... | collective-permute-start | bytes 2752520 | tf_op jit(solution)/shard_map/ppermute | solution.py:48
  78.2 14.6 %copy-start.2 = (bf16[1,1,7168,128]{3,2,1,0:T(8,128)(2,1)S(1)}, bf16[1,1,7168,128]{3,2,1,0:T(8,128)(2,1)}, u32[]{:S(2)}) copy-start(bf16[1,1,7168,128]{3,2,1,0:T(8,128)(2,1)} %get-tuple-element.8) | copy-start | bytes 5505028
  92.8 50.0 %collective-permute-start = (bf16[512,1024]{1,0:T(8,128)(2,1)}, bf16[512,1024]{1,0:T(8,128)(2,1)S(1)}, u32[]{:S(2)}, u32[]{:S(2)}) collective-permute-start(bf16[512,1024]{1,0:T(8,128)(2,1)} %attention.1.refs_0_), channel_id=1, source_target_pairs={{0,2},{1,3},{2,4},{3,5},{4,6},{5,7},{6,0},{7,1},{8,10},{9,11},{10,... | collective-permute-start | bytes 3145736 | tf_op jit(solution)/shard_map/ppermute | solution.py:52
  95.0 10.5 %copy-start = (bf16[512,1024]{1,0:T(8,128)(2,1)S(1)}, bf16[512,1024]{1,0:T(8,128)(2,1)}, u32[]{:S(2)}) copy-start(bf16[512,1024]{1,0:T(8,128)(2,1)} %attention.1.refs_0_) | copy-start | bytes 3145732
  95.0 134.9 %all-to-all-start.2 = ((bf16[8,896,256]{2,1,0:T(8,128)(2,1)}), bf16[8,896,256]{2,1,0:T(8,128)(2,1)}, u32[]{:S(2)}, u32[]{:S(2)}) async-start(bf16[8,896,256]{2,1,0:T(8,128)(2,1)} %pad_maximum_fusion), calls=%async_computation.2 | async-start | bytes 7340032 | tf_op jit(solution)/shard_map/all_to_all | solution.py:398
  101.7 21.3 %collective-permute-start.12 = (bf16[448,1024]{1,0:T(8,128)(2,1)}, bf16[448,1024]{1,0:T(8,128)(2,1)S(1)}, u32[]{:S(2)}, u32[]{:S(2)}) collective-permute-start(bf16[448,1024]{1,0:T(8,128)(2,1)} %collective-permute-done.9.refs_10_), channel_id=1, source_target_pairs={{0,96},{8,104},{16,112},{24,120},{32,0},{40,8},{48,16},{56,24},{64... | collective-permute-start | bytes 2752520 | tf_op jit(solution)/shard_map/ppermute | solution.py:48
  102.9 22.3 %collective-permute-start.15 = (bf16[448,1024]{1,0:T(8,128)(2,1)}, bf16[448,1024]{1,0:T(8,128)(2,1)S(1)}, u32[]{:S(2)}, u32[]{:S(2)}) collective-permute-start(bf16[448,1024]{1,0:T(8,128)(2,1)} %collective-permute-done.14.refs_15_), channel_id=1, source_target_pairs={{0,32},{8,40},{16,48},{24,56},{32,64},{40,72},{48,80},{56,88},{64,... | collective-permute-start | bytes 2752520 | tf_op jit(solution)/shard_map/ppermute | solution.py:48
  103.2 39.5 %collective-permute-start.17 = (bf16[448,1024]{1,0:T(8,128)(2,1)}, bf16[448,1024]{1,0:T(8,128)(2,1)S(1)}, u32[]{:S(2)}, u32[]{:S(2)}) collective-permute-start(bf16[448,1024]{1,0:T(8,128)(2,1)} %collective-permute-done.14.refs_15_), channel_id=1, source_target_pairs={{0,96},{8,104},{16,112},{24,120},{32,0},{40,8},{48,16},{56,24},{64... | collective-permute-start | bytes 2752520 | tf_op jit(solution)/shard_map/ppermute | solution.py:48
  105.5 59.7 %collective-permute-start.2 = (bf16[512,1024]{1,0:T(8,128)(2,1)S(1)}, bf16[512,1024]{1,0:T(8,128)(2,1)}, u32[]{:S(2)}, u32[]{:S(2)}) collective-permute-start(bf16[512,1024]{1,0:T(8,128)(2,1)S(1)} %copy-done), channel_id=1, source_target_pairs={{0,6},{1,7},{2,0},{3,1},{4,2},{5,3},{6,4},{7,5},{8,14},{9,15},{10,... | collective-permute-start | bytes 3145736 | tf_op jit(solution)/shard_map/ppermute | solution.py:52
  123.1 45.0 %copy-start.4 = (bf16[448,1024]{1,0:T(8,128)(2,1)}, bf16[448,1024]{1,0:T(8,128)(2,1)S(1)}, u32[]{:S(2)}) copy-start(bf16[448,1024]{1,0:T(8,128)(2,1)S(1)} %collective-permute-done.12.refs_14_) | copy-start | bytes 2752516
  123.1 45.0 %collective-permute-start.11 = (bf16[224,1024]{1,0:T(8,128)(2,1)S(1)}, bf16[224,1024]{1,0:T(8,128)(2,1)S(1)}, u32[]{:S(2)}, u32[]{:S(2)}) collective-permute-start(bf16[224,1024]{1,0:T(8,128)(2,1)S(1)} %slice.50), channel_id=1, source_target_pairs={{0,32},{8,40},{16,48},{24,56},{32,64},{40,72},{48,80},{56,88},{64,... | collective-permute-start | bytes 1376264 | tf_op jit(solution)/shard_map/ppermute | solution.py:48
  125.2 44.1 %copy-start.5 = (bf16[448,1024]{1,0:T(8,128)(2,1)}, bf16[448,1024]{1,0:T(8,128)(2,1)S(1)}, u32[]{:S(2)}) copy-start(bf16[448,1024]{1,0:T(8,128)(2,1)S(1)} %collective-permute-done.15.refs_16_) | copy-start | bytes 2752516
  125.2 44.1 %collective-permute-start.13 = (bf16[224,1024]{1,0:T(8,128)(2,1)S(1)}, bf16[224,1024]{1,0:T(8,128)(2,1)S(1)}, u32[]{:S(2)}, u32[]{:S(2)}) collective-permute-start(bf16[224,1024]{1,0:T(8,128)(2,1)S(1)} %slice.51), channel_id=1, source_target_pairs={{0,96},{8,104},{16,112},{24,120},{32,0},{40,8},{48,16},{56,24},{64... | collective-permute-start | bytes 1376264 | tf_op jit(solution)/shard_map/ppermute | solution.py:48
  142.8 26.6 %copy-start.6 = (bf16[448,1024]{1,0:T(8,128)(2,1)}, bf16[448,1024]{1,0:T(8,128)(2,1)S(1)}, u32[]{:S(2)}) copy-start(bf16[448,1024]{1,0:T(8,128)(2,1)S(1)} %collective-permute-done.17.refs_19_) | copy-start | bytes 2752516
  142.8 26.9 %collective-permute-start.16 = (bf16[224,1024]{1,0:T(8,128)(2,1)S(1)}, bf16[224,1024]{1,0:T(8,128)(2,1)S(1)}, u32[]{:S(2)}, u32[]{:S(2)}) collective-permute-start(bf16[224,1024]{1,0:T(8,128)(2,1)S(1)} %slice.52), channel_id=1, source_target_pairs={{0,32},{8,40},{16,48},{24,56},{32,64},{40,72},{48,80},{56,88},{64,... | collective-permute-start | bytes 1376264 | tf_op jit(solution)/shard_map/ppermute | solution.py:48
  142.8 43.6 %copy-start.3 = (bf16[512,1024]{1,0:T(8,128)(2,1)}, bf16[512,1024]{1,0:T(8,128)(2,1)S(1)}, u32[]{:S(2)}) copy-start(bf16[512,1024]{1,0:T(8,128)(2,1)S(1)} %collective-permute-done.refs_1_) | copy-start | bytes 3145732
  142.8 28.8 %collective-permute-start.18 = (bf16[224,1024]{1,0:T(8,128)(2,1)S(1)}, bf16[224,1024]{1,0:T(8,128)(2,1)S(1)}, u32[]{:S(2)}, u32[]{:S(2)}) collective-permute-start(bf16[224,1024]{1,0:T(8,128)(2,1)S(1)} %slice.53), channel_id=1, source_target_pairs={{0,96},{8,104},{16,112},{24,120},{32,0},{40,8},{48,16},{56,24},{64... | collective-permute-start | bytes 1376264 | tf_op jit(solution)/shard_map/ppermute | solution.py:48
  165.2 19.5 %collective-permute-start.4 = (bf16[512,1024]{1,0:T(8,128)(2,1)S(1)}, bf16[512,1024]{1,0:T(8,128)(2,1)S(1)}, u32[]{:S(2)}, u32[]{:S(2)}) collective-permute-start(bf16[512,1024]{1,0:T(8,128)(2,1)S(1)} %copy-done), channel_id=1, source_target_pairs={{0,8},{8,0},{16,24},{24,16},{32,40},{40,32},{48,56},{56,48},{64,72... | collective-permute-start | bytes 3145736 | tf_op jit(solution)/shard_map/ppermute | solution.py:48
  168.1 1.6 copy-start.8
  168.1 14.9 %collective-permute-start.1 = (bf16[256,1024]{1,0:T(8,128)(2,1)S(1)}, bf16[256,1024]{1,0:T(8,128)(2,1)}, u32[]{:S(2)}, u32[]{:S(2)}) collective-permute-start(bf16[256,1024]{1,0:T(8,128)(2,1)S(1)} %slice.48), channel_id=1, source_target_pairs={{0,2},{1,3},{2,4},{3,5},{4,6},{5,7},{6,0},{7,1},{8,10},{9,11},{10,... | collective-permute-start | bytes 1572872 | tf_op jit(solution)/shard_map/ppermute | solution.py:52
  169.3 0.8 copy-start.9
  169.3 15.4 %collective-permute-start.5 = (bf16[512,1024]{1,0:T(8,128)(2,1)S(1)}, bf16[512,1024]{1,0:T(8,128)(2,1)}, u32[]{:S(2)}, u32[]{:S(2)}) collective-permute-start(bf16[512,1024]{1,0:T(8,128)(2,1)S(1)} %collective-permute-done.refs_1_), channel_id=1, source_target_pairs={{0,8},{8,0},{16,24},{24,16},{32,40},{40,32},{48,56},{56,48},{64,72... | collective-permute-start | bytes 3145736 | tf_op jit(solution)/shard_map/ppermute | solution.py:48
  170.1 1.5 copy-start.10
  170.1 13.7 %collective-permute-start.3 = (bf16[256,1024]{1,0:T(8,128)(2,1)S(1)}, bf16[256,1024]{1,0:T(8,128)(2,1)}, u32[]{:S(2)}, u32[]{:S(2)}) collective-permute-start(bf16[256,1024]{1,0:T(8,128)(2,1)S(1)} %slice.49), channel_id=1, source_target_pairs={{0,6},{1,7},{2,0},{3,1},{4,2},{5,3},{6,4},{7,5},{8,14},{9,15},{10,... | collective-permute-start | bytes 1572872 | tf_op jit(solution)/shard_map/ppermute | solution.py:52
  171.6 0.8 copy-start.11
  172.4 14.1 %collective-permute-start.8 = (bf16[512,1024]{1,0:T(8,128)(2,1)}, bf16[512,1024]{1,0:T(8,128)(2,1)}, u32[]{:S(2)}, u32[]{:S(2)}) collective-permute-start(bf16[512,1024]{1,0:T(8,128)(2,1)} %collective-permute-done.2.refs_4_), channel_id=1, source_target_pairs={{0,8},{8,0},{16,24},{24,16},{32,40},{40,32},{48,56},{56,48},{64,72... | collective-permute-start | bytes 3145736 | tf_op jit(solution)/shard_map/ppermute | solution.py:48
  183.0 2.7 collective-permute-start.6
  183.8 2.6 collective-permute-start.7
  184.7 1.7 copy-start.7
  197.2 16.6 %collective-permute-start.19 = (bf16[448,512]{1,0:T(8,128)(2,1)S(1)}, bf16[448,512]{1,0:T(8,128)(2,1)S(1)}, u32[]{:S(2)}, u32[]{:S(2)}) collective-permute-start(bf16[448,512]{1,0:T(8,128)(2,1)S(1)} %get-tuple-element.10), channel_id=1, source_target_pairs={{0,1},{1,0},{2,3},{3,2},{4,5},{5,4},{6,7},{7,6},{8,9},{9,8},{10,11... | collective-permute-start | bytes 1376264 | tf_op jit(solution)/shard_map/ppermute | solution.py:52
  210.6 3.2 collective-permute-start.20
  211.3 13.7 %collective-permute-start.21 = (bf16[448,512]{1,0:T(8,128)(2,1)S(1)}, bf16[448,512]{1,0:T(8,128)(2,1)S(1)}, u32[]{:S(2)}, u32[]{:S(2)}) collective-permute-start(bf16[448,512]{1,0:T(8,128)(2,1)S(1)} %get-tuple-element.9), channel_id=1, source_target_pairs={{0,9},{1,8},{2,11},{3,10},{4,13},{5,12},{6,15},{7,14},{8,1},{9,0},... | collective-permute-start | bytes 1376264 | tf_op jit(solution)/shard_map/ppermute | solution.py:429
  213.8 11.2 %copy-start.12 = (bf16[448,512]{1,0:T(8,128)(2,1)}, bf16[448,512]{1,0:T(8,128)(2,1)S(1)}, u32[]{:S(2)}) copy-start(bf16[448,512]{1,0:T(8,128)(2,1)S(1)} %collective-permute-done.19.sent) | copy-start | bytes 1376260
  213.8 11.2 %copy-start.13 = (bf16[448,512]{1,0:T(8,128)(2,1)}, bf16[448,512]{1,0:T(8,128)(2,1)S(1)}, u32[]{:S(2)}) copy-start(bf16[448,512]{1,0:T(8,128)(2,1)S(1)} %collective-permute-done.20.kept_far) | copy-start | bytes 1376260
  225.0 0.8 copy-start.14
  230.0 19.5 %all-to-all-start.1 = ((bf16[16,32,1024]{2,1,0:T(8,128)(2,1)}), bf16[16,32,1024]{2,1,0:T(8,128)(2,1)S(1)}, u32[]{:S(2)}, u32[]{:S(2)}) async-start(bf16[16,32,1024]{2,1,0:T(8,128)(2,1)} %bitcast.33), calls=%async_computation.1 | async-start | bytes 2097152 | tf_op jit(solution)/shard_map/all_to_all | solution.py:433
  249.5 1.0 copy-start.1
  319.7 25.1 %all-to-all-start.5 = ((bf16[128,4,896]{2,1,0:T(4,128)(2,1)}), bf16[128,4,896]{2,1,0:T(4,128)(2,1)S(1)}, u32[]{:S(2)}, u32[]{:S(2)}) async-start(bf16[128,4,896]{2,1,0:T(4,128)(2,1)} %reshape.114), calls=%async_computation.5 | async-start | bytes 1835008 | tf_op jit(solution)/shard_map/all_to_all | solution.py:439
Sparse Core Ops, SparseCore 0:
  9.1 64.7 all-gather.1

commit v2 on v1

v2 whole, which is shorter than its diff:
```python
import functools

import jax
import jax.numpy as jnp
from jax import lax
from jax.experimental import pallas as pl
from jax.experimental.pallas import tpu as pltpu
from jax.sharding import PartitionSpec as P

SCALE = 192.0 ** (-0.5)
ROUTED = 2.5
EPSILON = 1e-06
NEGATIVE = -1e30
NZ, NX, NC, NY, NH = 4, 2, 2, 4, 2
RLEN, ENTRY, LAT, PLEN, HEADS, VHEAD = 32, 576, 512, 128, 8, 128
DIM, SLICE, HALF, FF, HID = 7168, 896, 448, 1024, 128
GROUP, BLOCK, CAP = 512, 64, 4
TILES = 2 * FF // 128 + 1
WEIGHTS = SLICE + 4 * BLOCK
ALONG_Y = [[y * NH + h for y in range(NY)] for h in range(NH)]
BF = jnp.bfloat16
F32 = jnp.float32


def params(mebibytes):
    return pltpu.CompilerParams(vmem_limit_bytes=mebibytes * 1024 * 1024)


def resp_perm(dz, dx, dc):
    pairs = []
    for z in range(NZ):
        for x in range(NX):
            for c in range(NC):
                source = (z * NX + x) * NC + c
                target = (((z + dz) % NZ) * NX + (x ^ dx)) * NC + (c ^ dc)
                pairs.append((source, target))
    return pairs


def exp_perm(dy, dh):
    pairs = []
    for y in range(NY):
        for h in range(NH):
            pairs.append((y * NH + h, ((y + dy) % NY) * NH + (h ^ dh)))
    return pairs


def over_resp(x, dz, dx, dc):
    return lax.ppermute(x, "resp", resp_perm(dz, dx, dc))


def over_exp(x, dy, dh):
    return lax.ppermute(x, "exp", exp_perm(dy, dh))


def everywhere(move):
    def number(z, x, c, y, h):
        return ((z * NX + x) * NC + c) * (NY * NH) + y * NH + h

    return [
        (number(z, x, c, y, h), number(*move(z, x, c, y, h)))
        for z in range(NZ)
        for x in range(NX)
        for c in range(NC)
        for y in range(NY)
        for h in range(NH)
    ]


def over_all(x, move):
    return lax.ppermute(x, ("resp", "exp"), everywhere(move))


def other_core(x, step):
    return over_all(x, lambda z, x, c, y, h: (z, x, 1 - c, (y + step) % NY, h))


def over_z(x, step):
    return over_resp(x, step, 0, 0)


def over_y(x, step):
    return over_exp(x, step, 0)


def after(x, y):
    return lax.optimization_barrier((x, y))


def near_pieces(x, shift):
    return [shift(x, 1), shift(x, 3)]


def ring_pieces(x, near, shift):
    half = x.shape[0] // 2
    left, right = near
    return [x, left, shift(left[:half], 1), shift(right[half:], 3), right]


def dot(a, b):
    return lax.dot_general(a, b, (((1,), (0,)), ((), ())), preferred_element_type=F32)


def dot_nt(a, b):
    return lax.dot_general(a, b, (((1,), (1,)), ((), ())), preferred_element_type=F32)


def attention_kernel(lens, q_ref, keys, own, w_uv, out, lat, even, odd, bias):
    step = pl.program_id(0)
    rows = HEADS * RLEN
    total = PLEN + RLEN

    @pl.when(step == 0)
    def _():
        even[:, PLEN:, ENTRY:] = jnp.zeros((2, RLEN, 640 - ENTRY), BF)
        odd[:, :, :64] = jnp.zeros((2, total, 64), BF)
        column = lax.broadcasted_iota(jnp.int32, (rows, total), 1)
        token = lax.broadcasted_iota(jnp.int32, (rows, total), 0) % RLEN
        seen = (column < PLEN) | (column <= token + PLEN)
        bias[...] = jnp.where(seen, 0.0, NEGATIVE)

    for part in range(2):
        resp = 2 * step + part
        even[part, :PLEN, :] = keys[part]
        even[part, PLEN:, :ENTRY] = own[part]
        odd[part, :PLEN, 64:] = keys[part, :, :ENTRY]
        odd[part, PLEN:, 64:] = own[part]
        first = [q_ref[part, :, p * 1152 : p * 1152 + 640] for p in range(HEADS // 2)]
        second = [q_ref[part, :, p * 1152 + 512 : p * 1152 + 1152] for p in range(HEADS // 2)]
        scores = jnp.concatenate(
            [
                dot_nt(jnp.concatenate(first, axis=0), even[part]),
                dot_nt(jnp.concatenate(second, axis=0), odd[part]),
            ],
            axis=0,
        )
        column = lax.broadcasted_iota(jnp.int32, (1, total), 1)
        dead = (column >= lens[resp]) & (column < PLEN)
        scores = scores + (bias[...] + jnp.where(dead, NEGATIVE, 0.0))
        peak = jnp.max(scores, axis=1, keepdims=True)
        weights = jnp.exp((scores - peak) * SCALE)
        probs = (weights * (1.0 / jnp.sum(weights, axis=1, keepdims=True))).astype(BF)
        latent = dot(probs, even[part, :, :LAT]).astype(BF)
        start = pl.multiple_of(resp * RLEN, RLEN)
        for p in range(HEADS // 2):
            lat[2 * p, pl.ds(start, RLEN), :] = latent[p * RLEN : (p + 1) * RLEN]
            lat[2 * p + 1, pl.ds(start, RLEN), :] = latent[
                rows // 2 + p * RLEN : rows // 2 + (p + 1) * RLEN
            ]

    @pl.when(step == pl.num_programs(0) - 1)
    def _():
        for head in range(HEADS):
            out[:, head * VHEAD : (head + 1) * VHEAD] = dot(lat[head], w_uv[head]).astype(BF)


def attention(lens, queries, keys, own, w_uv):
    count = queries.shape[0]
    spec = pltpu.PrefetchScalarGridSpec(
        num_scalar_prefetch=1,
        grid=(count // 2,),
        in_specs=[
            pl.BlockSpec((2, RLEN, HEADS * ENTRY), lambda i, n: (i, 0, 0)),
            pl.BlockSpec((2, PLEN, 640), lambda i, n: (i, 0, 0)),
            pl.BlockSpec((2, RLEN, ENTRY), lambda i, n: (i, 0, 0)),
            pl.BlockSpec((HEADS, LAT, VHEAD), lambda i, n: (0, 0, 0)),
        ],
        out_specs=pl.BlockSpec((GROUP, HEADS * VHEAD), lambda i, n: (0, 0)),
        scratch_shapes=[
            pltpu.VMEM((HEADS, GROUP, LAT), BF),
            pltpu.VMEM((2, PLEN + RLEN, 640), BF),
            pltpu.VMEM((2, PLEN + RLEN, 640), BF),
            pltpu.VMEM((HEADS * RLEN, PLEN + RLEN), F32),
        ],
    )
    return pl.pallas_call(
        attention_kernel,
        grid_spec=spec,
        out_shape=jax.ShapeDtypeStruct((GROUP, HEADS * VHEAD), BF),
        compiler_params=params(56),
        name="attention",
    )(lens, queries, keys, own, w_uv)


def project_kernel(count, by_rows, match, picks, *refs):
    heads, weights = refs[:4], refs[4:14]
    outs = refs[14 : 14 + 2 * count]
    v_all, w_all, v_sem, w_sem = refs[14 + 2 * count :]
    cut = HALF // 2

    def weight_copies(n, part, k):
        own = weights[5 * part : 5 * part + 5]
        copies = []
        for side in range(2):
            if k == 2:
                source = own[2 + side]
            else:
                source = own[min(k, 1) if k < 2 else 4].at[pl.ds(side * cut, cut)]
            target = w_all.at[n, part, pl.ds(side * cut, cut)]
            copies.append(pltpu.make_async_copy(source, target, w_sem.at[n, part, side]))
        return copies

    def start_weights(n):
        for k in range(NZ):

            @pl.when(picks[n] == k)
            def _():
                for part in range(2):
                    for copy in weight_copies(n, part, k):
                        copy.start()

    def head_copy(k):
        target = v_all.at[k // 2, pl.ds((k % 2) * GROUP, GROUP)]
        return pltpu.make_async_copy(heads[k], target, v_sem.at[k])

    start_weights(0)
    for k in range(4):
        head_copy(k).start()
    for n in range(1, count):
        start_weights(n)
    for k in range(4):
        head_copy(k).wait()
    for n in range(count):
        for part in range(2):
            for copy in weight_copies(n, part, 0):
                copy.wait()
        for core in range(2):
            total = None
            for part in range(2):
                group = v_all.at[match[0] if part == 0 else 1 - match[0]]
                term = dot_nt(w_all[n, part], group[core * GROUP : (core + 1) * GROUP, :])
                total = term if total is None else total + term
            total = total.astype(BF)
            if by_rows:
                for side in range(2):
                    outs[side][:, core * GROUP : (core + 1) * GROUP] = total[
                        side * cut : (side + 1) * cut
                    ]
            else:
                outs[2 * n + core][...] = total


def project(match, picks, heads, weights, by_rows=False):
    count = picks.shape[0]
    shape = (HALF // 2, 2 * GROUP) if by_rows else (HALF, GROUP)
    vmem = pl.BlockSpec(memory_space=pltpu.VMEM)
    smem = pl.BlockSpec(memory_space=pltpu.SMEM)
    anywhere = pl.BlockSpec(memory_space=pl.ANY)
    return pl.pallas_call(
        functools.partial(project_kernel, count, by_rows),
        in_specs=[smem, smem] + [anywhere] * 14,
        out_specs=[vmem] * (2 * count),
        out_shape=[jax.ShapeDtypeStruct(shape, BF)] * (2 * count),
        scratch_shapes=[
            pltpu.VMEM((2, 2 * GROUP, HEADS * VHEAD), BF),
            pltpu.VMEM((count, 2, HALF, HEADS * VHEAD), BF),
            pltpu.SemaphoreType.DMA((4,)),
            pltpu.SemaphoreType.DMA((count, 2, 2)),
        ],
        compiler_params=params(56),
        name="project",
    )(match, picks, *heads, *weights)


def merge_kernel(ahead0, ahead1, behind0, behind1, left, right, *outs):
    cut = HALF // 2
    for core, (ahead, behind) in enumerate(((ahead0, behind0), (ahead1, behind1))):
        lanes = slice(core * GROUP, (core + 1) * GROUP)
        first = ahead[:cut, :].astype(F32) + left[:, lanes].astype(F32)
        last = behind[cut:, :].astype(F32) + right[:, lanes].astype(F32)
        outs[core][:cut, :] = first.astype(BF)
        outs[core][cut:, :] = ahead[cut:, :]
        outs[2 + core][:cut, :] = behind[:cut, :]
        outs[2 + core][cut:, :] = last.astype(BF)


def merge(pieces, left, right):
    vmem = pl.BlockSpec(memory_space=pltpu.VMEM)
    return pl.pallas_call(
        merge_kernel,
        in_specs=[vmem] * 6,
        out_specs=[vmem] * 4,
        out_shape=[jax.ShapeDtypeStruct((HALF, GROUP), BF)] * 4,
        compiler_params=params(56),
        name="merge",
    )(*pieces, left, right)


def dispatch_kernel(core, near0, near1, near3, far0, far1, far3, rest, place, out, attended):
    near = near0[...].astype(F32) + near1[...].astype(F32) + near3[...].astype(F32)
    far = far0[...].astype(F32) + far1[...].astype(F32) + far3[...].astype(F32)
    lower = core[0] == 0
    attended[:HALF, :] = jnp.where(lower, near, far).astype(BF)
    attended[HALF:, :] = jnp.where(lower, far, near).astype(BF)
    rows = lax.broadcasted_iota(jnp.int32, (GROUP, GROUP), 0)
    select = jnp.where(rows == place[...], 1.0, 0.0).astype(BF)
    moved = dot(select, rest[...])
    out[:, :SLICE] = (moved[:, :SLICE] + dot_nt(select, attended[...])).astype(BF)
    out[:, SLICE:] = moved[:, SLICE:].astype(BF)


def dispatch(core, parts, rest, place):
    vmem = pl.BlockSpec(memory_space=pltpu.VMEM)
    return pl.pallas_call(
        dispatch_kernel,
        in_specs=[pl.BlockSpec(memory_space=pltpu.SMEM)] + [vmem] * 8,
        out_specs=vmem,
        out_shape=jax.ShapeDtypeStruct((GROUP, SLICE + 128), BF),
        scratch_shapes=[pltpu.VMEM((SLICE, GROUP), BF)],
        compiler_params=params(56),
        name="dispatch",
    )(core, *parts, rest, place)


def enter_kernel(half, tokens, gain, kept, come, out):
    hidden = tokens[:, :SLICE].astype(F32)
    square = jnp.sum(hidden * hidden, axis=1, keepdims=True)
    scaled = (hidden * gain[...]).astype(BF)

    def store(tile, value):
        for b in range(GROUP // BLOCK):
            start = pl.multiple_of((b * TILES + tile) * BLOCK, BLOCK)
            out[pl.ds(start, BLOCK), :] = value[b * BLOCK : (b + 1) * BLOCK]

    for k in range(NY):
        for weights, own in ((kept, half[0]), (come, 1 - half[0])):
            both = dot(scaled, weights[k, :SLICE, :]).astype(BF)
            for side in range(2):
                store((k * NH + own) * 2 + side, both[:, side * HID : (side + 1) * HID])
    high = square.astype(BF)
    low = (square - high.astype(F32)).astype(BF)
    lane = lax.broadcasted_iota(jnp.int32, (GROUP, 128), 1)
    store(TILES - 1, jnp.where(lane < 64, high.astype(F32), low.astype(F32)).astype(BF))


def enter(half, tokens, gain, kept, come):
    vmem = pl.BlockSpec(memory_space=pltpu.VMEM)
    return pl.pallas_call(
        enter_kernel,
        in_specs=[pl.BlockSpec(memory_space=pltpu.SMEM)] + [vmem] * 4,
        out_specs=vmem,
        out_shape=jax.ShapeDtypeStruct((GROUP * TILES, 128), BF),
        compiler_params=params(20),
        name="enter",
    )(half, tokens, gain, kept, come)


def act_kernel(parts, out):
    def total(tile):
        value = jnp.zeros((BLOCK, 128), F32)
        for k in range(GROUP // BLOCK):
            start = (k * TILES + tile) * BLOCK
            value = value + parts[start : start + BLOCK, :].astype(F32)
        return value

    square = total(TILES - 1)
    square = square[:, :1] + square[:, 64:65]
    scale = lax.rsqrt(square * (1.0 / DIM) + EPSILON)
    for k in range(FF // HID):
        gate = total(2 * k) * scale
        act = (gate / (1.0 + jnp.exp(-gate)) * (total(2 * k + 1) * scale)).astype(BF)
        for b in range(GROUP // BLOCK):
            out[b * BLOCK : (b + 1) * BLOCK, k * HID : (k + 1) * HID] = act


def activate(parts):
    vmem = pl.BlockSpec(memory_space=pltpu.VMEM)
    return pl.pallas_call(
        act_kernel,
        in_specs=[vmem],
        out_specs=vmem,
        out_shape=jax.ShapeDtypeStruct((GROUP, FF), BF),
        compiler_params=params(16),
        name="activate",
    )(parts)


def leave_kernel(act, w_out, tokens, out):
    result = dot(act[...], w_out[0]).astype(BF).astype(F32)
    parts = tokens[:, SLICE:].astype(F32)
    share = ROUTED * (parts[:, 1:2] + parts[:, 2:3] + parts[:, 3:4])
    out[...] = (tokens[:, :SLICE].astype(F32) + share * result).astype(BF)


def leave(act, w_out, tokens):
    vmem = pl.BlockSpec(memory_space=pltpu.VMEM)
    return pl.pallas_call(
        leave_kernel,
        in_specs=[vmem] * 3,
        out_specs=vmem,
        out_shape=jax.ShapeDtypeStruct((GROUP, SLICE), BF),
        compiler_params=params(16),
        name="leave",
    )(act, w_out, tokens)


def restore_kernel(rows, place, out, select):
    lane = lax.broadcasted_iota(jnp.int32, (BLOCK, GROUP), 1)
    count = DIM // SLICE
    for k in range(count):
        select[k * BLOCK : (k + 1) * BLOCK, :] = jnp.where(
            lane == place[...] + k * CAP, 1.0, 0.0
        ).astype(BF)
    moved = dot(select[...], rows[...]).astype(BF)
    for k in range(count):
        out[:, k * SLICE : (k + 1) * SLICE] = moved[k * BLOCK : (k + 1) * BLOCK]


def restore(rows, place):
    vmem = pl.BlockSpec(memory_space=pltpu.VMEM)
    return pl.pallas_call(
        restore_kernel,
        in_specs=[vmem] * 2,
        out_specs=vmem,
        out_shape=jax.ShapeDtypeStruct((BLOCK, DIM), BF),
        scratch_shapes=[pltpu.VMEM((GROUP, GROUP), BF)],
        compiler_params=params(8),
        name="restore",
    )(rows, place)


def body(
    queries,
    resp_latent,
    prompt_cache,
    prompt_len,
    w_uv,
    w_o,
    residual,
    norm_gain,
    expert_in,
    expert_out,
    routes,
    gate_probs,
):
    r = lax.axis_index("resp")
    e = lax.axis_index("exp")
    z, x, c = r // 4, (r // 2) % 2, r % 2
    y, h = e // 2, e % 2

    cache = jnp.pad(prompt_cache, ((0, 0), (0, 0), (0, 640 - ENTRY)))
    keys = lax.all_gather(cache, "resp", axis=0, tiled=True)

    first_base = over_all(w_o.T, lambda z, x, c, y, h: (z, h, c, y, x))
    second_base = over_resp(first_base, 0, 1, 0)
    first_near = near_pieces(first_base, over_z)
    first_w = ring_pieces(first_base, first_near, over_z)
    second_near = near_pieces(second_base, over_z)
    second_w = ring_pieces(second_base, second_near, over_z)

    both = jnp.concatenate([expert_in[0, 0], expert_in[0, 1]], axis=1)

    first = gate_probs.astype(BF)
    second = (gate_probs - first.astype(F32)).astype(BF)
    third = (gate_probs - first.astype(F32) - second.astype(F32)).astype(BF)
    extra = jnp.concatenate([routes.astype(BF), first, second, third], axis=1)
    extra = jnp.pad(extra, ((0, 0), (0, 124)))
    extra = jnp.broadcast_to(extra[None], (8, BLOCK, 128))
    rest = residual.reshape(BLOCK, 8, SLICE).transpose(1, 0, 2)
    rest = jnp.concatenate([rest, extra], axis=2).reshape(8, 4 * BLOCK, 256)
    both = jnp.concatenate([both.reshape(8, SLICE, 256), rest], axis=1)
    both, _ = after(both, first_base)
    both = lax.all_to_all(
        both, "exp", split_axis=0, concat_axis=0, axis_index_groups=ALONG_Y, tiled=True
    ).reshape(NY, NH, WEIGHTS, 256)

    def half_of(which):
        return lax.dynamic_index_in_dim(both, which, 1, keepdims=False)


    values = attention(prompt_len, queries, keys, resp_latent, w_uv)
    values, _ = after(values, first_near + [second_base])
    others = over_exp(values, 0, 1)
    gone, _ = after(half_of(1 - h), [others] + second_near + first_w)
    come, kept = over_exp(gone, 0, 1), half_of(h)
    rest = [data[:, SLICE:] for data in (kept, come)]
    rest = jnp.stack(
        [jnp.where(h == 0, rest[0], rest[1]), jnp.where(h == 0, rest[1], rest[0])], axis=1
    ).reshape(GROUP, SLICE + 128)
    others, _ = after(others, second_near + first_w)
    heads = [values, over_resp(values, 0, 0, 1), others, over_resp(others, 0, 0, 1)]

    table = rest[:, SLICE].astype(jnp.int32).reshape(8, BLOCK)
    earlier = jnp.arange(BLOCK)[None, :] < jnp.arange(BLOCK)[:, None]
    same = (table[:, :, None] == table[:, None, :]) & earlier[None]
    rank = jnp.sum(same.astype(jnp.int32), axis=2)
    place = table * (8 * CAP) + jnp.arange(8, dtype=jnp.int32)[:, None] * CAP + rank
    place = place.reshape(1, GROUP)
    gain = lax.dynamic_slice_in_dim(norm_gain, e * SLICE, SLICE, 0).reshape(1, SLICE)
    own_same = (routes == routes[:, 0][None, :]) & earlier
    own_place = routes * (8 * CAP) + jnp.sum(own_same.astype(jnp.int32), axis=1, keepdims=True)

    match = jnp.where(h == x, 0, 1).reshape(1).astype(jnp.int32)
    pick = [((z - y - dy + 2 * NY) % NY).astype(jnp.int32) for dy in range(NY)]
    top, bottom = project(match, jnp.stack(pick[2:3]), heads, first_w + second_w, True)
    from_left = over_exp(top, 1, 0)
    from_right = over_exp(bottom, 3, 0)
    order = jnp.stack([pick[1], pick[3], pick[0]])
    pieces = project(match, order, heads, first_w + second_w)
    near1, far1, near3, far3 = merge(pieces[:4], from_left, from_right)
    parts = [
        pieces[4],
        over_exp(near1, 1, 0),
        over_exp(near3, 3, 0),
        other_core(pieces[5], 0),
        other_core(far1, 1),
        other_core(far3, 3),
    ]
    core = c.reshape(1).astype(jnp.int32)
    sorted_rows = dispatch(core, parts, rest, place)
    tokens = lax.all_to_all(sorted_rows, "resp", split_axis=0, concat_axis=0, tiled=True)
    message = enter(h.reshape(1).astype(jnp.int32), tokens, gain, kept, come)
    message = lax.all_to_all(message, "exp", split_axis=0, concat_axis=0, tiled=True)
    act = activate(message)
    act = lax.all_to_all(act, "exp", split_axis=0, concat_axis=0, tiled=True)
    finished = leave(act, expert_out, tokens)
    finished = lax.all_to_all(
        finished.reshape(128, CAP, SLICE),
        ("resp", "exp"),
        split_axis=0,
        concat_axis=0,
        tiled=True,
    ).reshape(GROUP, SLICE)
    return restore(finished, own_place)


def solution(mesh):
    return jax.shard_map(
        body,
        mesh=mesh,
        in_specs=(
            P("resp", None, "exp"),
            P("resp", None, None),
            P("resp", None, None),
            P(),
            P("exp", None, None),
            P("exp", "resp"),
            P(("resp", "exp"), None),
            P(),
            P("resp", None, None, "exp"),
            P("resp", None, "exp"),
            P(("resp", "exp"), None),
            P(("resp", "exp"), None),
        ),
        out_specs=P(("resp", "exp"), None),
        check_vma=False,
    )
```

time: 358 us -> 289 us (0.81)
  waiting for transfers between devices: 114 us -> 80.3 us
  starting transfers between devices: 90.2 us -> 63.6 us
  Pallas kernels: 55.1 us -> 47 us
    ppermute x15 -> x11, starting transfers between devices: 51.4 us -> 20.8 us  [over_resp(): return lax.ppermute(x, 'resp', resp_perm(dz, dx, dc))]
    ppermute x5 -> x6, waiting for transfers between devices: 29.7 us -> 3.39 us  [over_exp(): return lax.ppermute(x, 'exp', exp_perm(dy, dh))]
    ppermute x15 -> x11, waiting for transfers between devices: 34.4 us -> 17.6 us  [over_resp(): return lax.ppermute(x, 'resp', resp_perm(dz, dx, dc))]
    all_to_all x2 -> x1, waiting for transfers between devices: 0.01 us -> 12.8 us  [body(): lax.all_to_all(both, 'exp', split_axis=0, concat_axis=0, axis_index_group...]
    ppermute x2 -> x4, starting transfers between devices: 8.58 us -> 16.6 us  [over_all(): return lax.ppermute(x, ('resp', 'exp'), everywhere(move))]
    all_to_all x2 -> x1, starting transfers between devices: 11.5 us -> 5.06 us  [body(): lax.all_to_all(both, 'exp', split_axis=0, concat_axis=0, axis_index_group...]
    ppermute x2 -> x4, waiting for transfers between devices: 11.2 us -> 6.28 us  [over_all(): return lax.ppermute(x, ('resp', 'exp'), everywhere(move))]
    all_gather x1 -> x0, local copies, waits for them, and re-layouts: 4.34 us -> none  [body(): keys = lax.all_gather(prompt_cache, 'resp', axis=0, tiled=True)]
  transfers between devices with their start and end apart: 27 -> 25, of which waited for: 11 -> 9; matrix products, arithmetic and copies ran while one was open for 7% -> 9% of each run, Pallas kernels for 11% -> 12%
where the time goes in v2:
time: 289 us; the launch traced here: 288 us
  waiting for transfers between devices  80.3 us (28%)
  starting transfers between devices  63.6 us (22%)
  blocking collectives  52 us (18%)
  Pallas kernels  47 us (16%)
  local copies, waits for them, and re-layouts  23 us (8%)
  between operations  13.6 us (5%)
  other arithmetic  7.94 us (3%)
    all_to_all x1, blocking collectives, body(): lax.all_to_all(message, 'exp', split_axis=0, concat_axis=0, tiled=True)  34.5 us
    ppermute x11, starting transfers between devices, over_resp(): return lax.ppermute(x, 'resp', resp_perm(dz, dx, dc))  20.8 us
    all_to_all x1, waiting for transfers between devices, body(): lax.all_to_all(finished.reshape(128, CAP, SLICE), ('resp', 'exp'), split_...  18.2 us
    ppermute x11, waiting for transfers between devices, over_resp(): return lax.ppermute(x, 'resp', resp_perm(dz, dx, dc))  17.6 us
    all_to_all x1, blocking collectives, body(): act = lax.all_to_all(act, 'exp', split_axis=0, concat_axis=0, tiled=True)  17.6 us
    pallas_call x2, Pallas kernels, project(): pl.pallas_call(functools.partial(project_kernel, count, by_rows), in_spec...  17.5 us
    ppermute x4, starting transfers between devices, over_all(): return lax.ppermute(x, ('resp', 'exp'), everywhere(move))  16.6 us
    all_to_all x1, waiting for transfers between devices, body(): lax.all_to_all(sorted_rows, 'resp', split_axis=0, concat_axis=0, tiled=True)  15.1 us
  transfers between devices with their start and end apart: 25, of which 9 were waited for; matrix products, arithmetic and copies ran while one was open for 9% of the time, Pallas kernels for 12%

profile of v2, /device:TPU:1, one launch (start us, length us, event | category | flops | bytes accessed | tf_op | source)
XLA Modules:
  0.0 287.5 jit_solution(13017778837597852220)
XLA Ops:
  6.5 1.1 copy.40
  7.6 0.7 pad.8
  8.3 8.4 %collective-permute-start = (bf16[448,1024]{1,0:T(8,128)(2,1)}, bf16[448,1024]{1,0:T(8,128)(2,1)}, u32[]{:S(2)}, u32[]{:S(2)}) collective-permute-start(bf16[448,1024]{1,0:T(8,128)(2,1)} %bitcast.51), channel_id=1, source_target_pairs={{0,0},{1,16},{2,2},{3,18},{4,4},{5,20},{6,6},{7,22},{8,8},{9,24},{... | collective-permute-start | bytes 2752520 | tf_op jit(solution)/shard_map/ppermute | solution.py:71
  16.8 3.5 %fusion.2 = (bf16[1,1,7168,128]{3,2,1,0:T(8,128)(2,1)S(1)}, bf16[1,1,7168,128]{3,2,1,0:T(8,128)(2,1)}) fusion(bf16[1,2,7168,128]{3,2,1,0:T(8,128)(2,1)} %param.20), kind=kLoop, calls=%fused_computation.22 | loop fusion | bytes 7340032 | tf_op jit(solution)/shard_map/slice | solution.py:451
  20.3 0.2 convert_reduce_fusion.2
  20.8 1.1 pad_maximum_fusion.1
  21.9 1.7 reshape.117
  23.7 3.6 %pad_maximum_fusion = bf16[8,1152,256]{2,1,0:T(8,128)(2,1)} fusion(bf16[8,256,256]{2,1,0:T(8,128)(2,1)S(1)} %reshape.117, bf16[8,896,128]{2,1,0:T(8,128)(2,1)} %bitcast.45, bf16[8,896,128]{2,1,0:T(8,128)(2,1)S(1)} %bitcast.44), kind=kLoop, calls=%fused_computation | loop fusion | flops 14155776 | bytes 9437184 | tf_op jit(solution)/shard_map/concatenate | solution.py:461
  27.3 5.1 %all-to-all-start = ((bf16[8,1152,256]{2,1,0:T(8,128)(2,1)}), bf16[8,1152,256]{2,1,0:T(8,128)(2,1)}, u32[]{:S(2)}, u32[]{:S(2)}) async-start(bf16[8,1152,256]{2,1,0:T(8,128)(2,1)} %pad_maximum_fusion), calls=%async_computation | async-start | bytes 9437184 | tf_op jit(solution)/shard_map/all_to_all | solution.py:463
  32.3 2.5 collective-permute-start.1
  34.8 2.2 collective-permute-start.2
  37.0 5.8 %collective-permute-start.3 = (bf16[448,1024]{1,0:T(8,128)(2,1)}, bf16[448,1024]{1,0:T(8,128)(2,1)}, u32[]{:S(2)}, u32[]{:S(2)}) collective-permute-start(bf16[448,1024]{1,0:T(8,128)(2,1)} %collective-permute-done.refs_4_), channel_id=1, source_target_pairs={{0,16},{8,24},{16,0},{24,8},{32,48},{40,56},{48,32},{56,40},{64,80... | collective-permute-start | bytes 2752520 | tf_op jit(solution)/shard_map/ppermute | solution.py:49
  42.8 6.9 %all-gather.2.cloned.1.call-done.keys = bf16[16,128,640]{2,1,0:T(8,128)(2,1)} async-done(((bf16[1,128,640]{2,1,0:T(8,128)(2,1)}), bf16[16,128,640]{2,1,0:T(8,128)(2,1)}) %all-gather.2.cloned.1.call-update) | async-done | bytes 2621456 | tf_op jit(solution)/shard_map/all_gather | solution.py:442
  49.7 14.5 %attention.1.refs_0_ = bf16[512,1024]{1,0:T(8,128)(2,1)} custom-call(s32[16]{0:T(128)} %lens.1, bf16[16,32,4608]{2,1,0:T(8,128)(2,1)} %q_ref.1, bf16[16,128,640]{2,1,0:T(8,128)(2,1)} %all-gather.2.cloned.1.call-done.keys, bf16[16,32,576]{2,1,0:T(8,128)(2,1)} %own.1, bf16[8,512,128]{2,1,0:T(8,128)(2,1)} %w_uv.1), custom_call_target="tpu_custom_call" | custom-call | tf_op jit(solution)/shard_map/attention/pallas_call | solution.py:176
  64.2 2.9 %collective-permute-start.5 = (bf16[512,1024]{1,0:T(8,128)(2,1)}, bf16[512,1024]{1,0:T(8,128)(2,1)}, u32[]{:S(2)}, u32[]{:S(2)}) collective-permute-start(bf16[512,1024]{1,0:T(8,128)(2,1)} %attention.1.refs_0_), channel_id=1, source_target_pairs={{0,1},{1,0},{2,3},{3,2},{4,5},{5,4},{6,7},{7,6},{8,9},{9,8},{10,11... | collective-permute-start | bytes 3145736 | tf_op jit(solution)/shard_map/ppermute | solution.py:53
  67.2 0.3 collective-permute-start.6
  67.5 2.4 collective-permute-start.7
  69.9 0.8 slice.36
  70.7 0.8 slice.37
  71.5 2.7 collective-permute-start.9
  74.2 12.8 %all-to-all-done = bf16[8,1152,256]{2,1,0:T(8,128)(2,1)} async-done(((bf16[8,1152,256]{2,1,0:T(8,128)(2,1)}), bf16[8,1152,256]{2,1,0:T(8,128)(2,1)}, u32[]{:S(2)}, u32[]{:S(2)}) %all-to-all-start) | async-done | bytes 4718624 | tf_op jit(solution)/shard_map/all_to_all | solution.py:463
  87.1 4.2 %dynamic-slice_bitcast_fusion.1 = (bf16[4,1152,256]{2,1,0:T(8,128)(2,1)S(1)}, bf16[4,1152,256]{2,1,0:T(8,128)(2,1)}) fusion(bf16[4,2,1152,256]{3,2,1,0:T(8,128)(2,1)} %bitcast.11, s32[]{:T(128)S(6)} %select_n.79, s32[]{:T(128)S(6)} %select_n.80), kind=kLoop, calls=%fused_computation.2 | loop fusion | bytes 9437192 | tf_op jit(solution)/shard_map/jit(dynamic_index_in_dim)/squeeze | solution.py:468
  91.3 7.8 %collective-permute-done.8.refs_6_ = bf16[224,1024]{1,0:T(8,128)(2,1)} collective-permute-done((bf16[224,1024]{1,0:T(8,128)(2,1)}, bf16[224,1024]{1,0:T(8,128)(2,1)}, u32[]{:S(2)}, u32[]{:S(2)}) %collective-permute-start.8) | collective-permute-done | bytes 458784 | tf_op jit(solution)/shard_map/ppermute | solution.py:49
  99.0 0.5 collective-permute-start.20
  99.6 2.2 collective-permute-start.4
  101.8 1.8 slice.38
  103.7 0.9 collective-permute-start.11
  104.6 1.8 slice.39
  106.4 1.7 collective-permute-start.12
  108.2 8.6 %collective-permute-done.11.refs_11_ = bf16[224,1024]{1,0:T(8,128)(2,1)} collective-permute-done((bf16[224,1024]{1,0:T(8,128)(2,1)}, bf16[224,1024]{1,0:T(8,128)(2,1)}, u32[]{:S(2)}, u32[]{:S(2)}) %collective-permute-start.11) | collective-permute-done | bytes 458784 | tf_op jit(solution)/shard_map/ppermute | solution.py:49
  116.8 1.3 collective-permute-done.12.refs_12_
  118.0 5.8 %project.3 = (bf16[224,1024]{1,0:T(8,128)(2,1)}, bf16[224,1024]{1,0:T(8,128)(2,1)}) custom-call(s32[1]{0:T(128)} %bitcast.2.match, s32[1]{0:T(128)} %bitcast.7.picks, bf16[512,1024]{1,0:T(8,128)(2,1)} %attention.1.refs_0_, bf16[512,1024]{1,0:T(8,128)(2,1)} %collective-permute-done.4.refs_1_, bf16[512,1024]{1,0:T(8,128)(2,1)} %collective-permute-done.5.refs_2_, ...), custom_call_target="tpu_custom_call" | custom-call | tf_op jit(solution)/shard_map/project/pallas_call | solution.py:249
  123.8 1.3 collective-permute-start.13
  125.1 1.5 collective-permute-start.14
  126.8 0.6 pad_add_fusion.picks
  127.4 11.7 %project.2 = (bf16[448,512]{1,0:T(8,128)(2,1)}, bf16[448,512]{1,0:T(8,128)(2,1)}, bf16[448,512]{1,0:T(8,128)(2,1)}, bf16[448,512]{1,0:T(8,128)(2,1)}, bf16[448,5...) custom-call(s32[1]{0:T(128)} %bitcast.2.match, s32[3]{0:T(128)} %pad_add_fusion.picks, bf16[512,1024]{1,0:T(8,128)(2,1)} %attention.1.refs_0_, ...), custom_call_target="tpu_custom_call" | custom-call | tf_op jit(solution)/shard_map/project/pallas_call | solution.py:249
  139.2 2.3 collective-permute-start.17
  141.4 0.8 copy-done.6
  142.2 0.2 copy-done.7
  142.3 3.0 %merge.1 = (bf16[448,512]{1,0:T(8,128)(2,1)}, bf16[448,512]{1,0:T(8,128)(2,1)}, bf16[448,512]{1,0:T(8,128)(2,1)}, bf16[448,512]{1,0:T(8,128)(2,1)}) custom-call(bf16[448,512]{1,0:T(8,128)(2,1)} %get-tuple-element.24.ahead0, bf16[448,512]{1,0:T(8,128)(2,1)} %get-tuple-element.25.ahead1, bf16[448,512]{1,0:T(8,128)(2,1)} %get-tuple-element.26.behind0, ...), custom_call_target="tpu_custom_call" | custom-call | tf_op jit(solution)/shard_map/merge/pallas_call | solution.py:279
  145.3 2.7 collective-permute-start.16
  148.0 3.4 %collective-permute-done.20.come = bf16[4,1152,256]{2,1,0:T(8,128)(2,1)} collective-permute-done((bf16[4,1152,256]{2,1,0:T(8,128)(2,1)}, bf16[4,1152,256]{2,1,0:T(8,128)(2,1)}, u32[]{:S(2)}, u32[]{:S(2)}) %collective-permute-start.20) | collective-permute-done | bytes 2359328 | tf_op jit(solution)/shard_map/ppermute | solution.py:53
  151.4 5.9 %collective-permute-start.19 = (bf16[448,512]{1,0:T(8,128)(2,1)}, bf16[448,512]{1,0:T(8,128)(2,1)}, u32[]{:S(2)}, u32[]{:S(2)}) collective-permute-start(bf16[448,512]{1,0:T(8,128)(2,1)} %get-tuple-element.34), channel_id=1, source_target_pairs={{0,14},{1,15},{2,8},{3,9},{4,10},{5,11},{6,12},{7,13},{8,6},{9,7},... | collective-permute-start | bytes 1376264 | tf_op jit(solution)/shard_map/ppermute | solution.py:71
  157.3 1.1 select_bitcast_fusion.1
  158.6 1.1 copy.43
  159.6 1.7 reshape.119.rest
  161.4 0.2 fusion
  161.7 0.3 convert_reduce_fusion.1
  162.1 0.6 add_add_fusion.place
  162.7 6.3 %collective-permute-done.18.far1 = bf16[448,512]{1,0:T(8,128)(2,1)} collective-permute-done((bf16[448,512]{1,0:T(8,128)(2,1)}, bf16[448,512]{1,0:T(8,128)(2,1)}, u32[]{:S(2)}, u32[]{:S(2)}) %collective-permute-start.18) | collective-permute-done | bytes 458784 | tf_op jit(solution)/shard_map/ppermute | solution.py:71
  168.9 4.3 %dispatch.1 = bf16[512,1024]{1,0:T(8,128)(2,1)} custom-call(s32[1]{0:T(128)} %bitcast.1.core, bf16[448,512]{1,0:T(8,128)(2,1)} %get-tuple-element.23.near0, bf16[448,512]{1,0:T(8,128)(2,1)} %collective-permute-done.15.near1, bf16[448,512]{1,0:T(8,128)(2,1)} %collective-permute-done.16.near3, bf16[448,512]{1,0:T(8,128)(2,1)} %collective-permute-done.17.far0, ...), custom_call_target="tpu_custom_call" | custom-call | tf_op jit(solution)/shard_map/dispatch/pallas_call | solution.py:304
  173.3 5.5 %all-to-all-start.1 = ((bf16[16,32,1024]{2,1,0:T(8,128)(2,1)}), bf16[16,32,1024]{2,1,0:T(8,128)(2,1)S(1)}, u32[]{:S(2)}, u32[]{:S(2)}) async-start(bf16[16,32,1024]{2,1,0:T(8,128)(2,1)} %bitcast.46), calls=%async_computation.1 | async-start | bytes 2097152 | tf_op jit(solution)/shard_map/all_to_all | solution.py:511
  178.7 0.8 dynamic_slice.12
  179.5 15.1 %all-to-all-done.1 = bf16[16,32,1024]{2,1,0:T(8,128)(2,1)S(1)} async-done(((bf16[16,32,1024]{2,1,0:T(8,128)(2,1)}), bf16[16,32,1024]{2,1,0:T(8,128)(2,1)S(1)}, u32[]{:S(2)}, u32[]{:S(2)}) %all-to-all-start.1) | async-done | bytes 1048608 | tf_op jit(solution)/shard_map/all_to_all | solution.py:511
  194.6 4.1 %enter.1 = bf16[8704,128]{1,0:T(8,128)(2,1)S(1)} custom-call(s32[1]{0:T(128)} %bitcast.half, bf16[512,1024]{1,0:T(8,128)(2,1)S(1)} %bitcast.38, f32[1,896]{1,0:T(1,128)S(1)} %reshape.120.gain, bf16[4,1152,256]{2,1,0:T(8,128)(2,1)S(1)} %get-tuple-element.41.kept, bf16[4,1152,256]{2,1,0:T(8,128)(2,1)} %collective-permute-done.20.come), custom_call_target="tpu_custom_call" | custom-call | tf_op jit(solution)/shard_map/enter/pallas_call | solution.py:338
  198.7 34.5 %all_to_all.43 = bf16[8,1088,128]{2,1,0:T(8,128)(2,1)S(1)} all-to-all(bf16[8,1088,128]{2,1,0:T(8,128)(2,1)S(1)} %bitcast.40), channel_id=1, replica_groups=mesh['resp'=16,'exp'=8] {'exp'}, dimensions={0} | all-to-all | bytes 4456448 | tf_op jit(solution)/shard_map/all_to_all | solution.py:513
  233.2 0.6 activate.1
  233.8 17.6 %all_to_all.44 = bf16[8,64,1024]{2,1,0:T(8,128)(2,1)S(1)} all-to-all(bf16[8,64,1024]{2,1,0:T(8,128)(2,1)S(1)} %bitcast.43), channel_id=1, replica_groups=mesh['resp'=16,'exp'=8] {'exp'}, dimensions={0} | all-to-all | bytes 2097152 | tf_op jit(solution)/shard_map/all_to_all | solution.py:515
  251.4 1.3 leave.1
  252.6 1.1 reshape.121
  253.8 6.7 %all-to-all-start.4 = ((bf16[128,4,896]{2,1,0:T(4,128)(2,1)}), bf16[128,4,896]{2,1,0:T(4,128)(2,1)S(1)}, u32[]{:S(2)}, u32[]{:S(2)}) async-start(bf16[128,4,896]{2,1,0:T(4,128)(2,1)} %reshape.121), calls=%async_computation.4 | async-start | bytes 1835008 | tf_op jit(solution)/shard_map/all_to_all | solution.py:517
  260.6 18.2 %all-to-all-done.4 = bf16[128,4,896]{2,1,0:T(4,128)(2,1)S(1)} async-done(((bf16[128,4,896]{2,1,0:T(4,128)(2,1)}), bf16[128,4,896]{2,1,0:T(4,128)(2,1)S(1)}, u32[]{:S(2)}, u32[]{:S(2)}) %all-to-all-start.4) | async-done | bytes 917536 | tf_op jit(solution)/shard_map/all_to_all | solution.py:517
  278.8 0.2 reshape.122.rows
  279.0 1.7 restore.1
  (56 shorter events, 0.9 us)
Async XLA Ops:
  6.5 43.2 %all-gather.2.cloned.1.call-start = ((), (), s32[]{:S(2)}) async-start(), calls=%async_computation.5 | async-start | bytes 2785280 | tf_op jit(solution)/shard_map/all_gather | solution.py:442
  8.3 12.0 %copy-start.9 = (s32[64,1]{0,1:T(1,128)S(1)}, s32[64,1]{0,1:T(1,128)}, u32[]{:S(2)}) copy-start(s32[64,1]{0,1:T(1,128)} %param.22) | copy-start | bytes 772
  8.3 12.2 %copy-start.8 = (f32[64,1]{0,1:T(1,128)S(1)}, f32[64,1]{0,1:T(1,128)}, u32[]{:S(2)}) copy-start(f32[64,1]{0,1:T(1,128)} %param.23) | copy-start | bytes 772
  8.3 12.3 %copy-start.5 = (bf16[64,7168]{1,0:T(8,128)(2,1)S(1)}, bf16[64,7168]{1,0:T(8,128)(2,1)}, u32[]{:S(2)}) copy-start(bf16[64,7168]{1,0:T(8,128)(2,1)} %param.18) | copy-start | bytes 2752516
  8.3 18.9 %collective-permute-start = (bf16[448,1024]{1,0:T(8,128)(2,1)}, bf16[448,1024]{1,0:T(8,128)(2,1)}, u32[]{:S(2)}, u32[]{:S(2)}) collective-permute-start(bf16[448,1024]{1,0:T(8,128)(2,1)} %bitcast.51), channel_id=1, source_target_pairs={{0,0},{1,16},{2,2},{3,18},{4,4},{5,20},{6,6},{7,22},{8,8},{9,24},{... | collective-permute-start | bytes 2752520 | tf_op jit(solution)/shard_map/ppermute | solution.py:71
  27.3 59.8 %all-to-all-start = ((bf16[8,1152,256]{2,1,0:T(8,128)(2,1)}), bf16[8,1152,256]{2,1,0:T(8,128)(2,1)}, u32[]{:S(2)}, u32[]{:S(2)}) async-start(bf16[8,1152,256]{2,1,0:T(8,128)(2,1)} %pad_maximum_fusion), calls=%async_computation | async-start | bytes 9437184 | tf_op jit(solution)/shard_map/all_to_all | solution.py:463
  32.3 31.9 %collective-permute-start.1 = (bf16[448,1024]{1,0:T(8,128)(2,1)}, bf16[448,1024]{1,0:T(8,128)(2,1)S(1)}, u32[]{:S(2)}, u32[]{:S(2)}) collective-permute-start(bf16[448,1024]{1,0:T(8,128)(2,1)} %collective-permute-done.refs_4_), channel_id=1, source_target_pairs={{0,32},{8,40},{16,48},{24,56},{32,64},{40,72},{48,80},{56,88},{64,... | collective-permute-start | bytes 2752520 | tf_op jit(solution)/shard_map/ppermute | solution.py:49
  34.8 29.4 %collective-permute-start.2 = (bf16[448,1024]{1,0:T(8,128)(2,1)}, bf16[448,1024]{1,0:T(8,128)(2,1)S(1)}, u32[]{:S(2)}, u32[]{:S(2)}) collective-permute-start(bf16[448,1024]{1,0:T(8,128)(2,1)} %collective-permute-done.refs_4_), channel_id=1, source_target_pairs={{0,96},{8,104},{16,112},{24,120},{32,0},{40,8},{48,16},{56,24},{64... | collective-permute-start | bytes 2752520 | tf_op jit(solution)/shard_map/ppermute | solution.py:49
  37.0 27.2 %collective-permute-start.3 = (bf16[448,1024]{1,0:T(8,128)(2,1)}, bf16[448,1024]{1,0:T(8,128)(2,1)}, u32[]{:S(2)}, u32[]{:S(2)}) collective-permute-start(bf16[448,1024]{1,0:T(8,128)(2,1)} %collective-permute-done.refs_4_), channel_id=1, source_target_pairs={{0,16},{8,24},{16,0},{24,8},{32,48},{40,56},{48,32},{56,40},{64,80... | collective-permute-start | bytes 2752520 | tf_op jit(solution)/shard_map/ppermute | solution.py:49
  64.2 22.8 %copy-start.2 = (bf16[448,1024]{1,0:T(8,128)(2,1)}, bf16[448,1024]{1,0:T(8,128)(2,1)S(1)}, u32[]{:S(2)}) copy-start(bf16[448,1024]{1,0:T(8,128)(2,1)S(1)} %collective-permute-done.1.refs_5_) | copy-start | bytes 2752516
  64.2 22.8 %copy-start.3 = (bf16[448,1024]{1,0:T(8,128)(2,1)}, bf16[448,1024]{1,0:T(8,128)(2,1)S(1)}, u32[]{:S(2)}) copy-start(bf16[448,1024]{1,0:T(8,128)(2,1)S(1)} %collective-permute-done.2.refs_8_) | copy-start | bytes 2752516
  64.2 34.8 %collective-permute-start.5 = (bf16[512,1024]{1,0:T(8,128)(2,1)}, bf16[512,1024]{1,0:T(8,128)(2,1)}, u32[]{:S(2)}, u32[]{:S(2)}) collective-permute-start(bf16[512,1024]{1,0:T(8,128)(2,1)} %attention.1.refs_0_), channel_id=1, source_target_pairs={{0,1},{1,0},{2,3},{3,2},{4,5},{5,4},{6,7},{7,6},{8,9},{9,8},{10,11... | collective-permute-start | bytes 3145736 | tf_op jit(solution)/shard_map/ppermute | solution.py:53
  67.2 31.8 %collective-permute-start.6 = (bf16[448,1024]{1,0:T(8,128)(2,1)}, bf16[448,1024]{1,0:T(8,128)(2,1)}, u32[]{:S(2)}, u32[]{:S(2)}) collective-permute-start(bf16[448,1024]{1,0:T(8,128)(2,1)} %collective-permute-done.3.refs_9_), channel_id=1, source_target_pairs={{0,32},{8,40},{16,48},{24,56},{32,64},{40,72},{48,80},{56,88},{64,... | collective-permute-start | bytes 2752520 | tf_op jit(solution)/shard_map/ppermute | solution.py:49
  67.5 31.6 %collective-permute-start.7 = (bf16[448,1024]{1,0:T(8,128)(2,1)}, bf16[448,1024]{1,0:T(8,128)(2,1)}, u32[]{:S(2)}, u32[]{:S(2)}) collective-permute-start(bf16[448,1024]{1,0:T(8,128)(2,1)} %collective-permute-done.3.refs_9_), channel_id=1, source_target_pairs={{0,96},{8,104},{16,112},{24,120},{32,0},{40,8},{48,16},{56,24},{64... | collective-permute-start | bytes 2752520 | tf_op jit(solution)/shard_map/ppermute | solution.py:49
  70.7 28.3 %collective-permute-start.8 = (bf16[224,1024]{1,0:T(8,128)(2,1)}, bf16[224,1024]{1,0:T(8,128)(2,1)}, u32[]{:S(2)}, u32[]{:S(2)}) collective-permute-start(bf16[224,1024]{1,0:T(8,128)(2,1)} %slice.36), channel_id=1, source_target_pairs={{0,32},{8,40},{16,48},{24,56},{32,64},{40,72},{48,80},{56,88},{64,... | collective-permute-start | bytes 1376264 | tf_op jit(solution)/shard_map/ppermute | solution.py:49
  71.5 27.5 %collective-permute-start.9 = (bf16[224,1024]{1,0:T(8,128)(2,1)}, bf16[224,1024]{1,0:T(8,128)(2,1)}, u32[]{:S(2)}, u32[]{:S(2)}) collective-permute-start(bf16[224,1024]{1,0:T(8,128)(2,1)} %slice.37), channel_id=1, source_target_pairs={{0,96},{8,104},{16,112},{24,120},{32,0},{40,8},{48,16},{56,24},{64... | collective-permute-start | bytes 1376264 | tf_op jit(solution)/shard_map/ppermute | solution.py:49
  87.1 12.5 %copy-start.1 = (bf16[512,1024]{1,0:T(8,128)(2,1)S(1)}, bf16[512,1024]{1,0:T(8,128)(2,1)}, u32[]{:S(2)}) copy-start(bf16[512,1024]{1,0:T(8,128)(2,1)} %attention.1.refs_0_) | copy-start | bytes 3145732
  99.0 52.3 %collective-permute-start.20 = (bf16[4,1152,256]{2,1,0:T(8,128)(2,1)}, bf16[4,1152,256]{2,1,0:T(8,128)(2,1)}, u32[]{:S(2)}, u32[]{:S(2)}) collective-permute-start(bf16[4,1152,256]{2,1,0:T(8,128)(2,1)} %get-tuple-element.36), channel_id=1, source_target_pairs={{0,1},{1,0},{2,3},{3,2},{4,5},{5,4},{6,7},{7,6},{8,9},{9,8},{10,11... | collective-permute-start | bytes 7077896 | tf_op jit(solution)/shard_map/ppermute | solution.py:53
  99.6 18.4 %collective-permute-start.4 = (bf16[512,1024]{1,0:T(8,128)(2,1)S(1)}, bf16[512,1024]{1,0:T(8,128)(2,1)}, u32[]{:S(2)}, u32[]{:S(2)}) collective-permute-start(bf16[512,1024]{1,0:T(8,128)(2,1)S(1)} %copy-done.1), channel_id=1, source_target_pairs={{0,8},{8,0},{16,24},{24,16},{32,40},{40,32},{48,56},{56,48},{64,72... | collective-permute-start | bytes 3145736 | tf_op jit(solution)/shard_map/ppermute | solution.py:49
  101.8 16.2 %collective-permute-start.10 = (bf16[512,1024]{1,0:T(8,128)(2,1)}, bf16[512,1024]{1,0:T(8,128)(2,1)}, u32[]{:S(2)}, u32[]{:S(2)}) collective-permute-start(bf16[512,1024]{1,0:T(8,128)(2,1)} %collective-permute-done.5.refs_2_), channel_id=1, source_target_pairs={{0,8},{8,0},{16,24},{24,16},{32,40},{40,32},{48,56},{56,48},{64,72... | collective-permute-start | bytes 3145736 | tf_op jit(solution)/shard_map/ppermute | solution.py:49
  103.7 13.1 %collective-permute-start.11 = (bf16[224,1024]{1,0:T(8,128)(2,1)}, bf16[224,1024]{1,0:T(8,128)(2,1)}, u32[]{:S(2)}, u32[]{:S(2)}) collective-permute-start(bf16[224,1024]{1,0:T(8,128)(2,1)} %slice.38), channel_id=1, source_target_pairs={{0,32},{8,40},{16,48},{24,56},{32,64},{40,72},{48,80},{56,88},{64,... | collective-permute-start | bytes 1376264 | tf_op jit(solution)/shard_map/ppermute | solution.py:49
  106.4 11.6 %collective-permute-start.12 = (bf16[224,1024]{1,0:T(8,128)(2,1)}, bf16[224,1024]{1,0:T(8,128)(2,1)}, u32[]{:S(2)}, u32[]{:S(2)}) collective-permute-start(bf16[224,1024]{1,0:T(8,128)(2,1)} %slice.39), channel_id=1, source_target_pairs={{0,96},{8,104},{16,112},{24,120},{32,0},{40,8},{48,16},{56,24},{64... | collective-permute-start | bytes 1376264 | tf_op jit(solution)/shard_map/ppermute | solution.py:49
  123.8 17.6 %collective-permute-start.13 = (bf16[224,1024]{1,0:T(8,128)(2,1)}, bf16[224,1024]{1,0:T(8,128)(2,1)S(1)}, u32[]{:S(2)}, u32[]{:S(2)}) collective-permute-start(bf16[224,1024]{1,0:T(8,128)(2,1)} %get-tuple-element.28), channel_id=1, source_target_pairs={{0,2},{1,3},{2,4},{3,5},{4,6},{5,7},{6,0},{7,1},{8,10},{9,11},{10,... | collective-permute-start | bytes 1376264 | tf_op jit(solution)/shard_map/ppermute | solution.py:53
  125.1 16.3 %collective-permute-start.14 = (bf16[224,1024]{1,0:T(8,128)(2,1)}, bf16[224,1024]{1,0:T(8,128)(2,1)S(1)}, u32[]{:S(2)}, u32[]{:S(2)}) collective-permute-start(bf16[224,1024]{1,0:T(8,128)(2,1)} %get-tuple-element.29), channel_id=1, source_target_pairs={{0,6},{1,7},{2,0},{3,1},{4,2},{5,3},{6,4},{7,5},{8,14},{9,15},{10,... | collective-permute-start | bytes 1376264 | tf_op jit(solution)/shard_map/ppermute | solution.py:53
  139.2 23.5 %collective-permute-start.17 = (bf16[448,512]{1,0:T(8,128)(2,1)}, bf16[448,512]{1,0:T(8,128)(2,1)}, u32[]{:S(2)}, u32[]{:S(2)}) collective-permute-start(bf16[448,512]{1,0:T(8,128)(2,1)} %get-tuple-element.32), channel_id=1, source_target_pairs={{0,8},{1,9},{2,10},{3,11},{4,12},{5,13},{6,14},{7,15},{8,0},{9,1},... | collective-permute-start | bytes 1376264 | tf_op jit(solution)/shard_map/ppermute | solution.py:71
  141.4 0.8 copy-start.6
  141.4 0.9 copy-start.7
  145.3 17.3 %collective-permute-start.15 = (bf16[448,512]{1,0:T(8,128)(2,1)}, bf16[448,512]{1,0:T(8,128)(2,1)}, u32[]{:S(2)}, u32[]{:S(2)}) collective-permute-start(bf16[448,512]{1,0:T(8,128)(2,1)} %get-tuple-element.30), channel_id=1, source_target_pairs={{0,2},{1,3},{2,4},{3,5},{4,6},{5,7},{6,0},{7,1},{8,10},{9,11},{10,... | collective-permute-start | bytes 1376264 | tf_op jit(solution)/shard_map/ppermute | solution.py:53
  145.3 17.3 %collective-permute-start.16 = (bf16[448,512]{1,0:T(8,128)(2,1)}, bf16[448,512]{1,0:T(8,128)(2,1)}, u32[]{:S(2)}, u32[]{:S(2)}) collective-permute-start(bf16[448,512]{1,0:T(8,128)(2,1)} %get-tuple-element.31), channel_id=1, source_target_pairs={{0,6},{1,7},{2,0},{3,1},{4,2},{5,3},{6,4},{7,5},{8,14},{9,15},{10,... | collective-permute-start | bytes 1376264 | tf_op jit(solution)/shard_map/ppermute | solution.py:53
  148.0 20.9 %collective-permute-start.18 = (bf16[448,512]{1,0:T(8,128)(2,1)}, bf16[448,512]{1,0:T(8,128)(2,1)}, u32[]{:S(2)}, u32[]{:S(2)}) collective-permute-start(bf16[448,512]{1,0:T(8,128)(2,1)} %get-tuple-element.33), channel_id=1, source_target_pairs={{0,10},{1,11},{2,12},{3,13},{4,14},{5,15},{6,8},{7,9},{8,2},{9,3},... | collective-permute-start | bytes 1376264 | tf_op jit(solution)/shard_map/ppermute | solution.py:71
  151.4 17.5 %collective-permute-start.19 = (bf16[448,512]{1,0:T(8,128)(2,1)}, bf16[448,512]{1,0:T(8,128)(2,1)}, u32[]{:S(2)}, u32[]{:S(2)}) collective-permute-start(bf16[448,512]{1,0:T(8,128)(2,1)} %get-tuple-element.34), channel_id=1, source_target_pairs={{0,14},{1,15},{2,8},{3,9},{4,10},{5,11},{6,12},{7,13},{8,6},{9,7},... | collective-permute-start | bytes 1376264 | tf_op jit(solution)/shard_map/ppermute | solution.py:71
  161.3 7.6 %copy-start.4 = (bf16[512,1024]{1,0:T(8,128)(2,1)}, bf16[512,1024]{1,0:T(8,128)(2,1)S(1)}, u32[]{:S(2)}) copy-start(bf16[512,1024]{1,0:T(8,128)(2,1)S(1)} %reshape.119.rest) | copy-start | bytes 3145732
  173.3 21.3 %all-to-all-start.1 = ((bf16[16,32,1024]{2,1,0:T(8,128)(2,1)}), bf16[16,32,1024]{2,1,0:T(8,128)(2,1)S(1)}, u32[]{:S(2)}, u32[]{:S(2)}) async-start(bf16[16,32,1024]{2,1,0:T(8,128)(2,1)} %bitcast.46), calls=%async_computation.1 | async-start | bytes 2097152 | tf_op jit(solution)/shard_map/all_to_all | solution.py:511
  233.2 18.2 %copy-start = (bf16[1,1024,896]{2,1,0:T(8,128)(2,1)S(1)}, bf16[1,1024,896]{2,1,0:T(8,128)(2,1)}, u32[]{:S(2)}) copy-start(bf16[1,1024,896]{2,1,0:T(8,128)(2,1)} %w_out.1) | copy-start | bytes 5505028
  253.8 25.0 %all-to-all-start.4 = ((bf16[128,4,896]{2,1,0:T(4,128)(2,1)}), bf16[128,4,896]{2,1,0:T(4,128)(2,1)S(1)}, u32[]{:S(2)}, u32[]{:S(2)}) async-start(bf16[128,4,896]{2,1,0:T(4,128)(2,1)} %reshape.121), calls=%async_computation.4 | async-start | bytes 1835008 | tf_op jit(solution)/shard_map/all_to_all | solution.py:517
Sparse Core Ops, SparseCore 0:
  9.1 40.6 all-gather.1

commit v3 on v2

--- a/solution.py
+++ b/solution.py
@@ -15,6 +15,7 @@
 RLEN, ENTRY, LAT, PLEN, HEADS, VHEAD = 32, 576, 512, 128, 8, 128
 DIM, SLICE, HALF, FF, HID = 7168, 896, 448, 1024, 128
 GROUP, BLOCK, CAP = 512, 64, 4
+BATCH = 4
 TILES = 2 * FF // 128 + 1
 WEIGHTS = SLICE + 4 * BLOCK
 ALONG_Y = [[y * NH + h for y in range(NY)] for h in range(NH)]
@@ -112,15 +113,15 @@
 
     @pl.when(step == 0)
     def _():
-        even[:, PLEN:, ENTRY:] = jnp.zeros((2, RLEN, 640 - ENTRY), BF)
-        odd[:, :, :64] = jnp.zeros((2, total, 64), BF)
+        even[:, PLEN:, ENTRY:] = jnp.zeros((BATCH, RLEN, 640 - ENTRY), BF)
+        odd[:, :, :64] = jnp.zeros((BATCH, total, 64), BF)
         column = lax.broadcasted_iota(jnp.int32, (rows, total), 1)
         token = lax.broadcasted_iota(jnp.int32, (rows, total), 0) % RLEN
         seen = (column < PLEN) | (column <= token + PLEN)
         bias[...] = jnp.where(seen, 0.0, NEGATIVE)
 
-    for part in range(2):
-        resp = 2 * step + part
+    for part in range(BATCH):
+        resp = BATCH * step + part
         even[part, :PLEN, :] = keys[part]
         even[part, PLEN:, :ENTRY] = own[part]
         odd[part, :PLEN, 64:] = keys[part, :, :ENTRY]
@@ -158,18 +159,18 @@
     count = queries.shape[0]
     spec = pltpu.PrefetchScalarGridSpec(
         num_scalar_prefetch=1,
-        grid=(count // 2,),
+        grid=(count // BATCH,),
         in_specs=[
-            pl.BlockSpec((2, RLEN, HEADS * ENTRY), lambda i, n: (i, 0, 0)),
-            pl.BlockSpec((2, PLEN, 640), lambda i, n: (i, 0, 0)),
-            pl.BlockSpec((2, RLEN, ENTRY), lambda i, n: (i, 0, 0)),
+            pl.BlockSpec((BATCH, RLEN, HEADS * ENTRY), lambda i, n: (i, 0, 0)),
+            pl.BlockSpec((BATCH, PLEN, 640), lambda i, n: (i, 0, 0)),
+            pl.BlockSpec((BATCH, RLEN, ENTRY), lambda i, n: (i, 0, 0)),
             pl.BlockSpec((HEADS, LAT, VHEAD), lambda i, n: (0, 0, 0)),
         ],
         out_specs=pl.BlockSpec((GROUP, HEADS * VHEAD), lambda i, n: (0, 0)),
         scratch_shapes=[
             pltpu.VMEM((HEADS, GROUP, LAT), BF),
-            pltpu.VMEM((2, PLEN + RLEN, 640), BF),
-            pltpu.VMEM((2, PLEN + RLEN, 640), BF),
+            pltpu.VMEM((BATCH, PLEN + RLEN, 640), BF),
+            pltpu.VMEM((BATCH, PLEN + RLEN, 640), BF),
             pltpu.VMEM((HEADS * RLEN, PLEN + RLEN), F32),
         ],
     )
@@ -492,17 +493,20 @@
 
     match = jnp.where(h == x, 0, 1).reshape(1).astype(jnp.int32)
     pick = [((z - y - dy + 2 * NY) % NY).astype(jnp.int32) for dy in range(NY)]
+    order = jnp.stack([pick[1], pick[3], pick[0]])
+    match, order = after(match, order)
     top, bottom = project(match, jnp.stack(pick[2:3]), heads, first_w + second_w, True)
     from_left = over_exp(top, 1, 0)
     from_right = over_exp(bottom, 3, 0)
-    order = jnp.stack([pick[1], pick[3], pick[0]])
     pieces = project(match, order, heads, first_w + second_w)
-    near1, far1, near3, far3 = merge(pieces[:4], from_left, from_right)
+    far0 = other_core(pieces[5], 0)
+    merged, far0 = after(merge(pieces[:4], from_left, from_right), far0)
+    near1, far1, near3, far3 = merged
     parts = [
         pieces[4],
         over_exp(near1, 1, 0),
         over_exp(near3, 3, 0),
-        other_core(pieces[5], 0),
+        far0,
         other_core(far1, 1),
         other_core(far3, 3),
     ]

time: 289 us -> 288 us (level)
    ppermute x4, waiting for transfers between devices: 6.28 us -> 9.96 us  [over_all(): return lax.ppermute(x, ('resp', 'exp'), everywhere(move))]
    ppermute x4, starting transfers between devices: 16.6 us -> 13.7 us  [over_all(): return lax.ppermute(x, ('resp', 'exp'), everywhere(move))]
  transfers between devices with their start and end apart: 25 -> 25, of which waited for: 9 -> 10; matrix products, arithmetic and copies ran while one was open for 9% -> 9% of each run, Pallas kernels for 12% -> 12%
where the time goes in v3:
time: 288 us; the launch traced here: 287 us
  waiting for transfers between devices  82.4 us (29%)
  starting transfers between devices  60.8 us (21%)
  blocking collectives  52.2 us (18%)
  Pallas kernels  46.7 us (16%)
  local copies, waits for them, and re-layouts  22.8 us (8%)
  between operations  13.7 us (5%)
  other arithmetic  7.9 us (3%)
    all_to_all x1, blocking collectives, body(): lax.all_to_all(message, 'exp', split_axis=0, concat_axis=0, tiled=True)  34.6 us
    ppermute x11, starting transfers between devices, over_resp(): return lax.ppermute(x, 'resp', resp_perm(dz, dx, dc))  21 us
    all_to_all x1, waiting for transfers between devices, body(): lax.all_to_all(finished.reshape(128, CAP, SLICE), ('resp', 'exp'), split_...  18.2 us
    all_to_all x1, blocking collectives, body(): act = lax.all_to_all(act, 'exp', split_axis=0, concat_axis=0, tiled=True)  17.6 us
    pallas_call x2, Pallas kernels, project(): pl.pallas_call(functools.partial(project_kernel, count, by_rows), in_spec...  17.5 us
    ppermute x11, waiting for transfers between devices, over_resp(): return lax.ppermute(x, 'resp', resp_perm(dz, dx, dc))  16.7 us
    all_to_all x1, waiting for transfers between devices, body(): lax.all_to_all(sorted_rows, 'resp', split_axis=0, concat_axis=0, tiled=True)  15.1 us
    pallas_call x1, Pallas kernels, attention(): pl.pallas_call(attention_kernel, grid_spec=spec, out_shape=jax.ShapeDtype...  14.2 us
  transfers between devices with their start and end apart: 25, of which 10 were waited for; matrix products, arithmetic and copies ran while one was open for 9% of the time, Pallas kernels for 12%

profile of v3, /device:TPU:1, one launch (start us, length us, event | category | flops | bytes accessed | tf_op | source)
XLA Modules:
  0.0 286.6 jit_solution(2470507710910917917)
XLA Ops:
  6.5 1.1 copy.40
  7.6 0.7 pad.8
  8.3 8.5 %collective-permute-start = (bf16[448,1024]{1,0:T(8,128)(2,1)}, bf16[448,1024]{1,0:T(8,128)(2,1)}, u32[]{:S(2)}, u32[]{:S(2)}) collective-permute-start(bf16[448,1024]{1,0:T(8,128)(2,1)} %bitcast.51), channel_id=1, source_target_pairs={{0,0},{1,16},{2,2},{3,18},{4,4},{5,20},{6,6},{7,22},{8,8},{9,24},{... | collective-permute-start | bytes 2752520 | tf_op jit(solution)/shard_map/ppermute | solution.py:72
  16.9 3.5 %fusion.2 = (bf16[1,1,7168,128]{3,2,1,0:T(8,128)(2,1)S(1)}, bf16[1,1,7168,128]{3,2,1,0:T(8,128)(2,1)}) fusion(bf16[1,2,7168,128]{3,2,1,0:T(8,128)(2,1)} %param.20), kind=kLoop, calls=%fused_computation.22 | loop fusion | bytes 7340032 | tf_op jit(solution)/shard_map/slice | solution.py:452
  20.4 0.2 convert_reduce_fusion.2
  20.8 0.1 copy.48
  20.9 1.1 pad_maximum_fusion.1
  22.0 1.7 reshape.117
  23.7 3.6 %pad_maximum_fusion = bf16[8,1152,256]{2,1,0:T(8,128)(2,1)} fusion(bf16[8,256,256]{2,1,0:T(8,128)(2,1)S(1)} %reshape.117, bf16[8,896,128]{2,1,0:T(8,128)(2,1)} %bitcast.45, bf16[8,896,128]{2,1,0:T(8,128)(2,1)S(1)} %bitcast.44), kind=kLoop, calls=%fused_computation | loop fusion | flops 14155776 | bytes 9437184 | tf_op jit(solution)/shard_map/concatenate | solution.py:462
  27.4 5.1 %all-to-all-start = ((bf16[8,1152,256]{2,1,0:T(8,128)(2,1)}), bf16[8,1152,256]{2,1,0:T(8,128)(2,1)}, u32[]{:S(2)}, u32[]{:S(2)}) async-start(bf16[8,1152,256]{2,1,0:T(8,128)(2,1)} %pad_maximum_fusion), calls=%async_computation | async-start | bytes 9437184 | tf_op jit(solution)/shard_map/all_to_all | solution.py:464
  32.4 2.5 collective-permute-start.1
  34.9 2.2 collective-permute-start.2
  37.1 5.7 %collective-permute-start.3 = (bf16[448,1024]{1,0:T(8,128)(2,1)}, bf16[448,1024]{1,0:T(8,128)(2,1)}, u32[]{:S(2)}, u32[]{:S(2)}) collective-permute-start(bf16[448,1024]{1,0:T(8,128)(2,1)} %collective-permute-done.refs_4_), channel_id=1, source_target_pairs={{0,16},{8,24},{16,0},{24,8},{32,48},{40,56},{48,32},{56,40},{64,80... | collective-permute-start | bytes 2752520 | tf_op jit(solution)/shard_map/ppermute | solution.py:50
  42.9 6.9 %all-gather.2.cloned.1.call-done.keys = bf16[16,128,640]{2,1,0:T(8,128)(2,1)} async-done(((bf16[1,128,640]{2,1,0:T(8,128)(2,1)}), bf16[16,128,640]{2,1,0:T(8,128)(2,1)}) %all-gather.2.cloned.1.call-update) | async-done | bytes 2621456 | tf_op jit(solution)/shard_map/all_gather | solution.py:443
  49.7 14.2 %attention.1.refs_0_ = bf16[512,1024]{1,0:T(8,128)(2,1)} custom-call(s32[16]{0:T(128)} %lens.1, bf16[16,32,4608]{2,1,0:T(8,128)(2,1)} %q_ref.1, bf16[16,128,640]{2,1,0:T(8,128)(2,1)} %all-gather.2.cloned.1.call-done.keys, bf16[16,32,576]{2,1,0:T(8,128)(2,1)} %own.1, bf16[8,512,128]{2,1,0:T(8,128)(2,1)} %w_uv.1), custom_call_target="tpu_custom_call" | custom-call | tf_op jit(solution)/shard_map/attention/pallas_call | solution.py:177
  64.0 3.2 %collective-permute-start.5 = (bf16[512,1024]{1,0:T(8,128)(2,1)}, bf16[512,1024]{1,0:T(8,128)(2,1)}, u32[]{:S(2)}, u32[]{:S(2)}) collective-permute-start(bf16[512,1024]{1,0:T(8,128)(2,1)} %attention.1.refs_0_), channel_id=1, source_target_pairs={{0,1},{1,0},{2,3},{3,2},{4,5},{5,4},{6,7},{7,6},{8,9},{9,8},{10,11... | collective-permute-start | bytes 3145736 | tf_op jit(solution)/shard_map/ppermute | solution.py:54
  67.3 2.6 collective-permute-start.7
  69.9 0.8 slice.36
  70.7 0.8 slice.37
  71.6 2.7 collective-permute-start.9
  74.2 13.0 %all-to-all-done = bf16[8,1152,256]{2,1,0:T(8,128)(2,1)} async-done(((bf16[8,1152,256]{2,1,0:T(8,128)(2,1)}), bf16[8,1152,256]{2,1,0:T(8,128)(2,1)}, u32[]{:S(2)}, u32[]{:S(2)}) %all-to-all-start) | async-done | bytes 4718624 | tf_op jit(solution)/shard_map/all_to_all | solution.py:464
  87.2 4.2 %dynamic-slice_bitcast_fusion.1 = (bf16[4,1152,256]{2,1,0:T(8,128)(2,1)S(1)}, bf16[4,1152,256]{2,1,0:T(8,128)(2,1)}) fusion(bf16[4,2,1152,256]{3,2,1,0:T(8,128)(2,1)} %bitcast.11, s32[]{:T(128)S(6)} %select_n.79, s32[]{:T(128)S(6)} %select_n.80), kind=kLoop, calls=%fused_computation.2 | loop fusion | bytes 9437192 | tf_op jit(solution)/shard_map/jit(dynamic_index_in_dim)/squeeze | solution.py:469
  91.4 7.6 %collective-permute-done.8.refs_6_ = bf16[224,1024]{1,0:T(8,128)(2,1)} collective-permute-done((bf16[224,1024]{1,0:T(8,128)(2,1)}, bf16[224,1024]{1,0:T(8,128)(2,1)}, u32[]{:S(2)}, u32[]{:S(2)}) %collective-permute-start.8) | collective-permute-done | bytes 458784 | tf_op jit(solution)/shard_map/ppermute | solution.py:50
  99.1 0.2 collective-permute-start.20
  99.3 2.5 collective-permute-start.4
  101.8 1.9 slice.38
  103.7 0.7 collective-permute-start.11
  104.4 1.8 slice.39
  106.2 2.0 collective-permute-start.12
  108.2 0.6 pad_add_fusion.picks
  108.8 8.0 %collective-permute-done.11.refs_11_ = bf16[224,1024]{1,0:T(8,128)(2,1)} collective-permute-done((bf16[224,1024]{1,0:T(8,128)(2,1)}, bf16[224,1024]{1,0:T(8,128)(2,1)}, u32[]{:S(2)}, u32[]{:S(2)}) %collective-permute-start.11) | collective-permute-done | bytes 458784 | tf_op jit(solution)/shard_map/ppermute | solution.py:50
  116.8 1.0 collective-permute-done.12.refs_12_
  117.8 5.8 %project.3 = (bf16[224,1024]{1,0:T(8,128)(2,1)}, bf16[224,1024]{1,0:T(8,128)(2,1)}) custom-call(s32[1]{0:T(128)} %bitcast.2.match, s32[1]{0:T(128)} %bitcast.7.picks, bf16[512,1024]{1,0:T(8,128)(2,1)} %attention.1.refs_0_, bf16[512,1024]{1,0:T(8,128)(2,1)} %collective-permute-done.4.refs_1_, bf16[512,1024]{1,0:T(8,128)(2,1)} %collective-permute-done.5.refs_2_, ...), custom_call_target="tpu_custom_call" | custom-call | tf_op jit(solution)/shard_map/project/pallas_call | solution.py:250
  123.6 1.3 collective-permute-start.13
  124.8 1.5 collective-permute-start.14
  126.4 11.7 %project.2 = (bf16[448,512]{1,0:T(8,128)(2,1)}, bf16[448,512]{1,0:T(8,128)(2,1)}, bf16[448,512]{1,0:T(8,128)(2,1)}, bf16[448,512]{1,0:T(8,128)(2,1)}, bf16[448,5...) custom-call(s32[1]{0:T(128)} %bitcast.2.match, s32[3]{0:T(128)} %pad_add_fusion.picks, bf16[512,1024]{1,0:T(8,128)(2,1)} %attention.1.refs_0_, ...), custom_call_target="tpu_custom_call" | custom-call | tf_op jit(solution)/shard_map/project/pallas_call | solution.py:250
  138.1 2.3 collective-permute-start.15
  140.5 0.7 copy-done.7
  141.3 3.0 %merge.1 = (bf16[448,512]{1,0:T(8,128)(2,1)}, bf16[448,512]{1,0:T(8,128)(2,1)}, bf16[448,512]{1,0:T(8,128)(2,1)}, bf16[448,512]{1,0:T(8,128)(2,1)}) custom-call(bf16[448,512]{1,0:T(8,128)(2,1)} %get-tuple-element.33.ahead0, bf16[448,512]{1,0:T(8,128)(2,1)} %get-tuple-element.34.ahead1, bf16[448,512]{1,0:T(8,128)(2,1)} %get-tuple-element.35.behind0, ...), custom_call_target="tpu_custom_call" | custom-call | tf_op jit(solution)/shard_map/merge/pallas_call | solution.py:280
  144.4 2.7 collective-permute-start.17
  147.0 3.0 %collective-permute-start.19 = (bf16[448,512]{1,0:T(8,128)(2,1)}, bf16[448,512]{1,0:T(8,128)(2,1)}, u32[]{:S(2)}, u32[]{:S(2)}) collective-permute-start(bf16[448,512]{1,0:T(8,128)(2,1)} %get-tuple-element.48), channel_id=1, source_target_pairs={{0,14},{1,15},{2,8},{3,9},{4,10},{5,11},{6,12},{7,13},{8,6},{9,7},... | collective-permute-start | bytes 1376264 | tf_op jit(solution)/shard_map/ppermute | solution.py:72
  150.0 1.4 collective-permute-done.20.come
  151.4 1.1 select_bitcast_fusion.1
  152.7 1.0 copy.43
  153.7 1.7 reshape.119.rest
  155.4 0.2 fusion
  155.7 0.3 convert_reduce_fusion.1
  156.1 0.6 add_add_fusion.place
  156.7 1.3 collective-permute-done.16.near1
  158.0 10.0 %collective-permute-done.18.far1 = bf16[448,512]{1,0:T(8,128)(2,1)} collective-permute-done((bf16[448,512]{1,0:T(8,128)(2,1)}, bf16[448,512]{1,0:T(8,128)(2,1)}, u32[]{:S(2)}, u32[]{:S(2)}) %collective-permute-start.18) | collective-permute-done | bytes 458784 | tf_op jit(solution)/shard_map/ppermute | solution.py:72
  167.9 4.4 %dispatch.1 = bf16[512,1024]{1,0:T(8,128)(2,1)} custom-call(s32[1]{0:T(128)} %bitcast.1.core, bf16[448,512]{1,0:T(8,128)(2,1)} %get-tuple-element.32.near0, bf16[448,512]{1,0:T(8,128)(2,1)} %collective-permute-done.16.near1, bf16[448,512]{1,0:T(8,128)(2,1)} %collective-permute-done.17.near3, bf16[448,512]{1,0:T(8,128)(2,1)} %copy-done.6, ...), custom_call_target="tpu_custom_call" | custom-call | tf_op jit(solution)/shard_map/dispatch/pallas_call | solution.py:305
  172.3 5.3 %all-to-all-start.1 = ((bf16[16,32,1024]{2,1,0:T(8,128)(2,1)}), bf16[16,32,1024]{2,1,0:T(8,128)(2,1)S(1)}, u32[]{:S(2)}, u32[]{:S(2)}) async-start(bf16[16,32,1024]{2,1,0:T(8,128)(2,1)} %bitcast.46), calls=%async_computation.1 | async-start | bytes 2097152 | tf_op jit(solution)/shard_map/all_to_all | solution.py:515
  177.6 0.8 dynamic_slice.12
  178.4 15.1 %all-to-all-done.1 = bf16[16,32,1024]{2,1,0:T(8,128)(2,1)S(1)} async-done(((bf16[16,32,1024]{2,1,0:T(8,128)(2,1)}), bf16[16,32,1024]{2,1,0:T(8,128)(2,1)S(1)}, u32[]{:S(2)}, u32[]{:S(2)}) %all-to-all-start.1) | async-done | bytes 1048608 | tf_op jit(solution)/shard_map/all_to_all | solution.py:515
  193.5 4.1 %enter.1 = bf16[8704,128]{1,0:T(8,128)(2,1)S(1)} custom-call(s32[1]{0:T(128)} %bitcast.half, bf16[512,1024]{1,0:T(8,128)(2,1)S(1)} %bitcast.38, f32[1,896]{1,0:T(1,128)S(1)} %reshape.120.gain, bf16[4,1152,256]{2,1,0:T(8,128)(2,1)S(1)} %get-tuple-element.55.kept, bf16[4,1152,256]{2,1,0:T(8,128)(2,1)} %collective-permute-done.20.come), custom_call_target="tpu_custom_call" | custom-call | tf_op jit(solution)/shard_map/enter/pallas_call | solution.py:339
  197.6 34.6 %all_to_all.43 = bf16[8,1088,128]{2,1,0:T(8,128)(2,1)S(1)} all-to-all(bf16[8,1088,128]{2,1,0:T(8,128)(2,1)S(1)} %bitcast.40), channel_id=1, replica_groups=mesh['resp'=16,'exp'=8] {'exp'}, dimensions={0} | all-to-all | bytes 4456448 | tf_op jit(solution)/shard_map/all_to_all | solution.py:517
  232.2 0.6 activate.1
  232.8 17.6 %all_to_all.44 = bf16[8,64,1024]{2,1,0:T(8,128)(2,1)S(1)} all-to-all(bf16[8,64,1024]{2,1,0:T(8,128)(2,1)S(1)} %bitcast.43), channel_id=1, replica_groups=mesh['resp'=16,'exp'=8] {'exp'}, dimensions={0} | all-to-all | bytes 2097152 | tf_op jit(solution)/shard_map/all_to_all | solution.py:519
  250.4 1.3 leave.1
  251.7 1.1 reshape.121
  252.8 6.7 %all-to-all-start.4 = ((bf16[128,4,896]{2,1,0:T(4,128)(2,1)}), bf16[128,4,896]{2,1,0:T(4,128)(2,1)S(1)}, u32[]{:S(2)}, u32[]{:S(2)}) async-start(bf16[128,4,896]{2,1,0:T(4,128)(2,1)} %reshape.121), calls=%async_computation.4 | async-start | bytes 1835008 | tf_op jit(solution)/shard_map/all_to_all | solution.py:521
  259.6 18.2 %all-to-all-done.4 = bf16[128,4,896]{2,1,0:T(4,128)(2,1)S(1)} async-done(((bf16[128,4,896]{2,1,0:T(4,128)(2,1)}), bf16[128,4,896]{2,1,0:T(4,128)(2,1)S(1)}, u32[]{:S(2)}, u32[]{:S(2)}) %all-to-all-start.4) | async-done | bytes 917536 | tf_op jit(solution)/shard_map/all_to_all | solution.py:521
  277.8 0.2 reshape.122.rows
  278.0 1.7 restore.1
  (56 shorter events, 0.9 us)
Async XLA Ops:
  6.5 43.2 %all-gather.2.cloned.1.call-start = ((), (), s32[]{:S(2)}) async-start(), calls=%async_computation.5 | async-start | bytes 2785280 | tf_op jit(solution)/shard_map/all_gather | solution.py:443
  8.3 12.1 %copy-start.9 = (s32[64,1]{0,1:T(1,128)S(1)}, s32[64,1]{0,1:T(1,128)}, u32[]{:S(2)}) copy-start(s32[64,1]{0,1:T(1,128)} %param.22) | copy-start | bytes 772
  8.3 12.2 %copy-start.8 = (f32[64,1]{0,1:T(1,128)S(1)}, f32[64,1]{0,1:T(1,128)}, u32[]{:S(2)}) copy-start(f32[64,1]{0,1:T(1,128)} %param.23) | copy-start | bytes 772
  8.3 12.4 %copy-start.5 = (bf16[64,7168]{1,0:T(8,128)(2,1)S(1)}, bf16[64,7168]{1,0:T(8,128)(2,1)}, u32[]{:S(2)}) copy-start(bf16[64,7168]{1,0:T(8,128)(2,1)} %param.18) | copy-start | bytes 2752516
  8.3 19.0 %collective-permute-start = (bf16[448,1024]{1,0:T(8,128)(2,1)}, bf16[448,1024]{1,0:T(8,128)(2,1)}, u32[]{:S(2)}, u32[]{:S(2)}) collective-permute-start(bf16[448,1024]{1,0:T(8,128)(2,1)} %bitcast.51), channel_id=1, source_target_pairs={{0,0},{1,16},{2,2},{3,18},{4,4},{5,20},{6,6},{7,22},{8,8},{9,24},{... | collective-permute-start | bytes 2752520 | tf_op jit(solution)/shard_map/ppermute | solution.py:72
  27.4 59.8 %all-to-all-start = ((bf16[8,1152,256]{2,1,0:T(8,128)(2,1)}), bf16[8,1152,256]{2,1,0:T(8,128)(2,1)}, u32[]{:S(2)}, u32[]{:S(2)}) async-start(bf16[8,1152,256]{2,1,0:T(8,128)(2,1)} %pad_maximum_fusion), calls=%async_computation | async-start | bytes 9437184 | tf_op jit(solution)/shard_map/all_to_all | solution.py:464
  32.4 31.5 %collective-permute-start.1 = (bf16[448,1024]{1,0:T(8,128)(2,1)}, bf16[448,1024]{1,0:T(8,128)(2,1)S(1)}, u32[]{:S(2)}, u32[]{:S(2)}) collective-permute-start(bf16[448,1024]{1,0:T(8,128)(2,1)} %collective-permute-done.refs_4_), channel_id=1, source_target_pairs={{0,32},{8,40},{16,48},{24,56},{32,64},{40,72},{48,80},{56,88},{64,... | collective-permute-start | bytes 2752520 | tf_op jit(solution)/shard_map/ppermute | solution.py:50
  34.9 29.1 %collective-permute-start.2 = (bf16[448,1024]{1,0:T(8,128)(2,1)}, bf16[448,1024]{1,0:T(8,128)(2,1)S(1)}, u32[]{:S(2)}, u32[]{:S(2)}) collective-permute-start(bf16[448,1024]{1,0:T(8,128)(2,1)} %collective-permute-done.refs_4_), channel_id=1, source_target_pairs={{0,96},{8,104},{16,112},{24,120},{32,0},{40,8},{48,16},{56,24},{64... | collective-permute-start | bytes 2752520 | tf_op jit(solution)/shard_map/ppermute | solution.py:50
  37.1 26.9 %collective-permute-start.3 = (bf16[448,1024]{1,0:T(8,128)(2,1)}, bf16[448,1024]{1,0:T(8,128)(2,1)}, u32[]{:S(2)}, u32[]{:S(2)}) collective-permute-start(bf16[448,1024]{1,0:T(8,128)(2,1)} %collective-permute-done.refs_4_), channel_id=1, source_target_pairs={{0,16},{8,24},{16,0},{24,8},{32,48},{40,56},{48,32},{56,40},{64,80... | collective-permute-start | bytes 2752520 | tf_op jit(solution)/shard_map/ppermute | solution.py:50
  64.0 23.2 %copy-start.2 = (bf16[448,1024]{1,0:T(8,128)(2,1)}, bf16[448,1024]{1,0:T(8,128)(2,1)S(1)}, u32[]{:S(2)}) copy-start(bf16[448,1024]{1,0:T(8,128)(2,1)S(1)} %collective-permute-done.1.refs_5_) | copy-start | bytes 2752516
  64.0 23.2 %copy-start.3 = (bf16[448,1024]{1,0:T(8,128)(2,1)}, bf16[448,1024]{1,0:T(8,128)(2,1)S(1)}, u32[]{:S(2)}) copy-start(bf16[448,1024]{1,0:T(8,128)(2,1)S(1)} %collective-permute-done.2.refs_8_) | copy-start | bytes 2752516
  64.0 35.1 %collective-permute-start.5 = (bf16[512,1024]{1,0:T(8,128)(2,1)}, bf16[512,1024]{1,0:T(8,128)(2,1)}, u32[]{:S(2)}, u32[]{:S(2)}) collective-permute-start(bf16[512,1024]{1,0:T(8,128)(2,1)} %attention.1.refs_0_), channel_id=1, source_target_pairs={{0,1},{1,0},{2,3},{3,2},{4,5},{5,4},{6,7},{7,6},{8,9},{9,8},{10,11... | collective-permute-start | bytes 3145736 | tf_op jit(solution)/shard_map/ppermute | solution.py:54
  67.2 31.8 %collective-permute-start.6 = (bf16[448,1024]{1,0:T(8,128)(2,1)}, bf16[448,1024]{1,0:T(8,128)(2,1)}, u32[]{:S(2)}, u32[]{:S(2)}) collective-permute-start(bf16[448,1024]{1,0:T(8,128)(2,1)} %collective-permute-done.3.refs_9_), channel_id=1, source_target_pairs={{0,32},{8,40},{16,48},{24,56},{32,64},{40,72},{48,80},{56,88},{64,... | collective-permute-start | bytes 2752520 | tf_op jit(solution)/shard_map/ppermute | solution.py:50
  67.3 31.8 %collective-permute-start.7 = (bf16[448,1024]{1,0:T(8,128)(2,1)}, bf16[448,1024]{1,0:T(8,128)(2,1)}, u32[]{:S(2)}, u32[]{:S(2)}) collective-permute-start(bf16[448,1024]{1,0:T(8,128)(2,1)} %collective-permute-done.3.refs_9_), channel_id=1, source_target_pairs={{0,96},{8,104},{16,112},{24,120},{32,0},{40,8},{48,16},{56,24},{64... | collective-permute-start | bytes 2752520 | tf_op jit(solution)/shard_map/ppermute | solution.py:50
  70.7 28.3 %collective-permute-start.8 = (bf16[224,1024]{1,0:T(8,128)(2,1)}, bf16[224,1024]{1,0:T(8,128)(2,1)}, u32[]{:S(2)}, u32[]{:S(2)}) collective-permute-start(bf16[224,1024]{1,0:T(8,128)(2,1)} %slice.36), channel_id=1, source_target_pairs={{0,32},{8,40},{16,48},{24,56},{32,64},{40,72},{48,80},{56,88},{64,... | collective-permute-start | bytes 1376264 | tf_op jit(solution)/shard_map/ppermute | solution.py:50
  71.6 27.5 %collective-permute-start.9 = (bf16[224,1024]{1,0:T(8,128)(2,1)}, bf16[224,1024]{1,0:T(8,128)(2,1)}, u32[]{:S(2)}, u32[]{:S(2)}) collective-permute-start(bf16[224,1024]{1,0:T(8,128)(2,1)} %slice.37), channel_id=1, source_target_pairs={{0,96},{8,104},{16,112},{24,120},{32,0},{40,8},{48,16},{56,24},{64... | collective-permute-start | bytes 1376264 | tf_op jit(solution)/shard_map/ppermute | solution.py:50
  87.2 12.1 %copy-start.1 = (bf16[512,1024]{1,0:T(8,128)(2,1)S(1)}, bf16[512,1024]{1,0:T(8,128)(2,1)}, u32[]{:S(2)}) copy-start(bf16[512,1024]{1,0:T(8,128)(2,1)} %attention.1.refs_0_) | copy-start | bytes 3145732
  99.1 52.4 %collective-permute-start.20 = (bf16[4,1152,256]{2,1,0:T(8,128)(2,1)}, bf16[4,1152,256]{2,1,0:T(8,128)(2,1)}, u32[]{:S(2)}, u32[]{:S(2)}) collective-permute-start(bf16[4,1152,256]{2,1,0:T(8,128)(2,1)} %get-tuple-element.50), channel_id=1, source_target_pairs={{0,1},{1,0},{2,3},{3,2},{4,5},{5,4},{6,7},{7,6},{8,9},{9,8},{10,11... | collective-permute-start | bytes 7077896 | tf_op jit(solution)/shard_map/ppermute | solution.py:54
  99.3 18.5 %collective-permute-start.4 = (bf16[512,1024]{1,0:T(8,128)(2,1)S(1)}, bf16[512,1024]{1,0:T(8,128)(2,1)}, u32[]{:S(2)}, u32[]{:S(2)}) collective-permute-start(bf16[512,1024]{1,0:T(8,128)(2,1)S(1)} %copy-done.1), channel_id=1, source_target_pairs={{0,8},{8,0},{16,24},{24,16},{32,40},{40,32},{48,56},{56,48},{64,72... | collective-permute-start | bytes 3145736 | tf_op jit(solution)/shard_map/ppermute | solution.py:50
  101.8 16.0 %collective-permute-start.10 = (bf16[512,1024]{1,0:T(8,128)(2,1)}, bf16[512,1024]{1,0:T(8,128)(2,1)}, u32[]{:S(2)}, u32[]{:S(2)}) collective-permute-start(bf16[512,1024]{1,0:T(8,128)(2,1)} %collective-permute-done.5.refs_2_), channel_id=1, source_target_pairs={{0,8},{8,0},{16,24},{24,16},{32,40},{40,32},{48,56},{56,48},{64,72... | collective-permute-start | bytes 3145736 | tf_op jit(solution)/shard_map/ppermute | solution.py:50
  103.7 13.1 %collective-permute-start.11 = (bf16[224,1024]{1,0:T(8,128)(2,1)}, bf16[224,1024]{1,0:T(8,128)(2,1)}, u32[]{:S(2)}, u32[]{:S(2)}) collective-permute-start(bf16[224,1024]{1,0:T(8,128)(2,1)} %slice.38), channel_id=1, source_target_pairs={{0,32},{8,40},{16,48},{24,56},{32,64},{40,72},{48,80},{56,88},{64,... | collective-permute-start | bytes 1376264 | tf_op jit(solution)/shard_map/ppermute | solution.py:50
  106.2 11.6 %collective-permute-start.12 = (bf16[224,1024]{1,0:T(8,128)(2,1)}, bf16[224,1024]{1,0:T(8,128)(2,1)}, u32[]{:S(2)}, u32[]{:S(2)}) collective-permute-start(bf16[224,1024]{1,0:T(8,128)(2,1)} %slice.39), channel_id=1, source_target_pairs={{0,96},{8,104},{16,112},{24,120},{32,0},{40,8},{48,16},{56,24},{64... | collective-permute-start | bytes 1376264 | tf_op jit(solution)/shard_map/ppermute | solution.py:50
  123.6 16.9 %collective-permute-start.13 = (bf16[224,1024]{1,0:T(8,128)(2,1)}, bf16[224,1024]{1,0:T(8,128)(2,1)S(1)}, u32[]{:S(2)}, u32[]{:S(2)}) collective-permute-start(bf16[224,1024]{1,0:T(8,128)(2,1)} %get-tuple-element.37), channel_id=1, source_target_pairs={{0,2},{1,3},{2,4},{3,5},{4,6},{5,7},{6,0},{7,1},{8,10},{9,11},{10,... | collective-permute-start | bytes 1376264 | tf_op jit(solution)/shard_map/ppermute | solution.py:54
  124.8 15.7 %collective-permute-start.14 = (bf16[224,1024]{1,0:T(8,128)(2,1)}, bf16[224,1024]{1,0:T(8,128)(2,1)}, u32[]{:S(2)}, u32[]{:S(2)}) collective-permute-start(bf16[224,1024]{1,0:T(8,128)(2,1)} %get-tuple-element.38), channel_id=1, source_target_pairs={{0,6},{1,7},{2,0},{3,1},{4,2},{5,3},{6,4},{7,5},{8,14},{9,15},{10,... | collective-permute-start | bytes 1376264 | tf_op jit(solution)/shard_map/ppermute | solution.py:54
  138.1 6.2 %collective-permute-start.15 = (bf16[448,512]{1,0:T(8,128)(2,1)}, bf16[448,512]{1,0:T(8,128)(2,1)S(1)}, u32[]{:S(2)}, u32[]{:S(2)}) collective-permute-start(bf16[448,512]{1,0:T(8,128)(2,1)} %get-tuple-element.43), channel_id=1, source_target_pairs={{0,8},{1,9},{2,10},{3,11},{4,12},{5,13},{6,14},{7,15},{8,0},{9,1},... | collective-permute-start | bytes 1376264 | tf_op jit(solution)/shard_map/ppermute | solution.py:72
  140.5 0.8 copy-start.7
  144.3 8.4 %copy-start.6 = (bf16[448,512]{1,0:T(8,128)(2,1)}, bf16[448,512]{1,0:T(8,128)(2,1)S(1)}, u32[]{:S(2)}) copy-start(bf16[448,512]{1,0:T(8,128)(2,1)S(1)} %collective-permute-done.15.far0) | copy-start | bytes 1376260
  144.3 13.7 %collective-permute-start.16 = (bf16[448,512]{1,0:T(8,128)(2,1)}, bf16[448,512]{1,0:T(8,128)(2,1)}, u32[]{:S(2)}, u32[]{:S(2)}) collective-permute-start(bf16[448,512]{1,0:T(8,128)(2,1)} %get-tuple-element.44), channel_id=1, source_target_pairs={{0,2},{1,3},{2,4},{3,5},{4,6},{5,7},{6,0},{7,1},{8,10},{9,11},{10,... | collective-permute-start | bytes 1376264 | tf_op jit(solution)/shard_map/ppermute | solution.py:54
  144.4 13.6 %collective-permute-start.17 = (bf16[448,512]{1,0:T(8,128)(2,1)}, bf16[448,512]{1,0:T(8,128)(2,1)}, u32[]{:S(2)}, u32[]{:S(2)}) collective-permute-start(bf16[448,512]{1,0:T(8,128)(2,1)} %get-tuple-element.45), channel_id=1, source_target_pairs={{0,6},{1,7},{2,0},{3,1},{4,2},{5,3},{6,4},{7,5},{8,14},{9,15},{10,... | collective-permute-start | bytes 1376264 | tf_op jit(solution)/shard_map/ppermute | solution.py:54
  147.0 20.9 %collective-permute-start.18 = (bf16[448,512]{1,0:T(8,128)(2,1)}, bf16[448,512]{1,0:T(8,128)(2,1)}, u32[]{:S(2)}, u32[]{:S(2)}) collective-permute-start(bf16[448,512]{1,0:T(8,128)(2,1)} %get-tuple-element.47), channel_id=1, source_target_pairs={{0,10},{1,11},{2,12},{3,13},{4,14},{5,15},{6,8},{7,9},{8,2},{9,3},... | collective-permute-start | bytes 1376264 | tf_op jit(solution)/shard_map/ppermute | solution.py:72
  147.0 20.9 %collective-permute-start.19 = (bf16[448,512]{1,0:T(8,128)(2,1)}, bf16[448,512]{1,0:T(8,128)(2,1)}, u32[]{:S(2)}, u32[]{:S(2)}) collective-permute-start(bf16[448,512]{1,0:T(8,128)(2,1)} %get-tuple-element.48), channel_id=1, source_target_pairs={{0,14},{1,15},{2,8},{3,9},{4,10},{5,11},{6,12},{7,13},{8,6},{9,7},... | collective-permute-start | bytes 1376264 | tf_op jit(solution)/shard_map/ppermute | solution.py:72
  155.4 12.6 %copy-start.4 = (bf16[512,1024]{1,0:T(8,128)(2,1)}, bf16[512,1024]{1,0:T(8,128)(2,1)S(1)}, u32[]{:S(2)}) copy-start(bf16[512,1024]{1,0:T(8,128)(2,1)S(1)} %reshape.119.rest) | copy-start | bytes 3145732
  172.3 21.2 %all-to-all-start.1 = ((bf16[16,32,1024]{2,1,0:T(8,128)(2,1)}), bf16[16,32,1024]{2,1,0:T(8,128)(2,1)S(1)}, u32[]{:S(2)}, u32[]{:S(2)}) async-start(bf16[16,32,1024]{2,1,0:T(8,128)(2,1)} %bitcast.46), calls=%async_computation.1 | async-start | bytes 2097152 | tf_op jit(solution)/shard_map/all_to_all | solution.py:515
  232.2 18.2 %copy-start = (bf16[1,1024,896]{2,1,0:T(8,128)(2,1)S(1)}, bf16[1,1024,896]{2,1,0:T(8,128)(2,1)}, u32[]{:S(2)}) copy-start(bf16[1,1024,896]{2,1,0:T(8,128)(2,1)} %w_out.1) | copy-start | bytes 5505028
  252.8 25.0 %all-to-all-start.4 = ((bf16[128,4,896]{2,1,0:T(4,128)(2,1)}), bf16[128,4,896]{2,1,0:T(4,128)(2,1)S(1)}, u32[]{:S(2)}, u32[]{:S(2)}) async-start(bf16[128,4,896]{2,1,0:T(4,128)(2,1)} %reshape.121), calls=%async_computation.4 | async-start | bytes 1835008 | tf_op jit(solution)/shard_map/all_to_all | solution.py:521
Sparse Core Ops, SparseCore 0:
  9.1 40.6 all-gather.1

commit v4 on v3

--- a/solution.py
+++ b/solution.py
@@ -264,24 +264,25 @@
 
 
 def merge_kernel(ahead0, ahead1, behind0, behind1, left, right, *outs):
+    pieces = (ahead0, ahead1, behind0, behind1)
+    for n, (piece, out) in enumerate(zip(pieces, outs)):
+        arrived = left if n < 2 else right
+        lanes = slice((n % 2) * GROUP, (n % 2 + 1) * GROUP)
+        out[...] = (piece[...].astype(F32) + arrived[:, lanes].astype(F32)).astype(BF)
+
+
+def merge(pieces, left, right):
     cut = HALF // 2
-    for core, (ahead, behind) in enumerate(((ahead0, behind0), (ahead1, behind1))):
-        lanes = slice(core * GROUP, (core + 1) * GROUP)
-        first = ahead[:cut, :].astype(F32) + left[:, lanes].astype(F32)
-        last = behind[cut:, :].astype(F32) + right[:, lanes].astype(F32)
-        outs[core][:cut, :] = first.astype(BF)
-        outs[core][cut:, :] = ahead[cut:, :]
-        outs[2 + core][:cut, :] = behind[:cut, :]
-        outs[2 + core][cut:, :] = last.astype(BF)
-
-
-def merge(pieces, left, right):
-    vmem = pl.BlockSpec(memory_space=pltpu.VMEM)
+    upper = pl.BlockSpec((cut, GROUP), lambda i: (0, 0))
+    lower = pl.BlockSpec((cut, GROUP), lambda i: (1, 0))
+    whole = pl.BlockSpec((cut, 2 * GROUP), lambda i: (0, 0))
     return pl.pallas_call(
         merge_kernel,
-        in_specs=[vmem] * 6,
-        out_specs=[vmem] * 4,
+        grid=(1,),
+        in_specs=[upper, upper, lower, lower, whole, whole],
+        out_specs=[upper, upper, lower, lower],
         out_shape=[jax.ShapeDtypeStruct((HALF, GROUP), BF)] * 4,
+        input_output_aliases={0: 0, 1: 1, 2: 2, 3: 3},
         compiler_params=params(56),
         name="merge",
     )(*pieces, left, right)

time: 288 us -> 287 us (level)
  no operation moved by 1% of the time
where the time goes in v4:
time: 287 us; the launch traced here: 286 us
  waiting for transfers between devices  82.4 us (29%)
  starting transfers between devices  60.8 us (21%)
  blocking collectives  52.1 us (18%)
  Pallas kernels  46.3 us (16%)
  local copies, waits for them, and re-layouts  22.9 us (8%)
  between operations  13.7 us (5%)
  other arithmetic  7.91 us (3%)
    all_to_all x1, blocking collectives, body(): lax.all_to_all(message, 'exp', split_axis=0, concat_axis=0, tiled=True)  34.5 us
    ppermute x11, starting transfers between devices, over_resp(): return lax.ppermute(x, 'resp', resp_perm(dz, dx, dc))  20.9 us
    all_to_all x1, waiting for transfers between devices, body(): lax.all_to_all(finished.reshape(128, CAP, SLICE), ('resp', 'exp'), split_...  18.2 us
    all_to_all x1, blocking collectives, body(): act = lax.all_to_all(act, 'exp', split_axis=0, concat_axis=0, tiled=True)  17.6 us
    pallas_call x2, Pallas kernels, project(): pl.pallas_call(functools.partial(project_kernel, count, by_rows), in_spec...  17.5 us
    ppermute x11, waiting for transfers between devices, over_resp(): return lax.ppermute(x, 'resp', resp_perm(dz, dx, dc))  16.7 us
    all_to_all x1, waiting for transfers between devices, body(): lax.all_to_all(sorted_rows, 'resp', split_axis=0, concat_axis=0, tiled=True)  15.1 us
    pallas_call x1, Pallas kernels, attention(): pl.pallas_call(attention_kernel, grid_spec=spec, out_shape=jax.ShapeDtype...  14.2 us
  transfers between devices with their start and end apart: 25, of which 10 were waited for; matrix products, arithmetic and copies ran while one was open for 9% of the time, Pallas kernels for 12%

profile of v4, /device:TPU:1, one launch (start us, length us, event | category | flops | bytes accessed | tf_op | source)
XLA Modules:
  0.0 286.2 jit_solution(6695992781691871263)
XLA Ops:
  6.5 1.1 copy.44
  7.6 0.7 pad.8
  8.3 8.5 %collective-permute-start = (bf16[448,1024]{1,0:T(8,128)(2,1)}, bf16[448,1024]{1,0:T(8,128)(2,1)}, u32[]{:S(2)}, u32[]{:S(2)}) collective-permute-start(bf16[448,1024]{1,0:T(8,128)(2,1)} %bitcast.51), channel_id=1, source_target_pairs={{0,0},{1,16},{2,2},{3,18},{4,4},{5,20},{6,6},{7,22},{8,8},{9,24},{... | collective-permute-start | bytes 2752520 | tf_op jit(solution)/shard_map/ppermute | solution.py:72
  16.9 3.5 %fusion.2 = (bf16[1,1,7168,128]{3,2,1,0:T(8,128)(2,1)S(1)}, bf16[1,1,7168,128]{3,2,1,0:T(8,128)(2,1)}) fusion(bf16[1,2,7168,128]{3,2,1,0:T(8,128)(2,1)} %param.20), kind=kLoop, calls=%fused_computation.22 | loop fusion | bytes 7340032 | tf_op jit(solution)/shard_map/slice | solution.py:453
  20.4 0.2 convert_reduce_fusion.2
  20.8 0.1 copy.52
  20.9 1.1 pad_maximum_fusion.1
  22.0 1.7 reshape.117
  23.7 3.6 %pad_maximum_fusion = bf16[8,1152,256]{2,1,0:T(8,128)(2,1)} fusion(bf16[8,256,256]{2,1,0:T(8,128)(2,1)S(1)} %reshape.117, bf16[8,896,128]{2,1,0:T(8,128)(2,1)} %bitcast.45, bf16[8,896,128]{2,1,0:T(8,128)(2,1)S(1)} %bitcast.44), kind=kLoop, calls=%fused_computation | loop fusion | flops 14155776 | bytes 9437184 | tf_op jit(solution)/shard_map/concatenate | solution.py:463
  27.4 5.1 %all-to-all-start = ((bf16[8,1152,256]{2,1,0:T(8,128)(2,1)}), bf16[8,1152,256]{2,1,0:T(8,128)(2,1)}, u32[]{:S(2)}, u32[]{:S(2)}) async-start(bf16[8,1152,256]{2,1,0:T(8,128)(2,1)} %pad_maximum_fusion), calls=%async_computation | async-start | bytes 9437184 | tf_op jit(solution)/shard_map/all_to_all | solution.py:465
  32.4 2.5 collective-permute-start.1
  34.9 2.2 collective-permute-start.2
  37.1 5.7 %collective-permute-start.3 = (bf16[448,1024]{1,0:T(8,128)(2,1)}, bf16[448,1024]{1,0:T(8,128)(2,1)}, u32[]{:S(2)}, u32[]{:S(2)}) collective-permute-start(bf16[448,1024]{1,0:T(8,128)(2,1)} %collective-permute-done.refs_4_), channel_id=1, source_target_pairs={{0,16},{8,24},{16,0},{24,8},{32,48},{40,56},{48,32},{56,40},{64,80... | collective-permute-start | bytes 2752520 | tf_op jit(solution)/shard_map/ppermute | solution.py:50
  42.8 6.9 %all-gather.2.cloned.1.call-done.keys = bf16[16,128,640]{2,1,0:T(8,128)(2,1)} async-done(((bf16[1,128,640]{2,1,0:T(8,128)(2,1)}), bf16[16,128,640]{2,1,0:T(8,128)(2,1)}) %all-gather.2.cloned.1.call-update) | async-done | bytes 2621456 | tf_op jit(solution)/shard_map/all_gather | solution.py:444
  49.7 14.2 %attention.1.refs_0_ = bf16[512,1024]{1,0:T(8,128)(2,1)} custom-call(s32[16]{0:T(128)} %lens.1, bf16[16,32,4608]{2,1,0:T(8,128)(2,1)} %q_ref.1, bf16[16,128,640]{2,1,0:T(8,128)(2,1)} %all-gather.2.cloned.1.call-done.keys, bf16[16,32,576]{2,1,0:T(8,128)(2,1)} %own.1, bf16[8,512,128]{2,1,0:T(8,128)(2,1)} %w_uv.1), custom_call_target="tpu_custom_call" | custom-call | tf_op jit(solution)/shard_map/attention/pallas_call | solution.py:177
  64.0 3.2 %collective-permute-start.5 = (bf16[512,1024]{1,0:T(8,128)(2,1)}, bf16[512,1024]{1,0:T(8,128)(2,1)}, u32[]{:S(2)}, u32[]{:S(2)}) collective-permute-start(bf16[512,1024]{1,0:T(8,128)(2,1)} %attention.1.refs_0_), channel_id=1, source_target_pairs={{0,1},{1,0},{2,3},{3,2},{4,5},{5,4},{6,7},{7,6},{8,9},{9,8},{10,11... | collective-permute-start | bytes 3145736 | tf_op jit(solution)/shard_map/ppermute | solution.py:54
  67.3 2.6 collective-permute-start.7
  69.9 0.8 slice.36
  70.7 0.8 slice.37
  71.6 2.7 collective-permute-start.9
  74.2 12.9 %all-to-all-done = bf16[8,1152,256]{2,1,0:T(8,128)(2,1)} async-done(((bf16[8,1152,256]{2,1,0:T(8,128)(2,1)}), bf16[8,1152,256]{2,1,0:T(8,128)(2,1)}, u32[]{:S(2)}, u32[]{:S(2)}) %all-to-all-start) | async-done | bytes 4718624 | tf_op jit(solution)/shard_map/all_to_all | solution.py:465
  87.2 4.2 %dynamic-slice_bitcast_fusion.1 = (bf16[4,1152,256]{2,1,0:T(8,128)(2,1)S(1)}, bf16[4,1152,256]{2,1,0:T(8,128)(2,1)}) fusion(bf16[4,2,1152,256]{3,2,1,0:T(8,128)(2,1)} %bitcast.11, s32[]{:T(128)S(6)} %select_n.79, s32[]{:T(128)S(6)} %select_n.80), kind=kLoop, calls=%fused_computation.2 | loop fusion | bytes 9437192 | tf_op jit(solution)/shard_map/jit(dynamic_index_in_dim)/squeeze | solution.py:470
  91.4 7.7 %collective-permute-done.8.refs_6_ = bf16[224,1024]{1,0:T(8,128)(2,1)} collective-permute-done((bf16[224,1024]{1,0:T(8,128)(2,1)}, bf16[224,1024]{1,0:T(8,128)(2,1)}, u32[]{:S(2)}, u32[]{:S(2)}) %collective-permute-start.8) | collective-permute-done | bytes 458784 | tf_op jit(solution)/shard_map/ppermute | solution.py:50
  99.1 0.2 collective-permute-start.20
  99.3 2.5 collective-permute-start.4
  101.8 1.8 slice.38
  103.7 0.7 collective-permute-start.11
  104.4 1.8 slice.39
  106.2 1.9 collective-permute-start.12
  108.2 0.6 pad_add_fusion.picks
  108.8 8.0 %collective-permute-done.11.refs_11_ = bf16[224,1024]{1,0:T(8,128)(2,1)} collective-permute-done((bf16[224,1024]{1,0:T(8,128)(2,1)}, bf16[224,1024]{1,0:T(8,128)(2,1)}, u32[]{:S(2)}, u32[]{:S(2)}) %collective-permute-start.11) | collective-permute-done | bytes 458784 | tf_op jit(solution)/shard_map/ppermute | solution.py:50
  116.8 1.0 collective-permute-done.12.refs_12_
  117.8 5.8 %project.3 = (bf16[224,1024]{1,0:T(8,128)(2,1)}, bf16[224,1024]{1,0:T(8,128)(2,1)}) custom-call(s32[1]{0:T(128)} %bitcast.2.match, s32[1]{0:T(128)} %bitcast.7.picks, bf16[512,1024]{1,0:T(8,128)(2,1)} %attention.1.refs_0_, bf16[512,1024]{1,0:T(8,128)(2,1)} %collective-permute-done.4.refs_1_, bf16[512,1024]{1,0:T(8,128)(2,1)} %collective-permute-done.5.refs_2_, ...), custom_call_target="tpu_custom_call" | custom-call | tf_op jit(solution)/shard_map/project/pallas_call | solution.py:250
  123.6 1.2 collective-permute-start.13
  124.8 1.5 collective-permute-start.14
  126.4 11.7 %project.2 = (bf16[448,512]{1,0:T(8,128)(2,1)}, bf16[448,512]{1,0:T(8,128)(2,1)}, bf16[448,512]{1,0:T(8,128)(2,1)}, bf16[448,512]{1,0:T(8,128)(2,1)}, bf16[448,5...) custom-call(s32[1]{0:T(128)} %bitcast.2.match, s32[3]{0:T(128)} %pad_add_fusion.picks, bf16[512,1024]{1,0:T(8,128)(2,1)} %attention.1.refs_0_, ...), custom_call_target="tpu_custom_call" | custom-call | tf_op jit(solution)/shard_map/project/pallas_call | solution.py:250
  138.0 2.3 collective-permute-start.15
  140.5 0.7 copy-done.7
  141.3 2.6 merge.1
  144.0 2.7 collective-permute-start.17
  146.6 3.0 %collective-permute-start.19 = (bf16[448,512]{1,0:T(8,128)(2,1)}, bf16[448,512]{1,0:T(8,128)(2,1)}, u32[]{:S(2)}, u32[]{:S(2)}) collective-permute-start(bf16[448,512]{1,0:T(8,128)(2,1)} %get-tuple-element.48), channel_id=1, source_target_pairs={{0,14},{1,15},{2,8},{3,9},{4,10},{5,11},{6,12},{7,13},{8,6},{9,7},... | collective-permute-start | bytes 1376264 | tf_op jit(solution)/shard_map/ppermute | solution.py:72
  149.6 1.8 collective-permute-done.20.come
  151.4 1.1 select_bitcast_fusion.1
  152.7 1.0 copy.47
  153.7 1.7 reshape.119.rest
  155.4 0.2 fusion
  155.7 0.3 convert_reduce_fusion.1
  156.1 0.6 add_add_fusion.place
  156.7 0.9 collective-permute-done.16.near1
  157.6 10.0 %collective-permute-done.18.far1 = bf16[448,512]{1,0:T(8,128)(2,1)} collective-permute-done((bf16[448,512]{1,0:T(8,128)(2,1)}, bf16[448,512]{1,0:T(8,128)(2,1)}, u32[]{:S(2)}, u32[]{:S(2)}) %collective-permute-start.18) | collective-permute-done | bytes 458784 | tf_op jit(solution)/shard_map/ppermute | solution.py:72
  167.6 4.3 %dispatch.1 = bf16[512,1024]{1,0:T(8,128)(2,1)} custom-call(s32[1]{0:T(128)} %bitcast.1.core, bf16[448,512]{1,0:T(8,128)(2,1)} %get-tuple-element.32.near0, bf16[448,512]{1,0:T(8,128)(2,1)} %collective-permute-done.16.near1, bf16[448,512]{1,0:T(8,128)(2,1)} %collective-permute-done.17.near3, bf16[448,512]{1,0:T(8,128)(2,1)} %copy-done.6, ...), custom_call_target="tpu_custom_call" | custom-call | tf_op jit(solution)/shard_map/dispatch/pallas_call | solution.py:306
  171.9 5.4 %all-to-all-start.1 = ((bf16[16,32,1024]{2,1,0:T(8,128)(2,1)}), bf16[16,32,1024]{2,1,0:T(8,128)(2,1)S(1)}, u32[]{:S(2)}, u32[]{:S(2)}) async-start(bf16[16,32,1024]{2,1,0:T(8,128)(2,1)} %bitcast.46), calls=%async_computation.1 | async-start | bytes 2097152 | tf_op jit(solution)/shard_map/all_to_all | solution.py:516
  177.3 0.8 dynamic_slice.12
  178.0 15.1 %all-to-all-done.1 = bf16[16,32,1024]{2,1,0:T(8,128)(2,1)S(1)} async-done(((bf16[16,32,1024]{2,1,0:T(8,128)(2,1)}), bf16[16,32,1024]{2,1,0:T(8,128)(2,1)S(1)}, u32[]{:S(2)}, u32[]{:S(2)}) %all-to-all-start.1) | async-done | bytes 1048608 | tf_op jit(solution)/shard_map/all_to_all | solution.py:516
  193.1 4.1 %enter.1 = bf16[8704,128]{1,0:T(8,128)(2,1)S(1)} custom-call(s32[1]{0:T(128)} %bitcast.half, bf16[512,1024]{1,0:T(8,128)(2,1)S(1)} %bitcast.38, f32[1,896]{1,0:T(1,128)S(1)} %reshape.120.gain, bf16[4,1152,256]{2,1,0:T(8,128)(2,1)S(1)} %get-tuple-element.55.kept, bf16[4,1152,256]{2,1,0:T(8,128)(2,1)} %collective-permute-done.20.come), custom_call_target="tpu_custom_call" | custom-call | tf_op jit(solution)/shard_map/enter/pallas_call | solution.py:340
  197.3 34.5 %all_to_all.43 = bf16[8,1088,128]{2,1,0:T(8,128)(2,1)S(1)} all-to-all(bf16[8,1088,128]{2,1,0:T(8,128)(2,1)S(1)} %bitcast.40), channel_id=1, replica_groups=mesh['resp'=16,'exp'=8] {'exp'}, dimensions={0} | all-to-all | bytes 4456448 | tf_op jit(solution)/shard_map/all_to_all | solution.py:518
  231.8 0.6 activate.1
  232.4 17.6 %all_to_all.44 = bf16[8,64,1024]{2,1,0:T(8,128)(2,1)S(1)} all-to-all(bf16[8,64,1024]{2,1,0:T(8,128)(2,1)S(1)} %bitcast.43), channel_id=1, replica_groups=mesh['resp'=16,'exp'=8] {'exp'}, dimensions={0} | all-to-all | bytes 2097152 | tf_op jit(solution)/shard_map/all_to_all | solution.py:520
  250.0 1.3 leave.1
  251.2 1.1 reshape.121
  252.4 6.7 %all-to-all-start.4 = ((bf16[128,4,896]{2,1,0:T(4,128)(2,1)}), bf16[128,4,896]{2,1,0:T(4,128)(2,1)S(1)}, u32[]{:S(2)}, u32[]{:S(2)}) async-start(bf16[128,4,896]{2,1,0:T(4,128)(2,1)} %reshape.121), calls=%async_computation.4 | async-start | bytes 1835008 | tf_op jit(solution)/shard_map/all_to_all | solution.py:522
  259.2 18.2 %all-to-all-done.4 = bf16[128,4,896]{2,1,0:T(4,128)(2,1)S(1)} async-done(((bf16[128,4,896]{2,1,0:T(4,128)(2,1)}), bf16[128,4,896]{2,1,0:T(4,128)(2,1)S(1)}, u32[]{:S(2)}, u32[]{:S(2)}) %all-to-all-start.4) | async-done | bytes 917536 | tf_op jit(solution)/shard_map/all_to_all | solution.py:522
  277.4 0.2 reshape.122.rows
  277.6 1.7 restore.1
  (56 shorter events, 0.9 us)
Async XLA Ops:
  6.5 43.2 %all-gather.2.cloned.1.call-start = ((), (), s32[]{:S(2)}) async-start(), calls=%async_computation.5 | async-start | bytes 2785280 | tf_op jit(solution)/shard_map/all_gather | solution.py:444
  8.3 12.1 %copy-start.9 = (s32[64,1]{0,1:T(1,128)S(1)}, s32[64,1]{0,1:T(1,128)}, u32[]{:S(2)}) copy-start(s32[64,1]{0,1:T(1,128)} %param.22) | copy-start | bytes 772
  8.3 12.2 %copy-start.8 = (f32[64,1]{0,1:T(1,128)S(1)}, f32[64,1]{0,1:T(1,128)}, u32[]{:S(2)}) copy-start(f32[64,1]{0,1:T(1,128)} %param.23) | copy-start | bytes 772
  8.3 12.4 %copy-start.5 = (bf16[64,7168]{1,0:T(8,128)(2,1)S(1)}, bf16[64,7168]{1,0:T(8,128)(2,1)}, u32[]{:S(2)}) copy-start(bf16[64,7168]{1,0:T(8,128)(2,1)} %param.18) | copy-start | bytes 2752516
  8.3 19.0 %collective-permute-start = (bf16[448,1024]{1,0:T(8,128)(2,1)}, bf16[448,1024]{1,0:T(8,128)(2,1)}, u32[]{:S(2)}, u32[]{:S(2)}) collective-permute-start(bf16[448,1024]{1,0:T(8,128)(2,1)} %bitcast.51), channel_id=1, source_target_pairs={{0,0},{1,16},{2,2},{3,18},{4,4},{5,20},{6,6},{7,22},{8,8},{9,24},{... | collective-permute-start | bytes 2752520 | tf_op jit(solution)/shard_map/ppermute | solution.py:72
  27.4 59.8 %all-to-all-start = ((bf16[8,1152,256]{2,1,0:T(8,128)(2,1)}), bf16[8,1152,256]{2,1,0:T(8,128)(2,1)}, u32[]{:S(2)}, u32[]{:S(2)}) async-start(bf16[8,1152,256]{2,1,0:T(8,128)(2,1)} %pad_maximum_fusion), calls=%async_computation | async-start | bytes 9437184 | tf_op jit(solution)/shard_map/all_to_all | solution.py:465
  32.4 31.5 %collective-permute-start.1 = (bf16[448,1024]{1,0:T(8,128)(2,1)}, bf16[448,1024]{1,0:T(8,128)(2,1)S(1)}, u32[]{:S(2)}, u32[]{:S(2)}) collective-permute-start(bf16[448,1024]{1,0:T(8,128)(2,1)} %collective-permute-done.refs_4_), channel_id=1, source_target_pairs={{0,32},{8,40},{16,48},{24,56},{32,64},{40,72},{48,80},{56,88},{64,... | collective-permute-start | bytes 2752520 | tf_op jit(solution)/shard_map/ppermute | solution.py:50
  34.9 29.1 %collective-permute-start.2 = (bf16[448,1024]{1,0:T(8,128)(2,1)}, bf16[448,1024]{1,0:T(8,128)(2,1)S(1)}, u32[]{:S(2)}, u32[]{:S(2)}) collective-permute-start(bf16[448,1024]{1,0:T(8,128)(2,1)} %collective-permute-done.refs_4_), channel_id=1, source_target_pairs={{0,96},{8,104},{16,112},{24,120},{32,0},{40,8},{48,16},{56,24},{64... | collective-permute-start | bytes 2752520 | tf_op jit(solution)/shard_map/ppermute | solution.py:50
  37.1 26.9 %collective-permute-start.3 = (bf16[448,1024]{1,0:T(8,128)(2,1)}, bf16[448,1024]{1,0:T(8,128)(2,1)}, u32[]{:S(2)}, u32[]{:S(2)}) collective-permute-start(bf16[448,1024]{1,0:T(8,128)(2,1)} %collective-permute-done.refs_4_), channel_id=1, source_target_pairs={{0,16},{8,24},{16,0},{24,8},{32,48},{40,56},{48,32},{56,40},{64,80... | collective-permute-start | bytes 2752520 | tf_op jit(solution)/shard_map/ppermute | solution.py:50
  63.9 23.2 %copy-start.2 = (bf16[448,1024]{1,0:T(8,128)(2,1)}, bf16[448,1024]{1,0:T(8,128)(2,1)S(1)}, u32[]{:S(2)}) copy-start(bf16[448,1024]{1,0:T(8,128)(2,1)S(1)} %collective-permute-done.1.refs_5_) | copy-start | bytes 2752516
  63.9 23.2 %copy-start.3 = (bf16[448,1024]{1,0:T(8,128)(2,1)}, bf16[448,1024]{1,0:T(8,128)(2,1)S(1)}, u32[]{:S(2)}) copy-start(bf16[448,1024]{1,0:T(8,128)(2,1)S(1)} %collective-permute-done.2.refs_8_) | copy-start | bytes 2752516
  64.0 35.1 %collective-permute-start.5 = (bf16[512,1024]{1,0:T(8,128)(2,1)}, bf16[512,1024]{1,0:T(8,128)(2,1)}, u32[]{:S(2)}, u32[]{:S(2)}) collective-permute-start(bf16[512,1024]{1,0:T(8,128)(2,1)} %attention.1.refs_0_), channel_id=1, source_target_pairs={{0,1},{1,0},{2,3},{3,2},{4,5},{5,4},{6,7},{7,6},{8,9},{9,8},{10,11... | collective-permute-start | bytes 3145736 | tf_op jit(solution)/shard_map/ppermute | solution.py:54
  67.2 31.8 %collective-permute-start.6 = (bf16[448,1024]{1,0:T(8,128)(2,1)}, bf16[448,1024]{1,0:T(8,128)(2,1)}, u32[]{:S(2)}, u32[]{:S(2)}) collective-permute-start(bf16[448,1024]{1,0:T(8,128)(2,1)} %collective-permute-done.3.refs_9_), channel_id=1, source_target_pairs={{0,32},{8,40},{16,48},{24,56},{32,64},{40,72},{48,80},{56,88},{64,... | collective-permute-start | bytes 2752520 | tf_op jit(solution)/shard_map/ppermute | solution.py:50
  67.3 31.8 %collective-permute-start.7 = (bf16[448,1024]{1,0:T(8,128)(2,1)}, bf16[448,1024]{1,0:T(8,128)(2,1)}, u32[]{:S(2)}, u32[]{:S(2)}) collective-permute-start(bf16[448,1024]{1,0:T(8,128)(2,1)} %collective-permute-done.3.refs_9_), channel_id=1, source_target_pairs={{0,96},{8,104},{16,112},{24,120},{32,0},{40,8},{48,16},{56,24},{64... | collective-permute-start | bytes 2752520 | tf_op jit(solution)/shard_map/ppermute | solution.py:50
  70.7 28.3 %collective-permute-start.8 = (bf16[224,1024]{1,0:T(8,128)(2,1)}, bf16[224,1024]{1,0:T(8,128)(2,1)}, u32[]{:S(2)}, u32[]{:S(2)}) collective-permute-start(bf16[224,1024]{1,0:T(8,128)(2,1)} %slice.36), channel_id=1, source_target_pairs={{0,32},{8,40},{16,48},{24,56},{32,64},{40,72},{48,80},{56,88},{64,... | collective-permute-start | bytes 1376264 | tf_op jit(solution)/shard_map/ppermute | solution.py:50
  71.6 27.5 %collective-permute-start.9 = (bf16[224,1024]{1,0:T(8,128)(2,1)}, bf16[224,1024]{1,0:T(8,128)(2,1)}, u32[]{:S(2)}, u32[]{:S(2)}) collective-permute-start(bf16[224,1024]{1,0:T(8,128)(2,1)} %slice.37), channel_id=1, source_target_pairs={{0,96},{8,104},{16,112},{24,120},{32,0},{40,8},{48,16},{56,24},{64... | collective-permute-start | bytes 1376264 | tf_op jit(solution)/shard_map/ppermute | solution.py:50
  87.2 12.1 %copy-start.1 = (bf16[512,1024]{1,0:T(8,128)(2,1)S(1)}, bf16[512,1024]{1,0:T(8,128)(2,1)}, u32[]{:S(2)}) copy-start(bf16[512,1024]{1,0:T(8,128)(2,1)} %attention.1.refs_0_) | copy-start | bytes 3145732
  99.1 52.4 %collective-permute-start.20 = (bf16[4,1152,256]{2,1,0:T(8,128)(2,1)}, bf16[4,1152,256]{2,1,0:T(8,128)(2,1)}, u32[]{:S(2)}, u32[]{:S(2)}) collective-permute-start(bf16[4,1152,256]{2,1,0:T(8,128)(2,1)} %get-tuple-element.50), channel_id=1, source_target_pairs={{0,1},{1,0},{2,3},{3,2},{4,5},{5,4},{6,7},{7,6},{8,9},{9,8},{10,11... | collective-permute-start | bytes 7077896 | tf_op jit(solution)/shard_map/ppermute | solution.py:54
  99.3 18.5 %collective-permute-start.4 = (bf16[512,1024]{1,0:T(8,128)(2,1)S(1)}, bf16[512,1024]{1,0:T(8,128)(2,1)}, u32[]{:S(2)}, u32[]{:S(2)}) collective-permute-start(bf16[512,1024]{1,0:T(8,128)(2,1)S(1)} %copy-done.1), channel_id=1, source_target_pairs={{0,8},{8,0},{16,24},{24,16},{32,40},{40,32},{48,56},{56,48},{64,72... | collective-permute-start | bytes 3145736 | tf_op jit(solution)/shard_map/ppermute | solution.py:50
  101.8 16.0 %collective-permute-start.10 = (bf16[512,1024]{1,0:T(8,128)(2,1)}, bf16[512,1024]{1,0:T(8,128)(2,1)}, u32[]{:S(2)}, u32[]{:S(2)}) collective-permute-start(bf16[512,1024]{1,0:T(8,128)(2,1)} %collective-permute-done.5.refs_2_), channel_id=1, source_target_pairs={{0,8},{8,0},{16,24},{24,16},{32,40},{40,32},{48,56},{56,48},{64,72... | collective-permute-start | bytes 3145736 | tf_op jit(solution)/shard_map/ppermute | solution.py:50
  103.7 13.1 %collective-permute-start.11 = (bf16[224,1024]{1,0:T(8,128)(2,1)}, bf16[224,1024]{1,0:T(8,128)(2,1)}, u32[]{:S(2)}, u32[]{:S(2)}) collective-permute-start(bf16[224,1024]{1,0:T(8,128)(2,1)} %slice.38), channel_id=1, source_target_pairs={{0,32},{8,40},{16,48},{24,56},{32,64},{40,72},{48,80},{56,88},{64,... | collective-permute-start | bytes 1376264 | tf_op jit(solution)/shard_map/ppermute | solution.py:50
  106.2 11.6 %collective-permute-start.12 = (bf16[224,1024]{1,0:T(8,128)(2,1)}, bf16[224,1024]{1,0:T(8,128)(2,1)}, u32[]{:S(2)}, u32[]{:S(2)}) collective-permute-start(bf16[224,1024]{1,0:T(8,128)(2,1)} %slice.39), channel_id=1, source_target_pairs={{0,96},{8,104},{16,112},{24,120},{32,0},{40,8},{48,16},{56,24},{64... | collective-permute-start | bytes 1376264 | tf_op jit(solution)/shard_map/ppermute | solution.py:50
  123.6 16.9 %collective-permute-start.13 = (bf16[224,1024]{1,0:T(8,128)(2,1)}, bf16[224,1024]{1,0:T(8,128)(2,1)S(1)}, u32[]{:S(2)}, u32[]{:S(2)}) collective-permute-start(bf16[224,1024]{1,0:T(8,128)(2,1)} %get-tuple-element.37), channel_id=1, source_target_pairs={{0,2},{1,3},{2,4},{3,5},{4,6},{5,7},{6,0},{7,1},{8,10},{9,11},{10,... | collective-permute-start | bytes 1376264 | tf_op jit(solution)/shard_map/ppermute | solution.py:54
  124.8 15.7 %collective-permute-start.14 = (bf16[224,1024]{1,0:T(8,128)(2,1)}, bf16[224,1024]{1,0:T(8,128)(2,1)}, u32[]{:S(2)}, u32[]{:S(2)}) collective-permute-start(bf16[224,1024]{1,0:T(8,128)(2,1)} %get-tuple-element.38), channel_id=1, source_target_pairs={{0,6},{1,7},{2,0},{3,1},{4,2},{5,3},{6,4},{7,5},{8,14},{9,15},{10,... | collective-permute-start | bytes 1376264 | tf_op jit(solution)/shard_map/ppermute | solution.py:54
  138.0 5.8 %collective-permute-start.15 = (bf16[448,512]{1,0:T(8,128)(2,1)}, bf16[448,512]{1,0:T(8,128)(2,1)S(1)}, u32[]{:S(2)}, u32[]{:S(2)}) collective-permute-start(bf16[448,512]{1,0:T(8,128)(2,1)} %get-tuple-element.43), channel_id=1, source_target_pairs={{0,8},{1,9},{2,10},{3,11},{4,12},{5,13},{6,14},{7,15},{8,0},{9,1},... | collective-permute-start | bytes 1376264 | tf_op jit(solution)/shard_map/ppermute | solution.py:72
  140.5 0.8 copy-start.7
  143.9 8.8 %copy-start.6 = (bf16[448,512]{1,0:T(8,128)(2,1)}, bf16[448,512]{1,0:T(8,128)(2,1)S(1)}, u32[]{:S(2)}) copy-start(bf16[448,512]{1,0:T(8,128)(2,1)S(1)} %collective-permute-done.15.far0) | copy-start | bytes 1376260
  143.9 13.7 %collective-permute-start.16 = (bf16[448,512]{1,0:T(8,128)(2,1)}, bf16[448,512]{1,0:T(8,128)(2,1)}, u32[]{:S(2)}, u32[]{:S(2)}) collective-permute-start(bf16[448,512]{1,0:T(8,128)(2,1)} %get-tuple-element.44), channel_id=1, source_target_pairs={{0,2},{1,3},{2,4},{3,5},{4,6},{5,7},{6,0},{7,1},{8,10},{9,11},{10,... | collective-permute-start | bytes 1376264 | tf_op jit(solution)/shard_map/ppermute | solution.py:54
  144.0 13.6 %collective-permute-start.17 = (bf16[448,512]{1,0:T(8,128)(2,1)}, bf16[448,512]{1,0:T(8,128)(2,1)}, u32[]{:S(2)}, u32[]{:S(2)}) collective-permute-start(bf16[448,512]{1,0:T(8,128)(2,1)} %get-tuple-element.45), channel_id=1, source_target_pairs={{0,6},{1,7},{2,0},{3,1},{4,2},{5,3},{6,4},{7,5},{8,14},{9,15},{10,... | collective-permute-start | bytes 1376264 | tf_op jit(solution)/shard_map/ppermute | solution.py:54
  146.6 20.9 %collective-permute-start.18 = (bf16[448,512]{1,0:T(8,128)(2,1)}, bf16[448,512]{1,0:T(8,128)(2,1)}, u32[]{:S(2)}, u32[]{:S(2)}) collective-permute-start(bf16[448,512]{1,0:T(8,128)(2,1)} %get-tuple-element.47), channel_id=1, source_target_pairs={{0,10},{1,11},{2,12},{3,13},{4,14},{5,15},{6,8},{7,9},{8,2},{9,3},... | collective-permute-start | bytes 1376264 | tf_op jit(solution)/shard_map/ppermute | solution.py:72
  146.6 20.9 %collective-permute-start.19 = (bf16[448,512]{1,0:T(8,128)(2,1)}, bf16[448,512]{1,0:T(8,128)(2,1)}, u32[]{:S(2)}, u32[]{:S(2)}) collective-permute-start(bf16[448,512]{1,0:T(8,128)(2,1)} %get-tuple-element.48), channel_id=1, source_target_pairs={{0,14},{1,15},{2,8},{3,9},{4,10},{5,11},{6,12},{7,13},{8,6},{9,7},... | collective-permute-start | bytes 1376264 | tf_op jit(solution)/shard_map/ppermute | solution.py:72
  155.4 12.2 %copy-start.4 = (bf16[512,1024]{1,0:T(8,128)(2,1)}, bf16[512,1024]{1,0:T(8,128)(2,1)S(1)}, u32[]{:S(2)}) copy-start(bf16[512,1024]{1,0:T(8,128)(2,1)S(1)} %reshape.119.rest) | copy-start | bytes 3145732
  171.9 21.2 %all-to-all-start.1 = ((bf16[16,32,1024]{2,1,0:T(8,128)(2,1)}), bf16[16,32,1024]{2,1,0:T(8,128)(2,1)S(1)}, u32[]{:S(2)}, u32[]{:S(2)}) async-start(bf16[16,32,1024]{2,1,0:T(8,128)(2,1)} %bitcast.46), calls=%async_computation.1 | async-start | bytes 2097152 | tf_op jit(solution)/shard_map/all_to_all | solution.py:516
  231.8 18.2 %copy-start = (bf16[1,1024,896]{2,1,0:T(8,128)(2,1)S(1)}, bf16[1,1024,896]{2,1,0:T(8,128)(2,1)}, u32[]{:S(2)}) copy-start(bf16[1,1024,896]{2,1,0:T(8,128)(2,1)} %w_out.1) | copy-start | bytes 5505028
  252.4 25.0 %all-to-all-start.4 = ((bf16[128,4,896]{2,1,0:T(4,128)(2,1)}), bf16[128,4,896]{2,1,0:T(4,128)(2,1)S(1)}, u32[]{:S(2)}, u32[]{:S(2)}) async-start(bf16[128,4,896]{2,1,0:T(4,128)(2,1)} %reshape.121), calls=%async_computation.4 | async-start | bytes 1835008 | tf_op jit(solution)/shard_map/all_to_all | solution.py:522
Sparse Core Ops, SparseCore 0:
  9.1 40.5 all-gather.1
